TPU v7x, 32 devices: a whole 2x2x4 slice. The times are simulated.
32 devices in a mesh: pages: 8 (over z, x), blk: 4 (over y, core).
Axes of the slice: x: 2, y: 2, z: 4, core: 2. Of those that a mesh axis runs over, the one named last changes fastest.
Arguments:
- hidden: bfloat16 [8, 512, 768], P('pages', 'blk'), may hold values from -6 to 6
- boxes: int32 [8, 512, 2], P('pages', 'blk'), may hold values from 0 to 255
- lengths: int32 [8], P('pages'), may hold values from 40 to 512, as said below
- w_qkv: bfloat16 [768, 2304], P(('pages', 'blk')), may hold values from -0.21875 to 0.21875
- b_qkv: bfloat16 [2304], P(('pages', 'blk')), may hold values from -1.1953125 to 1.1953125
- w_relq: bfloat16 [768, 768], P(('pages', 'blk')), may hold values from -0.21875 to 0.21875
- w_relk: bfloat16 [768, 768], P(('pages', 'blk')), may hold values from -0.21875 to 0.21875
- w_out: bfloat16 [768, 768], P(('pages', 'blk')), may hold values from -0.875 to 0.875
- b_out: bfloat16 [768], P(('pages', 'blk')), may hold values from -1.1953125 to 1.1953125
- ln1_gain: bfloat16 [768], P(('pages', 'blk')), may hold values from 0.5 to 1.5
- ln1_bias: bfloat16 [768], P(('pages', 'blk')), may hold values from -1.1953125 to 1.1953125
- w_up: bfloat16 [768, 3072], P(('pages', 'blk')), may hold values from -0.21875 to 0.21875
- b_up: bfloat16 [3072], P(('pages', 'blk')), may hold values from -1.1953125 to 1.1953125
- w_down: bfloat16 [3072, 768], P(('pages', 'blk')), may hold values from -0.21875 to 0.21875
- b_down: bfloat16 [768], P(('pages', 'blk')), may hold values from -1.1953125 to 1.1953125
- ln2_gain: bfloat16 [768], P(('pages', 'blk')), may hold values from 0.5 to 1.5
- ln2_bias: bfloat16 [768], P(('pages', 'blk')), may hold values from -1.1953125 to 1.1953125
- cotangent: bfloat16 [8, 512, 768], P('pages', 'blk'), may hold values from -6 to 6
Outputs:
- output: bfloat16 [8, 512, 768], P('pages', 'blk')
- grad_hidden: bfloat16 [8, 512, 768], P('pages', 'blk')
- grad_w_qkv: float32 [768, 2304], P(('pages', 'blk'))
- grad_b_qkv: float32 [2304], P(('pages', 'blk'))
- grad_w_relq: float32 [768, 768], P(('pages', 'blk'))
- grad_w_relk: float32 [768, 768], P(('pages', 'blk'))
- grad_w_out: float32 [768, 768], P(('pages', 'blk'))
- grad_b_out: float32 [768], P(('pages', 'blk'))
- grad_ln1_gain: float32 [768], P(('pages', 'blk'))
- grad_ln1_bias: float32 [768], P(('pages', 'blk'))
- grad_w_up: float32 [768, 3072], P(('pages', 'blk'))
- grad_b_up: float32 [3072], P(('pages', 'blk'))
- grad_w_down: float32 [3072, 768], P(('pages', 'blk'))
- grad_b_down: float32 [768], P(('pages', 'blk'))
- grad_ln2_gain: float32 [768], P(('pages', 'blk'))
- grad_ln2_bias: float32 [768], P(('pages', 'blk'))
Inputs may be any that keep to these rules, and one draw needn't show every extreme that they name: `lengths`: exactly one page has all 512 slots real; the others have fewer than 512.
All inputs are finite; a program needn't handle non-finite values.
Results may differ from a plain program's by a relative error of at most 0.025.
Values may be sent and summed in bfloat16 or wider, within the bound.
A program may use at most 256 MiB of HBM per device.

v0:
```python
import math

import jax
import jax.numpy as jnp
from jax import lax
from jax.sharding import PartitionSpec as P

HEAD_DIM = 64
FREQ = 192


precise = lax.Precision.HIGHEST


def passed_along(block, axis, distance):
    devices = range(lax.axis_size(axis))
    route = [((i - distance) % len(devices), i) for i in devices]
    return lax.ppermute(block, axis, route)


def box_features(boxes):
    ladder = jnp.arange(FREQ).astype(jnp.float32)
    rates = jnp.exp(ladder * (-math.log(10000.0) / FREQ))
    coords = boxes.astype(jnp.float32)
    angles = jnp.concatenate([coords[..., 0:1] * rates, coords[..., 1:2] * rates], axis=-1)
    return jnp.concatenate([jnp.cos(angles), jnp.sin(angles)], axis=-1)


def turn_query(rel_vals, cos_part, sin_part):
    middle = rel_vals.shape[-1] // 2
    lead_part, tail_part = (rel_vals[..., :middle], rel_vals[..., middle:])
    cos_wide = cos_part[..., None, :]
    sin_wide = sin_part[..., None, :]
    return jnp.concatenate(
        [lead_part * cos_wide + tail_part * sin_wide, lead_part * sin_wide - tail_part * cos_wide],
        axis=-1,
    )


def turn_key(rel_vals, cos_part, sin_part):
    middle = rel_vals.shape[-1] // 2
    lead_part, tail_part = (rel_vals[..., :middle], rel_vals[..., middle:])
    cos_wide = cos_part[..., None, :]
    sin_wide = sin_part[..., None, :]
    return jnp.concatenate(
        [lead_part * cos_wide - tail_part * sin_wide, lead_part * sin_wide + tail_part * cos_wide],
        axis=-1,
    )


def unturn_key(grad_vals, cos_part, sin_part):
    middle = grad_vals.shape[-1] // 2
    first_part, second_part = (grad_vals[..., :middle], grad_vals[..., middle:])
    cos_wide = cos_part[..., None, :]
    sin_wide = sin_part[..., None, :]
    return jnp.concatenate(
        [
            first_part * cos_wide + second_part * sin_wide,
            second_part * cos_wide - first_part * sin_wide,
        ],
        axis=-1,
    )


def normalize(values, gain, shift):
    centre = values - jnp.mean(values, axis=-1, keepdims=True)
    spread = jnp.mean(centre * centre, axis=-1, keepdims=True)
    return centre * lax.rsqrt(spread + 1e-12) * gain + shift


def exact_gelu(values):
    return jax.nn.gelu(values, approximate=False)


def key_mask(lengths, owner, tok_blk):
    positions = owner * tok_blk + lax.iota(jnp.int32, tok_blk)
    return positions[None, :] < lengths[:, None]


def key_block(key_vals, extra, whole_relk, heads):
    pages_dev, tok_blk, doubled = key_vals.shape
    width = doubled // 2
    feat_wide = extra.astype(jnp.float32)
    span = feat_wide.shape[-1] // 2
    cos_part, sin_part = (feat_wide[..., :span], feat_wide[..., span:])
    key_rows = key_vals[..., :width].reshape(pages_dev, tok_blk, heads, HEAD_DIM)
    value_rows = key_vals[..., width:].reshape(pages_dev, tok_blk, heads, HEAD_DIM)
    key_in = jnp.einsum(
        "pthc,rhc->pthr",
        key_rows,
        whole_relk.reshape(2 * span, heads, HEAD_DIM),
        preferred_element_type=jnp.float32,
    )
    key_rel = turn_key(key_in, cos_part, sin_part).astype(jnp.bfloat16)
    feat_heads = jnp.broadcast_to(extra[:, :, None, :], key_rel.shape)
    key_hat = jnp.concatenate([key_rows, feat_heads, key_rel], axis=-1)
    return (key_hat, value_rows, key_rows, cos_part, sin_part)


def on_device(
    hidden,
    boxes,
    lengths,
    w_qkv,
    b_qkv,
    w_relq,
    w_relk,
    w_out,
    b_out,
    ln1_gain,
    ln1_bias,
    w_up,
    b_up,
    w_down,
    b_down,
    ln2_gain,
    ln2_bias,
    cotangent,
):
    shard_set = (
        w_qkv,
        b_qkv,
        w_relq,
        w_relk,
        w_out,
        b_out,
        ln1_gain,
        ln1_bias,
        w_up,
        b_up,
        w_down,
        b_down,
        ln2_gain,
        ln2_bias,
    )
    sectioned = (
        lax.all_gather(shard_set[0], "blk", axis=0, tiled=True),
        lax.all_gather(shard_set[1], "blk", axis=0, tiled=True),
        lax.all_gather(shard_set[2], "blk", axis=0, tiled=True),
        lax.all_gather(shard_set[3], "blk", axis=0, tiled=True),
        lax.all_gather(shard_set[4], "blk", axis=0, tiled=True),
        lax.all_gather(shard_set[5], "blk", axis=0, tiled=True),
        lax.all_gather(shard_set[6], "blk", axis=0, tiled=True),
        lax.all_gather(shard_set[7], "blk", axis=0, tiled=True),
        lax.all_gather(shard_set[8], "blk", axis=0, tiled=True),
        lax.all_gather(shard_set[9], "blk", axis=0, tiled=True),
        lax.all_gather(shard_set[10], "blk", axis=0, tiled=True),
        lax.all_gather(shard_set[11], "blk", axis=0, tiled=True),
        lax.all_gather(shard_set[12], "blk", axis=0, tiled=True),
        lax.all_gather(shard_set[13], "blk", axis=0, tiled=True),
    )
    whole_set = (
        lax.all_gather(sectioned[0], "pages", axis=0, tiled=True),
        lax.all_gather(sectioned[1], "pages", axis=0, tiled=True),
        lax.all_gather(sectioned[2], "pages", axis=0, tiled=True),
        lax.all_gather(sectioned[3], "pages", axis=0, tiled=True),
        lax.all_gather(sectioned[4], "pages", axis=0, tiled=True),
        lax.all_gather(sectioned[5], "pages", axis=0, tiled=True),
        lax.all_gather(sectioned[6], "pages", axis=0, tiled=True),
        lax.all_gather(sectioned[7], "pages", axis=0, tiled=True),
        lax.all_gather(sectioned[8], "pages", axis=0, tiled=True),
        lax.all_gather(sectioned[9], "pages", axis=0, tiled=True),
        lax.all_gather(sectioned[10], "pages", axis=0, tiled=True),
        lax.all_gather(sectioned[11], "pages", axis=0, tiled=True),
        lax.all_gather(sectioned[12], "pages", axis=0, tiled=True),
        lax.all_gather(sectioned[13], "pages", axis=0, tiled=True),
    )
    (
        whole_qkv,
        whole_qkv_bias,
        whole_relq,
        whole_relk,
        whole_out,
        whole_out_bias,
        whole_gain_one,
        whole_shift_one,
        whole_up,
        whole_up_bias,
        whole_down,
        whole_down_bias,
        whole_gain_two,
        whole_shift_two,
    ) = whole_set
    pages_dev, tok_blk, width = hidden.shape
    heads = width // HEAD_DIM
    row_count = pages_dev * tok_blk
    cycle_size = lax.axis_size("blk")
    place_idx = lax.axis_index("blk")
    flat_rows = hidden.reshape(row_count, width)
    qkv_wide = jnp.dot(
        flat_rows, whole_qkv, preferred_element_type=jnp.float32
    ) + whole_qkv_bias.astype(jnp.float32)
    qkv_low = qkv_wide.astype(jnp.bfloat16)
    queries = qkv_low[:, :width].reshape(pages_dev, tok_blk, heads, HEAD_DIM)
    own_kv = qkv_low[:, width:].reshape(pages_dev, tok_blk, 2 * width)
    feat_low = box_features(boxes).astype(jnp.bfloat16)
    feat_wide = feat_low.astype(jnp.float32)
    span = feat_wide.shape[-1] // 2
    cos_own, sin_own = (feat_wide[..., :span], feat_wide[..., span:])
    relq_heads = whole_relq.reshape(2 * span, heads, HEAD_DIM)
    relk_heads = whole_relk.reshape(2 * span, heads, HEAD_DIM)
    rel_in = jnp.einsum("pthc,rhc->pthr", queries, relq_heads, preferred_element_type=jnp.float32)
    query_rel = turn_query(rel_in, cos_own, sin_own).astype(jnp.bfloat16)
    query_hat = jnp.concatenate(
        [queries, query_rel, jnp.broadcast_to(feat_low[:, :, None, :], query_rel.shape)], axis=-1
    )
    row_max = jnp.full((pages_dev, heads, tok_blk), -1e30, jnp.float32)
    row_sum = jnp.zeros((pages_dev, heads, tok_blk), jnp.float32)
    context_acc = jnp.zeros((pages_dev, tok_blk, heads, HEAD_DIM), jnp.float32)
    moving_kv, moving_extra = (own_kv, feat_low)
    for cycle_step in range(cycle_size):
        key_hat, value_rows, key_rows, cos_key, sin_key = key_block(
            moving_kv, moving_extra, whole_relk, heads
        )
        usable = key_mask(lengths, (place_idx - cycle_step) % cycle_size, tok_blk)[:, None, None, :]
        scores = 0.125 * jnp.einsum(
            "pqhc,pkhc->phqk", query_hat, key_hat, preferred_element_type=jnp.float32
        )
        masked = jnp.where(usable, scores, -1e30)
        new_max = jnp.maximum(row_max, jnp.max(masked, axis=-1))
        fresh = jnp.where(usable, jnp.exp(masked - new_max[..., None]), 0.0)
        factor = jnp.exp(row_max - new_max)
        row_sum = row_sum * factor + jnp.sum(fresh, axis=-1)
        fresh_low = fresh.astype(jnp.bfloat16)
        context_acc = context_acc * jnp.transpose(factor, (0, 2, 1))[..., None] + jnp.einsum(
            "phqk,pkhc->pqhc", fresh_low, value_rows, preferred_element_type=jnp.float32
        )
        row_max = new_max
        if cycle_step + 1 < cycle_size:
            moving_kv, moving_extra = passed_along((moving_kv, moving_extra), "blk", 1)
    log_norm = row_max + jnp.log(row_sum)
    context = context_acc / jnp.transpose(row_sum, (0, 2, 1))[..., None]
    ctx_low = context.reshape(row_count, width).astype(jnp.bfloat16)
    attn_out = jnp.dot(
        ctx_low, whole_out, preferred_element_type=jnp.float32
    ) + whole_out_bias.astype(jnp.float32)
    normed_one, back_one = jax.vjp(
        normalize,
        flat_rows.astype(jnp.float32) + attn_out,
        whole_gain_one.astype(jnp.float32),
        whole_shift_one.astype(jnp.float32),
    )
    normed_low = normed_one.astype(jnp.bfloat16)
    middle_rows = jnp.dot(
        normed_low, whole_up, preferred_element_type=jnp.float32
    ) + whole_up_bias.astype(jnp.float32)
    activated, gelu_back = jax.vjp(exact_gelu, middle_rows)
    act_low = activated.astype(jnp.bfloat16)
    branch_out = jnp.dot(
        act_low, whole_down, preferred_element_type=jnp.float32
    ) + whole_down_bias.astype(jnp.float32)
    result, back_two = jax.vjp(
        normalize,
        normed_one + branch_out,
        whole_gain_two.astype(jnp.float32),
        whole_shift_two.astype(jnp.float32),
    )
    grad_resid_two, grad_gain_two, grad_shift_two = back_two(
        cotangent.reshape(row_count, width).astype(jnp.float32)
    )
    grad_branch = grad_resid_two.astype(jnp.bfloat16)
    grad_down = jnp.dot(act_low.T, grad_branch, preferred_element_type=jnp.float32)
    grad_down_bias = jnp.sum(grad_branch.astype(jnp.float32), axis=0)
    (grad_middle,) = gelu_back(
        jnp.dot(grad_branch, whole_down.T, preferred_element_type=jnp.float32)
    )
    middle_low = grad_middle.astype(jnp.bfloat16)
    grad_up = jnp.dot(normed_low.T, middle_low, preferred_element_type=jnp.float32)
    grad_up_bias = jnp.sum(middle_low.astype(jnp.float32), axis=0)
    grad_normed = grad_resid_two + jnp.dot(
        middle_low, whole_up.T, preferred_element_type=jnp.float32
    )
    grad_resid_one, grad_gain_one, grad_shift_one = back_one(grad_normed)
    attn_low = grad_resid_one.astype(jnp.bfloat16)
    grad_out = jnp.dot(ctx_low.T, attn_low, preferred_element_type=jnp.float32)
    grad_out_bias = jnp.sum(attn_low.astype(jnp.float32), axis=0)
    grad_ctx = (
        jnp.dot(attn_low, whole_out.T, preferred_element_type=jnp.float32)
        .astype(jnp.bfloat16)
        .reshape(pages_dev, tok_blk, heads, HEAD_DIM)
    )
    ctx_heads = ctx_low.reshape(pages_dev, tok_blk, heads, HEAD_DIM)
    delta = jnp.einsum(
        "pqhc,pqhc->phq",
        grad_ctx.astype(jnp.float32),
        ctx_heads.astype(jnp.float32),
        precision=precise,
    )
    grad_hat = jnp.zeros(query_hat.shape, jnp.float32)
    grad_relk = jnp.zeros(relk_heads.shape, jnp.float32)
    travel = jnp.zeros((pages_dev, tok_blk, 2 * width), jnp.float32)
    moving_kv, moving_extra = (own_kv, feat_low)
    for cycle_step in range(cycle_size):
        key_hat, value_rows, key_rows, cos_key, sin_key = key_block(
            moving_kv, moving_extra, whole_relk, heads
        )
        usable = key_mask(lengths, (place_idx - cycle_step) % cycle_size, tok_blk)[:, None, None, :]
        scores = 0.125 * jnp.einsum(
            "pqhc,pkhc->phqk", query_hat, key_hat, preferred_element_type=jnp.float32
        )
        attention = jnp.where(usable, jnp.exp(scores - log_norm[..., None]), 0.0)
        attention_low = attention.astype(jnp.bfloat16)
        grad_attention = jnp.einsum(
            "pqhc,pkhc->phqk", grad_ctx, value_rows, preferred_element_type=jnp.float32
        )
        grad_scores = (attention * (grad_attention - delta[..., None])).astype(jnp.bfloat16)
        grad_hat = grad_hat + 0.125 * jnp.einsum(
            "phqk,pkhc->pqhc", grad_scores, key_hat, preferred_element_type=jnp.float32
        )
        grad_key_hat = 0.125 * jnp.einsum(
            "phqk,pqhc->pkhc", grad_scores, query_hat, preferred_element_type=jnp.float32
        )
        grad_values = jnp.einsum(
            "phqk,pqhc->pkhc", attention_low, grad_ctx, preferred_element_type=jnp.float32
        )
        key_turned = unturn_key(grad_key_hat[..., HEAD_DIM + 2 * span :], cos_key, sin_key).astype(
            jnp.bfloat16
        )
        grad_relk = grad_relk + jnp.einsum(
            "pthc,pthr->rhc", key_rows, key_turned, preferred_element_type=jnp.float32
        )
        grad_key_extra = jnp.einsum(
            "pthr,rhc->pthc", key_turned, relk_heads, preferred_element_type=jnp.float32
        )
        grad_keys = grad_key_hat[..., :HEAD_DIM] + grad_key_extra
        block_grad = jnp.concatenate(
            [
                grad_keys.reshape(pages_dev, tok_blk, width),
                grad_values.reshape(pages_dev, tok_blk, width),
            ],
            axis=-1,
        )
        travel = passed_along((travel + block_grad).astype(jnp.bfloat16), "blk", 1).astype(
            jnp.float32
        )
        if cycle_step + 1 < cycle_size:
            moving_kv, moving_extra = passed_along((moving_kv, moving_extra), "blk", 1)
    grad_queries = grad_hat[..., :HEAD_DIM]
    grad_qrel = grad_hat[..., HEAD_DIM : HEAD_DIM + 2 * span]

    def query_turn(rel_vals):
        return turn_query(rel_vals, cos_own, sin_own)

    _, query_back = jax.vjp(query_turn, rel_in)
    (grad_rel_in,) = query_back(grad_qrel)
    rel_low = grad_rel_in.astype(jnp.bfloat16)
    grad_relq = jnp.einsum(
        "pthc,pthr->rhc", queries, rel_low, preferred_element_type=jnp.float32
    ).reshape(2 * span, width)
    grad_queries = grad_queries + jnp.einsum(
        "pthr,rhc->pthc", rel_low, relq_heads, preferred_element_type=jnp.float32
    )
    grad_qkv = jnp.concatenate(
        [grad_queries.reshape(row_count, width), travel.reshape(row_count, 2 * width)], axis=-1
    ).astype(jnp.bfloat16)
    grad_w_qkv = jnp.dot(flat_rows.T, grad_qkv, preferred_element_type=jnp.float32)
    grad_qkv_bias = jnp.sum(grad_qkv.astype(jnp.float32), axis=0)
    grad_input = (
        (grad_resid_one + jnp.dot(grad_qkv, whole_qkv.T, preferred_element_type=jnp.float32))
        .astype(jnp.bfloat16)
        .reshape(pages_dev, tok_blk, width)
    )
    grad_relk_flat = grad_relk.reshape(2 * span, width)
    grad_set = (
        grad_w_qkv,
        grad_qkv_bias,
        grad_relq,
        grad_relk_flat,
        grad_out,
        grad_out_bias,
        grad_gain_one,
        grad_shift_one,
        grad_up,
        grad_up_bias,
        grad_down,
        grad_down_bias,
        grad_gain_two,
        grad_shift_two,
    )
    partial_set = (
        lax.psum_scatter(grad_set[0], "pages", scatter_dimension=0, tiled=True),
        lax.psum_scatter(grad_set[1], "pages", scatter_dimension=0, tiled=True),
        lax.psum_scatter(grad_set[2], "pages", scatter_dimension=0, tiled=True),
        lax.psum_scatter(grad_set[3], "pages", scatter_dimension=0, tiled=True),
        lax.psum_scatter(grad_set[4], "pages", scatter_dimension=0, tiled=True),
        lax.psum_scatter(grad_set[5], "pages", scatter_dimension=0, tiled=True),
        lax.psum_scatter(grad_set[6], "pages", scatter_dimension=0, tiled=True),
        lax.psum_scatter(grad_set[7], "pages", scatter_dimension=0, tiled=True),
        lax.psum_scatter(grad_set[8], "pages", scatter_dimension=0, tiled=True),
        lax.psum_scatter(grad_set[9], "pages", scatter_dimension=0, tiled=True),
        lax.psum_scatter(grad_set[10], "pages", scatter_dimension=0, tiled=True),
        lax.psum_scatter(grad_set[11], "pages", scatter_dimension=0, tiled=True),
        lax.psum_scatter(grad_set[12], "pages", scatter_dimension=0, tiled=True),
        lax.psum_scatter(grad_set[13], "pages", scatter_dimension=0, tiled=True),
    )
    summed_set = (
        lax.psum_scatter(
            partial_set[0].astype(jnp.bfloat16), "blk", scatter_dimension=0, tiled=True
        ).astype(jnp.float32),
        lax.psum_scatter(
            partial_set[1].astype(jnp.bfloat16), "blk", scatter_dimension=0, tiled=True
        ).astype(jnp.float32),
        lax.psum_scatter(
            partial_set[2].astype(jnp.bfloat16), "blk", scatter_dimension=0, tiled=True
        ).astype(jnp.float32),
        lax.psum_scatter(
            partial_set[3].astype(jnp.bfloat16), "blk", scatter_dimension=0, tiled=True
        ).astype(jnp.float32),
        lax.psum_scatter(
            partial_set[4].astype(jnp.bfloat16), "blk", scatter_dimension=0, tiled=True
        ).astype(jnp.float32),
        lax.psum_scatter(
            partial_set[5].astype(jnp.bfloat16), "blk", scatter_dimension=0, tiled=True
        ).astype(jnp.float32),
        lax.psum_scatter(
            partial_set[6].astype(jnp.bfloat16), "blk", scatter_dimension=0, tiled=True
        ).astype(jnp.float32),
        lax.psum_scatter(
            partial_set[7].astype(jnp.bfloat16), "blk", scatter_dimension=0, tiled=True
        ).astype(jnp.float32),
        lax.psum_scatter(
            partial_set[8].astype(jnp.bfloat16), "blk", scatter_dimension=0, tiled=True
        ).astype(jnp.float32),
        lax.psum_scatter(
            partial_set[9].astype(jnp.bfloat16), "blk", scatter_dimension=0, tiled=True
        ).astype(jnp.float32),
        lax.psum_scatter(
            partial_set[10].astype(jnp.bfloat16), "blk", scatter_dimension=0, tiled=True
        ).astype(jnp.float32),
        lax.psum_scatter(
            partial_set[11].astype(jnp.bfloat16), "blk", scatter_dimension=0, tiled=True
        ).astype(jnp.float32),
        lax.psum_scatter(
            partial_set[12].astype(jnp.bfloat16), "blk", scatter_dimension=0, tiled=True
        ).astype(jnp.float32),
        lax.psum_scatter(
            partial_set[13].astype(jnp.bfloat16), "blk", scatter_dimension=0, tiled=True
        ).astype(jnp.float32),
    )
    return (result.astype(jnp.bfloat16).reshape(pages_dev, tok_blk, width), grad_input) + tuple(
        summed_set
    )


def solution(mesh):
    return jax.shard_map(
        on_device,
        mesh=mesh,
        in_specs=(
            P("pages", "blk", None),
            P("pages", "blk", None),
            P("pages"),
            P(("pages", "blk"), None),
            P(("pages", "blk")),
            P(("pages", "blk"), None),
            P(("pages", "blk"), None),
            P(("pages", "blk"), None),
            P(("pages", "blk")),
            P(("pages", "blk")),
            P(("pages", "blk")),
            P(("pages", "blk"), None),
            P(("pages", "blk")),
            P(("pages", "blk"), None),
            P(("pages", "blk")),
            P(("pages", "blk")),
            P(("pages", "blk")),
            P("pages", "blk", None),
        ),
        out_specs=(
            P("pages", "blk", None),
            P("pages", "blk", None),
            P(("pages", "blk"), None),
            P(("pages", "blk")),
            P(("pages", "blk"), None),
            P(("pages", "blk"), None),
            P(("pages", "blk"), None),
            P(("pages", "blk")),
            P(("pages", "blk")),
            P(("pages", "blk")),
            P(("pages", "blk"), None),
            P(("pages", "blk")),
            P(("pages", "blk"), None),
            P(("pages", "blk")),
            P(("pages", "blk")),
            P(("pages", "blk")),
        ),
        check_vma=False,
    )
```

profile of v0, /device:TPU:0, one launch (start us, length us, event | category | flops | bytes accessed | tf_op | source)
XLA Modules:
  0.0 1216.0 jit_solution(6600283643279100901)
XLA Ops:
  7.2 8.6 all_gather.88
  15.9 6.2 all_gather.90
  22.1 8.7 all_gather.84
  30.9 6.2 all_gather.92
  37.2 9.5 all_gather.100
  48.1 9.0 all_gather.104
  63.8 6.3 all-reduce.36
  71.6 37.3 %all-reduce.34 = (bf16[2304]{0:T(1024)(128)(2,1)S(1)}, bf16[768]{0:T(1024)(128)(2,1)S(1)}, bf16[768]{0:T(1024)(128)(2,1)S(1)}, bf16[768]{0:T(1024)(128)(2,1)S(1)...) all-reduce(bf16[2304]{0:T(1024)(128)(2,1)S(1)} %dynamic-update-slic, ...), channel_id=1, replica_groups=mesh['pages'=8,'blk'=4] {'pages'}, use_global_device_ids=true, to_apply=%add.3 | all-reduce | flops 6912 | bytes 27648
  111.9 26.1 %all-gather = bf16[8,1,384]{2,1,0:T(2,128)(2,1)S(1)} all-gather(bf16[1,1,384]{2,1,0:T(2,128)(2,1)S(1)} %reshape.1274), channel_id=1, replica_groups=mesh['pages'=8,'blk'=4] {'pages'}, dimensions={0}, use_global_device_ids=true | all-gather | bytes 6912 | tf_op jit(solution)/shard_map/all_gather | solution.py:162
  140.6 4.3 collective-permute-done.3
  145.7 4.3 collective-permute-done.5
  154.5 11.5 all-gather.8.cloned.1.call-done
  166.0 2.6 fusion
  176.6 3.2 select_reduce_fusion.3
  186.3 2.3 select_reduce_fusion.2
  197.2 2.3 copy-done.45
  199.5 2.3 select_reduce_fusion.1
  210.5 2.3 copy-done.46
  222.8 65.4 %all-gather.16.cloned.1.call-done = bf16[768,3072]{1,0:T(8,128)(2,1)} async-done(((bf16[96,3072]{1,0:T(8,128)(2,1)}), bf16[768,3072]{1,0:T(8,128)(2,1)}) %all-gather.16.cloned.1.call-update) | async-done | bytes 4718608 | tf_op jit(solution)/shard_map/all_gather | solution.py:161
  288.3 9.0 multiply_convert_fusion
  297.2 71.1 %all-gather.18.cloned.1.call-done = bf16[3072,768]{1,0:T(8,128)(2,1)} async-done(((bf16[384,768]{1,0:T(8,128)(2,1)}), bf16[3072,768]{1,0:T(8,128)(2,1)}) %all-gather.18.cloned.1.call-update) | async-done | bytes 4718608 | tf_op jit(solution)/shard_map/all_gather | solution.py:163
  368.4 3.6 fusion.198
  374.7 2.5 convert_reduce_fusion
  377.2 2.4 multiply_reduce_fusion
  391.3 7.8 fusion.3
  400.9 4.7 fusion.5
  405.7 4.7 fusion.7
  410.4 4.6 multiply_bitcast_fusion.4
  415.0 17.0 %multiply_bitcast_fusion = f32[1,128,12,1600]{1,3,2,0:T(8,128)} fusion(f32[12,1600,128]{2,1,0:T(8,128)} %fusion.3, f32[12,1600,128]{2,1,0:T(8,128)} %fusion.7, f32[12,1600,128]{2,1,0:T(8,128)} %fusion.5, bf16[12,128,128]{1,2,0:T(8,128)(2,1)} %fusion.33, bf16[1,128,12,384]{1,3,2,0:T(8,128)(2,1)} %copy-done.21, bf16[1,128,12,384]{1,3,2,0:T(8,128)(2,1)} %copy-done.20, ...), kind=kOutput, calls=%fused_computation | convolution fusion | flops 658636800 | bytes 44630016 | tf_op jit(solution)/shard_map/phqk,pkhc->pqhc/dot_general | solution.py:307
  432.0 6.6 multiply_add_fusion.1
  438.6 2.3 fusion.126
  440.9 3.0 copy.309
  444.1 2.7 fusion.20
  447.2 9.0 multiply_bitcast_fusion.3
  456.2 3.1 fusion.54
  460.8 4.6 multiply_bitcast_fusion.2
  465.4 3.1 fusion.56
  469.9 4.5 multiply_bitcast_fusion.1
  474.3 3.1 fusion.58
  477.5 2.3 add_add_fusion
  479.8 3.1 copy.314
  484.7 2.4 fusion.60
  489.4 5.0 collective-permute-done.6
  496.8 5.0 collective-permute-done.7
  504.4 4.9 collective-permute-done.8
  511.2 5.5 collective-permute-done.9
  517.5 4.0 convolution_bitcast_fusion
  521.5 8.1 copy.359
  530.9 5.0 fusion.183
  537.1 5.1 fusion.200
  545.7 56.5 %reduce-scatter.21.cloned.1.call-done = f32[96,768]{1,0:T(8,128)} async-done(((f32[768,768]{1,0:T(8,128)}), f32[96,768]{1,0:T(8,128)}) %reduce-scatter.21.cloned.1.call-update) | async-done | bytes 294928 | tf_op jit(solution)/shard_map/reduce_scatter | solution.py:384
  603.9 129.9 %reduce-scatter.37.cloned.1.call-done = f32[96,2304]{1,0:T(8,128)} async-done(((f32[768,2304]{1,0:T(8,128)}), f32[96,2304]{1,0:T(8,128)}) %reduce-scatter.37.cloned.1.call-update) | async-done | bytes 884752
  736.4 163.8 %reduce-scatter.29.cloned.1.call-done = f32[96,3072]{1,0:T(8,128)} async-done(((f32[768,3072]{1,0:T(8,128)}), f32[96,3072]{1,0:T(8,128)}) %reduce-scatter.29.cloned.1.call-update) | async-done | bytes 1179664 | tf_op jit(solution)/shard_map/reduce_scatter | solution.py:389
  900.2 2.2 convert_element_type.433
  909.6 39.5 %all-reduce.33 = (bf16[2304]{0:T(1024)(128)(2,1)}, bf16[768]{0:T(1024)(128)(2,1)}, bf16[768]{0:T(1024)(128)(2,1)}, bf16[768]{0:T(1024)(128)(2,1)}, bf16[3072]{0:...) all-reduce(f32[2304]{0:T(1024)S(1)} %convert_reduce_fusion.1, ...), channel_id=4, replica_groups=mesh['pages'=8,'blk'=4] {'pages'}, use_global_device_ids=true, to_apply=%region_19.20.clone | all-reduce | flops 9984 | bytes 59904
  957.6 6.8 all-reduce.35
  964.4 103.0 %reduce-scatter.33.cloned.1.call-done = f32[384,768]{1,0:T(8,128)} async-done(((f32[3072,768]{1,0:T(8,128)}), f32[384,768]{1,0:T(8,128)}) %reduce-scatter.33.cloned.1.call-update) | async-done | bytes 1179664 | tf_op jit(solution)/shard_map/reduce_scatter | solution.py:391
  1077.5 3.2 fusion.63
  1080.7 8.0 reduce-scatter.27.cloned.1.call-done
  1090.1 21.3 %reduce-scatter.19.cloned.1.call-done = bf16[24,768]{1,0:T(8,128)(2,1)} async-done(((bf16[96,768]{1,0:T(8,128)(2,1)}), bf16[24,768]{1,0:T(8,128)(2,1)}) %reduce-scatter.19.cloned.1.call-update) | async-done | bytes 36880 | tf_op jit(solution)/shard_map/reduce_scatter | solution.py:403
  1112.8 21.3 %reduce-scatter.23.cloned.1.call-done = bf16[24,768]{1,0:T(8,128)(2,1)} async-done(((bf16[96,768]{1,0:T(8,128)(2,1)}), bf16[24,768]{1,0:T(8,128)(2,1)}) %reduce-scatter.23.cloned.1.call-update) | async-done | bytes 36880 | tf_op jit(solution)/shard_map/reduce_scatter | solution.py:406
  1135.5 22.3 %reduce-scatter.39.cloned.1.call-done = bf16[24,2304]{1,0:T(8,128)(2,1)} async-done(((bf16[96,2304]{1,0:T(8,128)(2,1)}), bf16[24,2304]{1,0:T(8,128)(2,1)}) %reduce-scatter.39.cloned.1.call-update) | async-done | bytes 110608
  1160.0 22.4 %reduce-scatter.31.cloned.1.call-done = bf16[24,3072]{1,0:T(8,128)(2,1)} async-done(((bf16[96,3072]{1,0:T(8,128)(2,1)}), bf16[24,3072]{1,0:T(8,128)(2,1)}) %reduce-scatter.31.cloned.1.call-update) | async-done | bytes 147472 | tf_op jit(solution)/shard_map/reduce_scatter | solution.py:421
  1184.0 23.0 %reduce-scatter.35.cloned.1.call-done = bf16[96,768]{1,0:T(8,128)(2,1)} async-done(((bf16[384,768]{1,0:T(8,128)(2,1)}), bf16[96,768]{1,0:T(8,128)(2,1)}) %reduce-scatter.35.cloned.1.call-update) | async-done | bytes 147472 | tf_op jit(solution)/shard_map/reduce_scatter | solution.py:427
  (588 shorter events, 129.5 us)
Async XLA Ops:
  7.2 39.6 %copy-start.162 = (s32[1,128,2]{1,2,0:T(2,128)S(1)}, s32[1,128,2]{1,2,0:T(2,128)}, u32[]{:S(2)}) copy-start(s32[1,128,2]{1,2,0:T(2,128)} %param.19) | copy-start | bytes 3076
  7.2 40.9 %copy-start.126 = (bf16[96,768]{1,0:T(8,128)(2,1)S(1)}, bf16[96,768]{1,0:T(8,128)(2,1)}, u32[]{:S(2)}) copy-start(bf16[96,768]{1,0:T(8,128)(2,1)} %param.31) | copy-start | bytes 442372
  7.2 143.6 %all-gather.10.cloned.1.call-start = ((), (), s32[]{:S(2)}) async-start(), calls=%async_computation.13 | async-start | bytes 1327104 | tf_op jit(solution)/shard_map/all_gather | solution.py:155
  15.8 136.6 %all-gather.12.cloned.1.call-start = ((), (), s32[]{:S(2)}) async-start(), calls=%async_computation.14 | async-start | bytes 1327104 | tf_op jit(solution)/shard_map/all_gather | solution.py:156
  22.1 143.9 %all-gather.8.cloned.1.call-start = ((), (), s32[]{:S(2)}) async-start(), calls=%async_computation.12 | async-start | bytes 3981312 | tf_op jit(solution)/shard_map/all_gather | solution.py:153
  30.8 187.7 %all-gather.14.cloned.1.call-start = ((), (), s32[]{:S(2)}) async-start(), calls=%async_computation.15 | async-start | bytes 1327104 | tf_op jit(solution)/shard_map/all_gather | solution.py:157
  37.0 20.9 %copy-start.158 = (u32[32]{0:T(128)S(1)}, u32[32]{0:T(128)}, u32[]{:S(2)}) copy-start(u32[32]{0:T(128)} %constant.164) | copy-start | bytes 388
  37.0 20.9 %copy-start.159 = (u32[32]{0:T(128)S(1)}, u32[32]{0:T(128)}, u32[]{:S(2)}) copy-start(u32[32]{0:T(128)} %constant.159) | copy-start | bytes 388
  37.0 24.8 %copy-start.167 = (bf16[24]{0:T(256)(128)(2,1)S(1)}, bf16[24]{0:T(256)(128)(2,1)}, u32[]{:S(2)}) copy-start(bf16[24]{0:T(256)(128)(2,1)} %param.34) | copy-start | bytes 148
  37.0 25.1 %copy-start.168 = (bf16[24]{0:T(256)(128)(2,1)S(1)}, bf16[24]{0:T(256)(128)(2,1)}, u32[]{:S(2)}) copy-start(bf16[24]{0:T(256)(128)(2,1)} %param.33) | copy-start | bytes 148
  37.0 25.3 %copy-start.169 = (bf16[24]{0:T(256)(128)(2,1)S(1)}, bf16[24]{0:T(256)(128)(2,1)}, u32[]{:S(2)}) copy-start(bf16[24]{0:T(256)(128)(2,1)} %param.32) | copy-start | bytes 148
  37.1 25.6 %copy-start.170 = (bf16[24]{0:T(256)(128)(2,1)S(1)}, bf16[24]{0:T(256)(128)(2,1)}, u32[]{:S(2)}) copy-start(bf16[24]{0:T(256)(128)(2,1)} %param.28) | copy-start | bytes 148
  37.1 25.8 %copy-start.171 = (bf16[24]{0:T(256)(128)(2,1)S(1)}, bf16[24]{0:T(256)(128)(2,1)}, u32[]{:S(2)}) copy-start(bf16[24]{0:T(256)(128)(2,1)} %param.27) | copy-start | bytes 148
  37.1 26.0 %copy-start.172 = (bf16[24]{0:T(256)(128)(2,1)S(1)}, bf16[24]{0:T(256)(128)(2,1)}, u32[]{:S(2)}) copy-start(bf16[24]{0:T(256)(128)(2,1)} %param.26) | copy-start | bytes 148
  37.1 26.3 %copy-start.173 = (bf16[72]{0:T(256)(128)(2,1)S(1)}, bf16[72]{0:T(256)(128)(2,1)}, u32[]{:S(2)}) copy-start(bf16[72]{0:T(256)(128)(2,1)} %param.22) | copy-start | bytes 436
  37.1 26.5 %copy-start.174 = (bf16[96]{0:T(256)(128)(2,1)S(1)}, bf16[96]{0:T(256)(128)(2,1)}, u32[]{:S(2)}) copy-start(bf16[96]{0:T(256)(128)(2,1)} %param.30) | copy-start | bytes 580
  37.1 251.2 %all-gather.16.cloned.1.call-start = ((), (), s32[]{:S(2)}) async-start(), calls=%async_computation.16 | async-start | bytes 5308416 | tf_op jit(solution)/shard_map/all_gather | solution.py:161
  46.7 321.7 %all-gather.18.cloned.1.call-start = ((), (), s32[]{:S(2)}) async-start(), calls=%async_computation.17 | async-start | bytes 5308416 | tf_op jit(solution)/shard_map/all_gather | solution.py:163
  47.7 92.0 %collective-permute-start.1 = (bf16[1,128,768]{1,2,0:T(8,128)(2,1)S(1)}, bf16[1,128,768]{1,2,0:T(8,128)(2,1)S(1)}, u32[]{:S(2)}, u32[]{:S(2)}) collective-permute-start(bf16[1,128,768]{1,2,0:T(8,128)(2,1)S(1)} %get-tuple-element.172), channel_id=1, source_target_pairs={{3,0},{0,1},{1,2},{2,3},{7,4},{4,5},{5,6},{6,7},{11,8},{8,9},{9,10... | collective-permute-start | bytes 589832 | tf_op jit(solution)/shard_map/ppermute | solution.py:18
  57.1 485.1 %reduce-scatter.25.cloned.1.call-start = ((), (), s32[]{:S(2)}) async-start(), calls=%async_computation.22 | async-start | bytes 2654208 | tf_op jit(solution)/shard_map/reduce_scatter | solution.py:385
  139.6 56.9 %copy-start.146 = (pred[128]{0:T(512)(128)(4,1)}, pred[128]{0:T(512)(128)(4,1)S(1)}, u32[]{:S(2)}) copy-start(pred[128]{0:T(512)(128)(4,1)S(1)} %add_compare_fusion.1) | copy-start | bytes 388
  139.6 46.0 %copy-start.149 = (pred[128]{0:T(512)(128)(4,1)}, pred[128]{0:T(512)(128)(4,1)S(1)}, u32[]{:S(2)}) copy-start(pred[128]{0:T(512)(128)(4,1)S(1)} %add_compare_fusion.2) | copy-start | bytes 388
  139.7 34.7 %copy-start.52 = (f32[128,384]{0,1:T(8,128)}, f32[128,384]{0,1:T(8,128)S(1)}, u32[]{:S(2)}) copy-start(f32[128,384]{0,1:T(8,128)S(1)} %get-tuple-element.168) | copy-start | bytes 589828
  139.7 34.7 %copy-start.53 = (f32[128,384]{0,1:T(8,128)}, f32[128,384]{0,1:T(8,128)S(1)}, u32[]{:S(2)}) copy-start(f32[128,384]{0,1:T(8,128)S(1)} %get-tuple-element.169) | copy-start | bytes 589828
  139.7 10.3 copy-start.109
  139.7 5.1 collective-permute-start.3
  140.6 42.2 %copy-start.78 = (f32[128,384]{0,1:T(8,128)}, f32[128,384]{0,1:T(8,128)S(1)}, u32[]{:S(2)}) copy-start(f32[128,384]{0,1:T(8,128)S(1)} %get-tuple-element.164) | copy-start | bytes 589828
  144.9 5.1 collective-permute-start.5
  150.8 15.1 %copy-start.60 = (bf16[1,128,768]{2,1,0:T(8,128)(2,1)S(1)}, bf16[1,128,768]{2,1,0:T(8,128)(2,1)}, u32[]{:S(2)}) copy-start(bf16[1,128,768]{2,1,0:T(8,128)(2,1)} %param.18) | copy-start | bytes 589828
  152.4 21.1 %copy-start.11 = (bf16[768,768]{0,1:T(8,128)(2,1)}, bf16[768,768]{0,1:T(8,128)(2,1)S(1)}, u32[]{:S(2)}) copy-start(bf16[768,768]{0,1:T(8,128)(2,1)S(1)} %copy.263) | copy-start | bytes 3538948
  171.2 9.4 collective-permute-start
  171.5 14.1 %copy-start.62 = (bf16[128,768]{0,1:T(8,128)(2,1)}, bf16[128,768]{0,1:T(8,128)(2,1)S(1)}, u32[]{:S(2)}) copy-start(bf16[128,768]{0,1:T(8,128)(2,1)S(1)} %copy.261) | copy-start | bytes 589828
  172.7 233.0 %copy-start.54 = (bf16[1,128,768]{1,2,0:T(8,128)(2,1)}, bf16[1,128,768]{1,2,0:T(8,128)(2,1)S(1)}, u32[]{:S(2)}) copy-start(bf16[1,128,768]{1,2,0:T(8,128)(2,1)S(1)} %copy.265) | copy-start | bytes 589828
  181.8 218.7 %copy-start.55 = (bf16[1,128,768]{1,2,0:T(8,128)(2,1)}, bf16[1,128,768]{1,2,0:T(8,128)(2,1)S(1)}, u32[]{:S(2)}) copy-start(bf16[1,128,768]{1,2,0:T(8,128)(2,1)S(1)} %copy.271) | copy-start | bytes 589828
  183.6 7.6 collective-permute-start.2
  188.6 196.8 %copy-start.7 = (f32[12,128,128]{1,2,0:T(8,128)}, f32[12,128,128]{1,2,0:T(8,128)S(1)}, u32[]{:S(2)}) copy-start(f32[12,128,128]{1,2,0:T(8,128)S(1)} %get-tuple-element.195) | copy-start | bytes 2359300
  193.1 10.7 collective-permute-start.4
  201.8 185.7 %copy-start.9 = (f32[12,128,128]{1,2,0:T(8,128)}, f32[12,128,128]{1,2,0:T(8,128)S(1)}, u32[]{:S(2)}) copy-start(f32[12,128,128]{1,2,0:T(8,128)S(1)} %get-tuple-element.193) | copy-start | bytes 2359300
  220.3 159.3 %copy-start.4 = (f32[128,768]{1,0:T(8,128)}, f32[128,768]{1,0:T(8,128)S(1)}, u32[]{:S(2)}) copy-start(f32[128,768]{1,0:T(8,128)S(1)} %get-tuple-element.199) | copy-start | bytes 1179652
  384.3 15.9 %copy-start.2 = (bf16[128,768]{0,1:T(8,128)(2,1)}, bf16[128,768]{0,1:T(8,128)(2,1)S(1)}, u32[]{:S(2)}) copy-start(bf16[128,768]{0,1:T(8,128)(2,1)S(1)} %copy.286) | copy-start | bytes 589828
  391.2 9.1 copy-start.19
  391.2 152.9 %reduce-scatter.17.cloned.1.call-start = ((), (), s32[]{:S(2)}) async-start(), calls=%async_computation.18 | async-start | bytes 2654208 | tf_op jit(solution)/shard_map/reduce_scatter | solution.py:383
  391.3 9.3 copy-start.104
  391.3 9.3 copy-start.106
  444.0 158.2 %reduce-scatter.21.cloned.1.call-start = ((), (), s32[]{:S(2)}) async-start(), calls=%async_computation.20 | async-start | bytes 2654208 | tf_op jit(solution)/shard_map/reduce_scatter | solution.py:384
  482.9 250.9 %reduce-scatter.37.cloned.1.call-start = ((), (), s32[]{:S(2)}) async-start(), calls=%async_computation.28 | async-start | bytes 7962624
  487.2 7.3 collective-permute-start.6
  494.5 7.3 collective-permute-start.7
  501.9 7.5 collective-permute-start.8
  509.5 7.3 collective-permute-start.9
  529.7 370.6 %reduce-scatter.29.cloned.1.call-start = ((), (), s32[]{:S(2)}) async-start(), calls=%async_computation.24 | async-start | bytes 10616832 | tf_op jit(solution)/shard_map/reduce_scatter | solution.py:389
  536.0 531.4 %reduce-scatter.33.cloned.1.call-start = ((), (), s32[]{:S(2)}) async-start(), calls=%async_computation.26 | async-start | bytes 10616832 | tf_op jit(solution)/shard_map/reduce_scatter | solution.py:391
  542.2 546.5 %reduce-scatter.27.cloned.1.call-start = ((), (), s32[]{:S(2)}) async-start(), calls=%async_computation.23 | async-start | bytes 184320 | tf_op jit(solution)/shard_map/reduce_scatter | solution.py:409
  543.9 567.5 %reduce-scatter.19.cloned.1.call-start = ((), (), s32[]{:S(2)}) async-start(), calls=%async_computation.19 | async-start | bytes 184320 | tf_op jit(solution)/shard_map/reduce_scatter | solution.py:403
  545.7 588.4 %reduce-scatter.23.cloned.1.call-start = ((), (), s32[]{:S(2)}) async-start(), calls=%async_computation.21 | async-start | bytes 184320 | tf_op jit(solution)/shard_map/reduce_scatter | solution.py:406
  603.9 553.9 %reduce-scatter.39.cloned.1.call-start = ((), (), s32[]{:S(2)}) async-start(), calls=%async_computation.29 | async-start | bytes 552960
  735.3 174.3 %copy-start.142 = (f32[768]{0:T(1024)S(1)}, f32[768]{0:T(1024)}, u32[]{:S(2)}) copy-start(f32[768]{0:T(1024)} %get-tuple-element.82) | copy-start | bytes 9220
  736.4 446.0 %reduce-scatter.31.cloned.1.call-start = ((), (), s32[]{:S(2)}) async-start(), calls=%async_computation.25 | async-start | bytes 737280 | tf_op jit(solution)/shard_map/reduce_scatter | solution.py:421
  902.4 175.1 %copy-start.6 = (bf16[768,2304]{1,0:T(8,128)(2,1)S(1)}, bf16[768,2304]{1,0:T(8,128)(2,1)}, u32[]{:S(2)}) copy-start(bf16[768,2304]{1,0:T(8,128)(2,1)} %all-gather.8.cloned.1.call-done) | copy-start | bytes 10616836
  902.4 304.6 %reduce-scatter.35.cloned.1.call-start = ((), (), s32[]{:S(2)}) async-start(), calls=%async_computation.27 | async-start | bytes 737280 | tf_op jit(solution)/shard_map/reduce_scatter | solution.py:427
  949.1 128.5 %copy-start.161 = (f32[128]{0:T(128)S(1)}, f32[128]{0:T(128)}, u32[]{:S(2)}) copy-start(f32[128]{0:T(128)} %copy-done.160) | copy-start | bytes 1540
  964.4 111.3 %copy-start.175 = (bf16[96]{0:T(256)(128)(2,1)S(1)}, bf16[96]{0:T(256)(128)(2,1)}, u32[]{:S(2)}) copy-start(bf16[96]{0:T(256)(128)(2,1)} %get-tuple-element.107) | copy-start | bytes 580
  964.4 111.9 %copy-start.166 = (bf16[384]{0:T(512)(128)(2,1)S(1)}, bf16[384]{0:T(512)(128)(2,1)}, u32[]{:S(2)}) copy-start(bf16[384]{0:T(512)(128)(2,1)} %get-tuple-element.104) | copy-start | bytes 2308
  964.4 112.5 %copy-start.165 = (bf16[288]{0:T(512)(128)(2,1)S(1)}, bf16[288]{0:T(512)(128)(2,1)}, u32[]{:S(2)}) copy-start(bf16[288]{0:T(512)(128)(2,1)} %get-tuple-element.100) | copy-start | bytes 1732
  (146 other events, 506.9 us)
Sparse Core Ops, SparseCore 0:
  16.0 41.3 all-gather.9
  59.5 40.0 all-gather.11
  101.8 64.0 all-gather.7
  168.0 39.5 all-gather.13
  209.6 78.6 all-gather.15
  290.3 78.0 all-gather.17
  391.3 67.3 reduce-scatter.24
  462.1 68.2 reduce-scatter.16
  533.9 68.2 reduce-scatter.20
  605.7 128.0 reduce-scatter.36
  737.8 162.3 reduce-scatter.28
  904.1 163.2 reduce-scatter.32
  1070.0 18.7 reduce-scatter.26
  1091.7 19.6 reduce-scatter.18
  1114.4 19.6 reduce-scatter.22
  1136.6 21.0 reduce-scatter.38
  1160.3 22.0 reduce-scatter.30
  1184.9 22.0 reduce-scatter.34
where the time goes:
time: 1230 us; the launch traced here: 1220 us
  waiting for transfers between devices  750 us (61%)
  blocking collectives  164 us (13%)
  matrix products  142 us (12%)
  local copies, waits for them, and re-layouts  70.4 us (6%)
  other arithmetic  59.7 us (5%)
  between operations  25.2 us (2%)
    reduce_scatter x1, waiting for transfers between devices, on_device(): lax.psum_scatter(grad_set[8], 'pages', scatter_dimension=0, tiled=True)  164 us
    unnamed x20, waiting for transfers between devices  152 us
    reduce_scatter x1, waiting for transfers between devices, on_device(): lax.psum_scatter(grad_set[10], 'pages', scatter_dimension=0, tiled=True)  103 us
    unnamed x4, blocking collectives  89.9 us
    all_gather x1, waiting for transfers between devices, on_device(): lax.all_gather(sectioned[10], 'pages', axis=0, tiled=True)  71.1 us
    all_gather x1, waiting for transfers between devices, on_device(): lax.all_gather(sectioned[8], 'pages', axis=0, tiled=True)  65.4 us
    reduce_scatter x1, waiting for transfers between devices, on_device(): lax.psum_scatter(grad_set[3], 'pages', scatter_dimension=0, tiled=True)  56.5 us
    unnamed x409, local copies, waits for them, and re-layouts  41.3 us
  transfers between devices with their start and end apart: 28, of which 20 were waited for; matrix products, arithmetic and copies ran while one was open for 19% of the time, Pallas kernels for 0%

commit v1 on v0

v1 whole, which is shorter than its diff:
```python
import functools
import math

import jax
import jax.numpy as jnp
from jax import lax
from jax.experimental import pallas as pl
from jax.experimental.pallas import tpu as pltpu
from jax.sharding import PartitionSpec as P

HEAD_DIM = 64
FREQ = 192
GRID_Z = 4
GRID_X = 2
GROUP = GRID_Z * GRID_X
BLK = 4
MESH = pl.DeviceIdType.MESH
F32 = jnp.float32
BF16 = jnp.bfloat16
VMEM_BYTES = 56 << 20


def mm(left, right):
    return jnp.dot(left, right, preferred_element_type=F32)


def mm_t(left, right):
    return lax.dot_general(left, right, (((1,), (1,)), ((), ())), preferred_element_type=F32)


def tmm(left, right):
    return lax.dot_general(left, right, (((0,), (0,)), ((), ())), preferred_element_type=F32)


class Place:
    def __init__(self, spread):
        pages = lax.axis_index("pages")
        self.spread = spread
        self.hi = pages // spread
        self.lo = pages % spread
        self.z = self.hi // GRID_X
        self.x = self.hi % GRID_X
        self.b = lax.axis_index("blk")
        self.pages = pages
        self.sib = self.b + 1 - 2 * (self.b % 2)
        self.across = (self.b + 2) % BLK
        self.diag = (self.sib + 2) % BLK

    def at(self, z, x):
        return ((z * GRID_X + x) * self.spread + self.lo, self.b)

    def in_page(self, b):
        return (self.pages, b)

    def blk_peers(self):
        return (self.sib, self.across, self.diag)

    def z_at(self, step):
        return (self.z + step) % GRID_Z


def remote(src, dst, send, recv, device):
    return pltpu.make_async_remote_copy(
        src_ref=src, dst_ref=dst, send_sem=send, recv_sem=recv, device_id=device, device_id_type=MESH
    )


def meet(devices):
    barrier = pltpu.get_barrier_semaphore()
    for device in devices:
        pl.semaphore_signal(barrier, inc=1, device_id=device, device_id_type=MESH)
    pl.semaphore_wait(barrier, len(devices))


class BlkGather:
    def __init__(self, place, dst, send, recv):
        self.place, self.dst = place, dst
        b, across = place.b, place.across
        self.to_sib = remote(dst.at[b], dst.at[b], send.at[0], recv.at[0], place.in_page(place.sib))
        self.to_across = remote(dst.at[b], dst.at[b], send.at[1], recv.at[1], place.in_page(across))
        self.forward = remote(
            dst.at[across], dst.at[across], send.at[2], recv.at[2], place.in_page(place.sib)
        )

    def start(self):
        self.to_across.start()
        self.to_sib.start()

    def wait_sib(self):
        self.to_sib.wait_recv()

    def wait_across(self):
        self.to_across.wait_recv()
        self.forward.start()

    def wait_diag(self):
        self.forward.wait_recv()

    def finish(self):
        self.to_sib.wait_send()
        self.to_across.wait_send()
        self.forward.wait_send()


class BlkReduce:
    def __init__(self, place, parts, near, far, send, recv):
        self.place, self.parts, self.near, self.far = place, parts, near, far
        sib, across = place.sib, place.across
        self.sib_far = remote(
            parts.at[place.diag], near.at[1], send.at[0], recv.at[0], place.in_page(sib)
        )
        self.sib_near = remote(parts.at[sib], near.at[0], send.at[1], recv.at[1], place.in_page(sib))
        self.cross = remote(near.at[1], far, send.at[2], recv.at[2], place.in_page(across))

    def send_cross(self):
        self.sib_far.wait_recv()
        both = self.parts[self.place.across].astype(F32) + self.near[1].astype(F32)
        self.near[1] = both.astype(BF16)
        self.cross.start()

    def total(self, own):
        self.sib_near.wait_recv()
        partial = own + self.near[0].astype(F32)
        self.cross.wait_recv()
        return partial + self.far[...].astype(F32)

    def finish(self):
        self.sib_far.wait_send()
        self.sib_near.wait_send()
        self.cross.wait_send()


def gather_kernel(
    spread,
    pack_a,
    pack_b,
    down,
    hidden,
    box,
    vec,
    all_a,
    all_b,
    all_c,
    all_hid,
    all_box,
    all_out,
    vec_sum,
    land_a,
    land_b,
    land_vec,
    all_vec,
    aa_send,
    aa_recv,
    z_send,
    z_recv,
    x_send,
    x_recv,
    bg_send,
    bg_recv,
):
    place = Place(spread)
    peers = place.blk_peers()
    meet(
        [place.in_page(peer) for peer in peers]
        + [place.at(place.z, 1 - place.x)]
        + [place.at(place.z_at(step), place.x) for step in range(1, GRID_Z)]
    )

    def exchange(which, pack, land):
        copies = []
        for slot, peer in enumerate(peers):
            copies.append(
                remote(
                    pack.at[peer],
                    land.at[slot],
                    aa_send.at[which, slot],
                    aa_recv.at[which, slot],
                    place.in_page(peer),
                )
            )
            copies[-1].start()
        return copies

    def spread_out(which, whole):
        copies = []
        own = whole.at[place.hi]
        copies.append(
            remote(own, own, x_send.at[which, 0], x_recv.at[which, 0], place.at(place.z, 1 - place.x))
        )
        for step in range(1, GRID_Z):
            copies.append(
                remote(
                    own,
                    own,
                    z_send.at[which, step - 1],
                    z_recv.at[which, step - 1],
                    place.at(place.z_at(step), place.x),
                )
            )
        for copy in copies:
            copy.start()
        return copies

    def pass_on(which, whole, copies):
        more = []
        for step in range(1, GRID_Z):
            copies[step].wait_recv()
            came = whole.at[place.z_at(GRID_Z - step) * GRID_X + place.x]
            more.append(
                remote(
                    came,
                    came,
                    x_send.at[which, step],
                    x_recv.at[which, step],
                    place.at(place.z, 1 - place.x),
                )
            )
            more[-1].start()
        return more

    def settle(copies, more):
        copies[0].wait_recv()
        for copy in more:
            copy.wait_recv()
        for copy in copies + more:
            copy.wait_send()

    swap_a = exchange(0, pack_a, land_a)
    swap_vec = exchange(1, vec, land_vec)
    all_hid[place.b] = hidden[...]
    all_box[place.b] = box[...]
    gather_hid = BlkGather(place, all_hid, bg_send.at[0], bg_recv.at[0])
    gather_box = BlkGather(place, all_box, bg_send.at[1], bg_recv.at[1])
    gather_box.start()
    gather_hid.start()
    swap_b = exchange(2, pack_b, land_b)
    all_c[place.hi] = down[...]
    def join(pack, land, copies, whole):
        for copy in copies:
            copy.wait_recv()
        held = [pack[place.b].astype(F32)] + [land[slot].astype(F32) for slot in range(3)]
        owners = [place.b] + list(peers)
        parts = []
        for blk in range(BLK):
            part = held[0]
            for other in range(1, BLK):
                part = jnp.where(owners[other] == blk, held[other], part)
            parts.append(part)
        whole[place.hi] = jnp.concatenate(parts, axis=0).astype(BF16)

    join(pack_a, land_a, swap_a, all_a)
    sent_a = spread_out(0, all_a)
    for copy in swap_vec:
        copy.wait_recv()
    whole_vec = vec[place.b].astype(F32)
    for slot in range(3):
        whole_vec = whole_vec + land_vec[slot].astype(F32)
    all_vec[place.hi] = whole_vec.astype(BF16)
    sent_vec = spread_out(3, all_vec)
    sent_c = spread_out(2, all_c)
    join(pack_b, land_b, swap_b, all_b)
    sent_b = spread_out(1, all_b)

    gather_box.wait_across()
    gather_hid.wait_across()
    more_a = pass_on(0, all_a, sent_a)
    more_vec = pass_on(3, all_vec, sent_vec)
    settle(sent_a, more_a)
    own_out = jnp.concatenate([all_a[shard][:, 960:1152] for shard in range(GROUP)], axis=0)
    all_out[place.b] = own_out
    gather_out = BlkGather(place, all_out, bg_send.at[2], bg_recv.at[2])
    gather_out.start()
    more_b = pass_on(1, all_b, sent_b)
    gather_out.wait_across()
    more_c = pass_on(2, all_c, sent_c)
    settle(sent_vec, more_vec)
    total = all_vec[0].astype(F32)
    for shard in range(1, GROUP):
        total = total + all_vec[shard].astype(F32)
    vec_sum[...] = total
    settle(sent_c, more_c)
    settle(sent_b, more_b)
    for gather in (gather_box, gather_hid, gather_out):
        gather.wait_sib()
        gather.wait_diag()
        gather.finish()
    for copy in swap_a + swap_vec + swap_b:
        copy.wait_send()


def vmem_call(kernel, outs, scratch, name, collective=None, smem=()):
    def run(*operands):
        params = dict(vmem_limit_bytes=VMEM_BYTES)
        if collective is not None:
            params.update(collective_id=collective, has_side_effects=True)
        return pl.pallas_call(
            kernel,
            name=name,
            out_shape=[jax.ShapeDtypeStruct(shape, kind) for shape, kind in outs],
            in_specs=[
                pl.BlockSpec(memory_space=pltpu.SMEM if i in smem else pltpu.VMEM)
                for i in range(len(operands))
            ],
            out_specs=[pl.BlockSpec(memory_space=pltpu.VMEM) for _ in outs],
            scratch_shapes=scratch,
            compiler_params=pltpu.CompilerParams(**params),
        )(*operands)

    return run


def attend_kernel(
    lengths, w_a, hid, box, vec, qkv, ctx, probs, feats, relq, relk, qrel, krel
):
    tokens, width = hid.shape
    span = 2 * FREQ
    places = lax.broadcasted_iota(jnp.int32, (256, FREQ), 0).astype(F32)
    ladder = lax.broadcasted_iota(jnp.int32, (256, FREQ), 1).astype(F32)
    angles = places * jnp.exp(ladder * (-math.log(10000.0) / FREQ))
    cosines, sines, blank = jnp.cos(angles), jnp.sin(angles), jnp.zeros((256, FREQ), F32)
    table = jnp.concatenate(
        [
            jnp.concatenate([cosines, blank, sines, blank], axis=1),
            jnp.concatenate([blank, cosines, blank, sines], axis=1),
        ],
        axis=0,
    ).astype(BF16)
    slots = lax.broadcasted_iota(jnp.int32, (256, tokens // BLK), 0)
    for blk in range(BLK):
        hot = jnp.concatenate(
            [
                jnp.where(slots == box[blk][0:1, :], 1.0, 0.0),
                jnp.where(slots == box[blk][1:2, :], 1.0, 0.0),
            ],
            axis=0,
        ).astype(BF16)
        feats[blk * 128 : (blk + 1) * 128, :] = tmm(hot, table).astype(BF16)

    bias = vec[0:1, : 9 * HEAD_DIM]
    for blk in range(BLK):
        rows = slice(blk * 128, (blk + 1) * 128)
        low = (mm(hid[rows, :], w_a[:, : 9 * HEAD_DIM]) + bias).astype(BF16)
        for part in range(9):
            qkv[part, rows, :] = low[:, part * HEAD_DIM : (part + 1) * HEAD_DIM]
    for head in range(3):
        start = 9 * HEAD_DIM + head * HEAD_DIM
        relq[head] = w_a[:, start : start + HEAD_DIM]
        relk[head] = w_a[:, start + 3 * HEAD_DIM : start + 4 * HEAD_DIM]

    usable = lax.broadcasted_iota(jnp.int32, (128, tokens), 1) < lengths[0]

    for head in range(3):

        def turn(blk, carry):
            rows = pl.ds(pl.multiple_of(blk * 128, 128), 128)
            cos_part = feats[rows, :span].astype(F32)
            sin_part = feats[rows, span:].astype(F32)
            u = mm_t(qkv[head, rows, :], relq[head])
            u1, u2 = u[:, :span], u[:, span:]
            qrel[rows, :span] = (u1 * cos_part + u2 * sin_part).astype(BF16)
            qrel[rows, span:] = (u1 * sin_part - u2 * cos_part).astype(BF16)
            v = mm_t(qkv[3 + head, rows, :], relk[head])
            v1, v2 = v[:, :span], v[:, span:]
            krel[rows, :span] = (v1 * cos_part - v2 * sin_part).astype(BF16)
            krel[rows, span:] = (v1 * sin_part + v2 * cos_part).astype(BF16)
            return carry

        lax.fori_loop(0, BLK, turn, 0)

        def rows_of(blk, carry):
            rows = pl.ds(pl.multiple_of(blk * 128, 128), 128)
            scores = mm_t(qrel[rows, :], feats[...])
            scores = scores + mm_t(feats[rows, :], krel[...])
            scores = scores + mm_t(qkv[head, rows, :], qkv[3 + head])
            masked = jnp.where(usable, scores * 0.125, -1e30)
            raised = jnp.exp(masked - jnp.max(masked, axis=-1, keepdims=True))
            prob = raised / jnp.sum(raised, axis=-1, keepdims=True)
            probs[head, rows, :] = prob
            ctx[rows, head * HEAD_DIM : (head + 1) * HEAD_DIM] = mm(
                prob.astype(BF16), qkv[6 + head]
            ).astype(BF16)
            return carry

        lax.fori_loop(0, BLK, rows_of, 0)


def centred(values):
    mean = jnp.mean(values, axis=-1, keepdims=True)
    centre = values - mean
    scale = lax.rsqrt(jnp.mean(centre * centre, axis=-1, keepdims=True) + 1e-12)
    return centre * scale, scale


def norm_back(grad_hat, hat, scale):
    first = jnp.mean(grad_hat, axis=-1, keepdims=True)
    second = jnp.mean(grad_hat * hat, axis=-1, keepdims=True)
    return scale * (grad_hat - first - hat * second)


def column_sum(values):
    return jnp.sum(values, axis=0, keepdims=True)


def middle_kernel(
    spread,
    ctx,
    hid,
    cot,
    vec,
    w_out,
    w_up,
    w_down,
    out,
    g_one_out,
    g_ctx,
    grad_out,
    grad_up,
    grad_down,
    grad_vec,
    ctx_own,
    ctx_all,
    normed_all,
    act,
    slope,
    parts_one,
    near_one,
    far_one,
    branch_all,
    parts_two,
    near_two,
    far_two,
    g_attn_own,
    g_attn_cols,
    g_ctx_own,
    ca_send,
    ca_recv,
    bg_send,
    bg_recv,
    br_send,
    br_recv,
):
    place = Place(spread)
    b = place.b
    peers = place.blk_peers()
    order = (b, place.sib, place.across, place.diag)
    width = hid.shape[1]
    third = 3 * HEAD_DIM
    meet([place.in_page(peer) for peer in peers])

    def exchange(which, source_of, target):
        copies = []
        for slot, peer in enumerate(peers):
            copies.append(
                remote(
                    source_of(peer),
                    target.at[b],
                    ca_send.at[which, slot],
                    ca_recv.at[which, slot],
                    place.in_page(peer),
                )
            )
            copies[-1].start()
        return copies

    def recv_all(copies):
        for copy in copies:
            copy.wait_recv()

    swap_ctx = exchange(0, lambda peer: ctx.at[peer], ctx_own)
    spread_ctx = exchange(1, lambda peer: ctx, ctx_all)
    ctx_own[b] = ctx[b]
    ctx_all[b] = ctx[...]
    recv_all(swap_ctx)
    own = jnp.concatenate([ctx_own[blk] for blk in range(BLK)], axis=1)
    attn = jnp.concatenate([mm(own, w_out[blk]) for blk in range(BLK)], axis=1) + vec[2:3, :]
    hat_one, scale_one = centred(hid[...].astype(F32) + attn)
    gain_one = vec[3:4, :]
    normed = hat_one * gain_one + vec[4:5, :]
    normed_all[b] = normed.astype(BF16)
    gather = BlkGather(place, normed_all, bg_send.at[0], bg_recv.at[0])
    gather.start()
    reduce = BlkReduce(place, parts_one, near_one, far_one, br_send.at[0], br_recv.at[0])
    own_branch = None
    for step, blk in enumerate(order):
        if step == 1:
            gather.wait_sib()
        elif step == 2:
            gather.wait_across()
        elif step == 3:
            gather.wait_diag()
        middle = mm(normed_all[blk], w_up[...]) + vec[1:2, :]
        half = 0.5 * (1.0 + lax.erf(middle * math.sqrt(0.5)))
        act[blk] = (middle * half).astype(BF16)
        slope[blk] = half + middle * jnp.exp(-0.5 * middle * middle) * (1.0 / math.sqrt(2.0 * math.pi))
        part = mm(act[blk], w_down[...])
        if step == 0:
            own_branch = part
        else:
            parts_one[blk] = part.astype(BF16)
        if step == 1:
            reduce.sib_near.start()
        elif step == 3:
            reduce.sib_far.start()
    reduce.send_cross()
    gather.finish()
    branch = reduce.total(own_branch) + vec[5:6, :]
    reduce.finish()
    hat_two, scale_two = centred(normed + branch)
    gain_two = vec[6:7, :]
    out[...] = (hat_two * gain_two + vec[7:8, :]).astype(BF16)
    cot_wide = cot[...].astype(F32)
    grad_vec[6:7, :] = column_sum(cot_wide * hat_two)
    grad_vec[7:8, :] = column_sum(cot_wide)
    g_two = norm_back(cot_wide * gain_two, hat_two, scale_two)
    g_branch = g_two.astype(BF16)
    branch_all[b] = g_branch
    gather = BlkGather(place, branch_all, bg_send.at[1], bg_recv.at[1])
    gather.start()
    grad_vec[5:6, :] = column_sum(g_branch.astype(F32))
    reduce = BlkReduce(place, parts_two, near_two, far_two, br_send.at[1], br_recv.at[1])
    up_bias = jnp.zeros((1, width), F32)
    for step, blk in enumerate(order):
        if step == 1:
            gather.wait_sib()
        elif step == 2:
            gather.wait_across()
        elif step == 3:
            gather.wait_diag()
        g_middle = (mm_t(branch_all[blk], w_down[...]) * slope[blk]).astype(BF16)
        up_bias = up_bias + column_sum(g_middle.astype(F32))
        slope[blk] = g_middle.astype(F32)
        part = mm_t(g_middle, w_up[...])
        if step == 0:
            own_branch = part
        else:
            parts_two[blk] = part.astype(BF16)
        if step == 1:
            reduce.sib_near.start()
        elif step == 3:
            reduce.sib_far.start()
    grad_vec[1:2, :] = up_bias
    reduce.send_cross()
    gather.finish()

    act_rows = act.reshape(4 * act.shape[1], act.shape[2])
    branch_rows = branch_all.reshape(4 * act.shape[1], width)
    normed_rows = normed_all.reshape(4 * act.shape[1], width)
    slope_rows = slope.reshape(4 * act.shape[1], act.shape[2])

    def down_rows(at, carry):
        cols = pl.ds(pl.multiple_of(at * 128, 128), 128)
        grad_down[cols, :] = tmm(act_rows[:, cols], branch_rows[...]).astype(BF16)
        return carry

    lax.fori_loop(0, act.shape[2] // 128, down_rows, 0)

    g_normed = g_two + reduce.total(own_branch)
    reduce.finish()
    grad_vec[3:4, :] = column_sum(g_normed * hat_one)
    grad_vec[4:5, :] = column_sum(g_normed)
    g_one = norm_back(g_normed * gain_one, hat_one, scale_one)
    g_one_out[...] = g_one
    g_attn = g_one.astype(BF16)
    grad_vec[2:3, :] = column_sum(g_attn.astype(F32))
    for blk in range(BLK):
        cols = g_attn[:, blk * third : (blk + 1) * third]
        g_attn_own[blk] = cols
    swap_attn = exchange(2, lambda peer: g_attn_own.at[peer], g_attn_cols)
    g_attn_cols[b] = g_attn_own[b]
    g_ctx_wide = jnp.zeros(g_one.shape, F32)
    for blk in range(BLK):
        g_ctx_wide = g_ctx_wide + mm_t(g_attn_own[blk], w_out[blk])
    for blk in range(BLK):
        g_ctx_own[blk] = g_ctx_wide[:, blk * third : (blk + 1) * third].astype(BF16)
    swap_back = exchange(3, lambda peer: g_ctx_own.at[peer], g_ctx)
    g_ctx[b] = g_ctx_own[b]

    g_middle_low = slope_rows[...].astype(BF16)

    act[...] = g_middle_low.reshape(act.shape)

    def up_rows(at, carry):
        cols = pl.ds(pl.multiple_of(at * 128, 128), 128)
        grad_up[cols, :] = tmm(normed_rows[:, cols], act_rows[...]).astype(BF16)
        return carry

    lax.fori_loop(0, width // 128, up_rows, 0)
    recv_all(swap_attn)
    recv_all(spread_ctx)
    columns = g_attn_cols.reshape(4 * act.shape[1], third)[...]
    for blk in range(BLK):
        heads = ctx_all[blk].reshape(4 * act.shape[1], third)
        grad_out[blk * third : (blk + 1) * third, :] = tmm(heads, columns).astype(BF16)
    recv_all(swap_back)
    for copy in swap_ctx + spread_ctx + swap_attn + swap_back:
        copy.wait_send()
    grad_vec[0:1, :] = jnp.zeros((1, width), F32)


def attend_back_kernel(
    w_a,
    hid,
    qkv,
    ctx,
    g_ctx,
    probs,
    feats,
    relq,
    relk,
    grad_a,
    part_hid,
    grad_bias,
    g_scores,
    p_low,
    g_turned_q,
    g_turned_k,
    g_heads,
    go_heads,
    g_qkv,
):
    tokens, width = hid.shape
    span = 2 * FREQ
    nine = 9 * HEAD_DIM
    for head in range(3):
        lanes = slice(head * HEAD_DIM, (head + 1) * HEAD_DIM)
        go_heads[...] = g_ctx[:, lanes]

        def query_rows(blk, carry):
            rows = pl.ds(pl.multiple_of(blk * 128, 128), 128)
            go = go_heads[rows, :]
            delta = jnp.sum(
                go.astype(F32) * ctx[rows, lanes].astype(F32), axis=-1, keepdims=True
            )
            prob = probs[head, rows, :]
            p_low[rows, :] = prob.astype(BF16)
            ds = (prob * (mm_t(go, qkv[6 + head]) - delta)).astype(BF16)
            g_scores[rows, :] = ds
            turned = 0.125 * mm(ds, feats[...])
            a1, a2 = turned[:, :span], turned[:, span:]
            cos_part = feats[rows, :span].astype(F32)
            sin_part = feats[rows, span:].astype(F32)
            g_turned_q[rows, :span] = (a1 * cos_part + a2 * sin_part).astype(BF16)
            g_turned_q[rows, span:] = (a1 * sin_part - a2 * cos_part).astype(BF16)
            gq = 0.125 * mm(ds, qkv[3 + head]) + mm(g_turned_q[rows, :], relq[head])
            g_heads[head, rows, :] = gq.astype(BF16)
            return carry

        lax.fori_loop(0, BLK, query_rows, 0)

        def key_rows(blk, carry):
            rows = pl.ds(pl.multiple_of(blk * 128, 128), 128)
            ds = g_scores[:, rows]
            turned = 0.125 * tmm(ds, feats[...])
            b1, b2 = turned[:, :span], turned[:, span:]
            cos_part = feats[rows, :span].astype(F32)
            sin_part = feats[rows, span:].astype(F32)
            g_turned_k[rows, :span] = (b1 * cos_part + b2 * sin_part).astype(BF16)
            g_turned_k[rows, span:] = (b2 * cos_part - b1 * sin_part).astype(BF16)
            gk = 0.125 * tmm(ds, qkv[head]) + mm(g_turned_k[rows, :], relk[head])
            g_heads[3 + head, rows, :] = gk.astype(BF16)
            g_heads[6 + head, rows, :] = tmm(p_low[:, rows], go_heads[...]).astype(BF16)
            return carry

        lax.fori_loop(0, BLK, key_rows, 0)
        start = nine + head * HEAD_DIM
        grad_a[:, start : start + HEAD_DIM] = tmm(g_turned_q[...], qkv[head]).astype(BF16)
        start = start + 3 * HEAD_DIM
        grad_a[:, start : start + HEAD_DIM] = tmm(g_turned_k[...], qkv[3 + head]).astype(BF16)
    g_qkv[...] = jnp.concatenate([g_heads[part] for part in range(9)], axis=1)
    grad_bias[0:1, :nine] = column_sum(g_qkv[...].astype(F32))
    grad_bias[0:1, nine:] = jnp.zeros((1, width - nine), F32)
    for blk in range(BLK):
        part_hid[blk] = mm_t(g_qkv[blk * 128 : (blk + 1) * 128, :], w_a[:, :nine]).astype(BF16)

    def weight_rows(at, carry):
        cols = pl.ds(pl.multiple_of(at * 128, 128), 128)
        grad_a[cols, :nine] = tmm(hid[:, cols], g_qkv[...]).astype(BF16)
        return carry

    lax.fori_loop(0, width // 128, weight_rows, 0)


def reduce_kernel(
    spread,
    grad_a,
    grad_b,
    grad_c,
    part_hid,
    g_one,
    sum_a,
    sum_b,
    sum_c,
    grad_hid,
    pair_a,
    pair_b,
    pair_c,
    line_a,
    line_b,
    line_c,
    cut_a,
    cut_b,
    near,
    far,
    x_send,
    x_recv,
    z_send,
    z_recv,
    aa_send,
    aa_recv,
    br_send,
    br_recv,
):
    place = Place(spread)
    peers = place.blk_peers()
    meet(
        [place.in_page(peer) for peer in peers]
        + [place.at(place.z, 1 - place.x)]
        + [place.at(place.z_at(step), place.x) for step in range(1, GRID_Z)]
    )
    chunks = ((grad_c, pair_c, line_c), (grad_b, pair_b, line_b), (grad_a, pair_a, line_a))

    def shard(step, x):
        return place.z_at(step) * GRID_X + x

    def to_partner(which):
        grad, pair, _ = chunks[which]
        copies = []
        for step in range(GRID_Z):
            copies.append(
                remote(
                    grad.at[shard(step, 1 - place.x)],
                    pair.at[step],
                    x_send.at[which, step],
                    x_recv.at[which, step],
                    place.at(place.z, 1 - place.x),
                )
            )
        for step in (1, 2, 3, 0):
            copies[step].start()
        return copies

    def to_line(which, copies):
        grad, pair, line = chunks[which]
        more = []
        for step in range(1, GRID_Z):
            copies[step].wait_recv()
            both = grad[shard(step, place.x)].astype(F32) + pair[step].astype(F32)
            pair[step] = both.astype(BF16)
            more.append(
                remote(
                    pair.at[step],
                    line.at[step - 1],
                    z_send.at[which, step - 1],
                    z_recv.at[which, step - 1],
                    place.at(place.z_at(step), place.x),
                )
            )
            more[-1].start()
        return more

    def total(which, copies, more):
        grad, pair, line = chunks[which]
        copies[0].wait_recv()
        value = grad[shard(0, place.x)].astype(F32) + pair[0].astype(F32)
        for step in range(1, GRID_Z):
            more[step - 1].wait_recv()
            value = value + line[step - 1].astype(F32)
        return value

    def cut(which, value, pieces, target):
        rows = value.shape[0] // BLK
        for blk in range(BLK):
            pieces[blk] = value[blk * rows : (blk + 1) * rows, :].astype(BF16)
        target[place.b] = pieces[place.b]
        copies = []
        for slot, peer in enumerate(peers):
            copies.append(
                remote(
                    pieces.at[peer],
                    target.at[place.b],
                    aa_send.at[which, slot],
                    aa_recv.at[which, slot],
                    place.in_page(peer),
                )
            )
            copies[-1].start()
        return copies

    first = [to_partner(which) for which in range(3)]
    reduce = BlkReduce(place, part_hid, near, far, br_send, br_recv)
    reduce.sib_far.start()
    reduce.sib_near.start()
    second = [to_line(0, first[0])]
    reduce.send_cross()
    second.append(to_line(1, first[1]))
    own = part_hid[place.b].astype(F32) + g_one[...]
    grad_hid[...] = reduce.total(own).astype(BF16)
    reduce.finish()
    second.append(to_line(2, first[2]))
    sum_c[...] = total(0, first[0], second[0])
    last = cut(0, total(1, first[1], second[1]), cut_b, sum_b)
    last = last + cut(1, total(2, first[2], second[2]), cut_a, sum_a)
    for copy in last:
        copy.wait_recv()
        copy.wait_send()
    for copies in first + second:
        for copy in copies:
            copy.wait_send()


def on_device(
    hidden,
    boxes,
    lengths,
    w_qkv,
    b_qkv,
    w_relq,
    w_relk,
    w_out,
    b_out,
    ln1_gain,
    ln1_bias,
    w_up,
    b_up,
    w_down,
    b_down,
    ln2_gain,
    ln2_bias,
    cotangent,
):
    page_count = lax.axis_size("pages")
    spread = page_count // GROUP
    b = lax.axis_index("blk")
    hi = lax.axis_index("pages") // spread
    _, tok, width = hidden.shape
    third = 3 * HEAD_DIM
    groups = [[h * spread + low for low in range(spread)] for h in range(GROUP)]

    def grow(rows):
        if spread == 1:
            return rows
        rows = lax.all_gather(rows, "blk", axis=0, tiled=True)
        rows = lax.all_gather(rows, "pages", axis=0, tiled=True, axis_index_groups=groups)
        count = rows.shape[0] // BLK
        return lax.dynamic_slice_in_dim(rows, b * count, count, 0)

    def shrink(rows):
        if spread == 1:
            return rows
        rows = lax.all_gather(rows, "blk", axis=0, tiled=True)
        rows = lax.psum_scatter(
            rows, "pages", scatter_dimension=0, tiled=True, axis_index_groups=groups
        )
        count = rows.shape[0] // BLK
        return lax.dynamic_slice_in_dim(rows, b * count, count, 0)

    w_qkv, w_relq, w_relk, w_out, w_up, w_down = map(
        grow, (w_qkv, w_relq, w_relk, w_out, w_up, w_down)
    )
    b_qkv, b_up, b_out, ln1_gain, ln1_bias, b_down, ln2_gain, ln2_bias = map(
        grow, (b_qkv, b_up, b_out, ln1_gain, ln1_bias, b_down, ln2_gain, ln2_bias)
    )
    rows = w_qkv.shape[0]
    shard = BLK * rows
    ff_part = w_up.shape[1] // (GROUP * BLK)

    def by_head(weight):
        return weight.reshape(rows, BLK, third).transpose(1, 0, 2)

    pack_a = jnp.concatenate(
        [
            w_qkv.reshape(rows, 3, BLK, third).transpose(2, 0, 1, 3).reshape(BLK, rows, 3 * third),
            by_head(w_relq),
            by_head(w_relk),
            by_head(w_out),
        ],
        axis=-1,
    )
    pack_b = (
        w_up.reshape(rows, GROUP, BLK, ff_part)
        .transpose(2, 0, 1, 3)
        .reshape(BLK, rows, GROUP * ff_part)
    )
    here = (lax.iota(jnp.int32, GROUP * BLK) == hi * BLK + b).astype(BF16)
    spot = here[:, None]
    own_bias = (spot * b_qkv[None, :]).reshape(3, BLK, third).transpose(1, 0, 2)
    own_bias = own_bias.reshape(BLK, 3 * third)
    own_bias = jnp.pad(own_bias, ((0, 0), (0, width - 3 * third)))
    up_spot = (spot * b_up[None, :]).reshape(GROUP, BLK, ff_part).transpose(1, 0, 2)
    up_spot = up_spot.reshape(BLK, GROUP * ff_part)
    plain = jnp.stack([b_out, ln1_gain, ln1_bias, b_down, ln2_gain, ln2_bias])
    plain = (spot[None] * plain[:, None, :]).reshape(6, width)
    vec = jnp.concatenate(
        [
            own_bias[:, None, :],
            up_spot[:, None, :],
            jnp.broadcast_to(plain[None], (BLK, 6, width)),
            jnp.zeros((BLK, 8, width), BF16),
        ],
        axis=1,
    )
    box = jnp.pad(boxes[0].T, ((0, 6), (0, 0)))

    hid = hidden[0]
    sem = pltpu.SemaphoreType.DMA
    cols_a, cols_b = pack_a.shape[-1], pack_b.shape[-1]
    all_a, all_b, all_c, all_hid, all_box, all_out, vec_sum = vmem_call(
        functools.partial(gather_kernel, spread),
        [
            ((GROUP, shard, cols_a), BF16),
            ((GROUP, shard, cols_b), BF16),
            ((GROUP, shard, width), BF16),
            ((BLK, tok, width), BF16),
            ((BLK, 8, tok), jnp.int32),
            ((BLK, GROUP * shard, third), BF16),
            ((16, width), F32),
        ],
        [
            pltpu.VMEM((3, rows, cols_a), BF16),
            pltpu.VMEM((3, rows, cols_b), BF16),
            pltpu.VMEM((3, 16, width), BF16),
            pltpu.VMEM((GROUP, 16, width), BF16),
            sem((3, 3)),
            sem((3, 3)),
            sem((4, 3)),
            sem((4, 3)),
            sem((4, 4)),
            sem((4, 4)),
            sem((3, 3)),
            sem((3, 3)),
        ],
        "gather",
        collective=1,
    )(pack_a, pack_b, w_down, hid, box, vec)
    w_a = all_a.reshape(GROUP * shard, cols_a)
    w_b = all_b.reshape(GROUP * shard, cols_b)
    w_c = all_c.reshape(GROUP * shard, width)
    hid_page = all_hid.reshape(BLK * tok, width)
    tokens = BLK * tok

    qkv, ctx, probs, feats, relq, relk = vmem_call(
        attend_kernel,
        [
            ((9, tokens, HEAD_DIM), BF16),
            ((tokens, third), BF16),
            ((3, tokens, tokens), F32),
            ((tokens, width), BF16),
            ((3, width, HEAD_DIM), BF16),
            ((3, width, HEAD_DIM), BF16),
        ],
        [pltpu.VMEM((tokens, width), BF16), pltpu.VMEM((tokens, width), BF16)],
        "attend",
        smem=(0,),
    )(lengths, w_a, hid_page, all_box, vec_sum)

    block = pltpu.VMEM((BLK, tok, width), BF16)
    thirds = pltpu.VMEM((BLK, tok, third), BF16)
    two, one = pltpu.VMEM((2, tok, width), BF16), pltpu.VMEM((tok, width), BF16)
    out, g_one, g_ctx, grad_out, grad_b, grad_c, grad_vec = vmem_call(
        functools.partial(middle_kernel, spread),
        [
            ((tok, width), BF16),
            ((tok, width), F32),
            ((BLK, tok, third), BF16),
            ((GROUP * shard, third), BF16),
            ((GROUP * shard, cols_b), BF16),
            ((GROUP * shard, width), BF16),
            ((8, width), F32),
        ],
        [
            thirds,
            pltpu.VMEM((BLK, BLK, tok, third), BF16),
            block,
            pltpu.VMEM((BLK, tok, cols_b), BF16),
            pltpu.VMEM((BLK, tok, cols_b), F32),
            block,
            two,
            one,
            block,
            block,
            two,
            one,
            thirds,
            thirds,
            thirds,
            sem((4, 3)),
            sem((4, 3)),
            sem((2, 3)),
            sem((2, 3)),
            sem((2, 3)),
            sem((2, 3)),
        ],
        "middle",
        collective=2,
    )(ctx.reshape(BLK, tok, third), hid, cotangent[0], vec_sum, all_out, w_b, w_c)

    grad_a, part_hid, grad_bias = vmem_call(
        attend_back_kernel,
        [
            ((width, 5 * third), BF16),
            ((BLK, tok, width), BF16),
            ((1, width), F32),
        ],
        [
            pltpu.VMEM((tokens, tokens), BF16),
            pltpu.VMEM((tokens, tokens), BF16),
            pltpu.VMEM((tokens, width), BF16),
            pltpu.VMEM((tokens, width), BF16),
            pltpu.VMEM((9, tokens, HEAD_DIM), BF16),
            pltpu.VMEM((tokens, HEAD_DIM), BF16),
            pltpu.VMEM((tokens, 3 * third), BF16),
        ],
        "attend_back",
    )(w_a, hid_page, qkv, ctx, g_ctx.reshape(tokens, third), probs, feats, relq, relk)
    grad_a = jnp.concatenate([grad_a, grad_out], axis=1).reshape(GROUP, shard, cols_a)

    sum_a, sum_b, sum_c, grad_hid = vmem_call(
        functools.partial(reduce_kernel, spread),
        [
            ((BLK, rows, cols_a), BF16),
            ((BLK, rows, cols_b), BF16),
            ((shard, width), F32),
            ((tok, width), BF16),
        ],
        [
            pltpu.VMEM((GRID_Z, shard, cols_a), BF16),
            pltpu.VMEM((GRID_Z, shard, cols_b), BF16),
            pltpu.VMEM((GRID_Z, shard, width), BF16),
            pltpu.VMEM((GRID_Z - 1, shard, cols_a), BF16),
            pltpu.VMEM((GRID_Z - 1, shard, cols_b), BF16),
            pltpu.VMEM((GRID_Z - 1, shard, width), BF16),
            pltpu.VMEM((BLK, rows, cols_a), BF16),
            pltpu.VMEM((BLK, rows, cols_b), BF16),
            two,
            one,
            sem((3, 4)),
            sem((3, 4)),
            sem((3, 3)),
            sem((3, 3)),
            sem((2, 3)),
            sem((2, 3)),
            sem((3,)),
            sem((3,)),
        ],
        "reduce",
        collective=3,
    )(
        grad_a,
        grad_b.reshape(GROUP, shard, cols_b),
        grad_c.reshape(GROUP, shard, width),
        part_hid,
        g_one,
    )

    def heads_back(cols):
        return cols.transpose(1, 0, 2).reshape(rows, BLK * third).astype(F32)

    grad_qkv = sum_a[:, :, : 3 * third].reshape(BLK, rows, 3, third).transpose(1, 2, 0, 3)
    grad_qkv = grad_qkv.reshape(rows, 3 * BLK * third).astype(F32)
    grad_relq = heads_back(sum_a[:, :, 3 * third : 4 * third])
    grad_relk = heads_back(sum_a[:, :, 4 * third : 5 * third])
    grad_w_out = heads_back(sum_a[:, :, 5 * third :])
    grad_up = sum_b.reshape(BLK, rows, GROUP, ff_part).transpose(1, 2, 0, 3)
    grad_up = grad_up.reshape(rows, GROUP * BLK * ff_part).astype(F32)

    mine = (lax.iota(jnp.int32, BLK) == b).astype(F32)
    count = page_count * BLK
    bias_parts = grad_bias[0, : 3 * third].reshape(3, 1, third) * mine[None, :, None]
    up_parts = grad_vec[1].reshape(GROUP, 1, ff_part) * mine[None, :, None]
    owned = jnp.concatenate(
        [bias_parts.reshape(count, -1), up_parts.reshape(count, -1)]
        + [grad_vec[row].reshape(count, -1) for row in range(2, 8)],
        axis=1,
    )
    vectors = lax.psum_scatter(owned, ("pages", "blk"), scatter_dimension=0, tiled=True)[0]
    sizes = [3 * BLK * third // count, GROUP * BLK * ff_part // count] + [width // count] * 6
    cuts = [sum(sizes[:at]) for at in range(len(sizes) + 1)]
    g_bias, g_up, g_out, g_gain1, g_shift1, g_down, g_gain2, g_shift2 = [
        vectors[cuts[at] : cuts[at + 1]] for at in range(8)
    ]
    return (
        out[None],
        grad_hid[None],
        shrink(grad_qkv),
        g_bias,
        shrink(grad_relq),
        shrink(grad_relk),
        shrink(grad_w_out),
        g_out,
        g_gain1,
        g_shift1,
        shrink(grad_up),
        g_up,
        shrink(sum_c),
        g_down,
        g_gain2,
        g_shift2,
    )


def solution(mesh):
    rows = P(("pages", "blk"), None)
    vector = P(("pages", "blk"))
    tokens = P("pages", "blk", None)
    return jax.shard_map(
        on_device,
        mesh=mesh,
        in_specs=(
            tokens,
            tokens,
            P("pages"),
            rows,
            vector,
            rows,
            rows,
            rows,
            vector,
            vector,
            vector,
            rows,
            vector,
            rows,
            vector,
            vector,
            vector,
            tokens,
        ),
        out_specs=(
            tokens,
            tokens,
            rows,
            vector,
            rows,
            rows,
            rows,
            vector,
            vector,
            vector,
            rows,
            vector,
            rows,
            vector,
            vector,
            vector,
        ),
        check_vma=False,
    )
```

time: 1230 us -> 311 us (0.25); the launches traced: 1220 us -> 310 us
  waiting for transfers between devices: 750 us -> 0 us
  Pallas kernels: 0 us -> 243 us
  matrix products: 142 us -> 0 us
  blocking collectives: 164 us -> 42 us
  other arithmetic: 59.7 us -> 5.59 us
  local copies, waits for them, and re-layouts: 70.4 us -> 18.5 us
  between operations: 25.2 us -> 1.68 us
    reduce_scatter x10 -> x0, waiting for transfers between devices: 419 us -> none  [the longest x1 164 us: on_device(): lax.psum_scatter(grad_set[8], 'pages', scatter_dimension=0, tiled=True)]
    pallas_call x0 -> x5, Pallas kernels: none -> 243 us  [run(): pl.pallas_call(kernel, name=name, out_shape=[jax.ShapeDtypeStruct(shape,...]
    unnamed x20 -> x0, waiting for transfers between devices: 152 us -> none
    all_gather x6 -> x0, waiting for transfers between devices: 148 us -> none  [the longest x1 71.1 us: on_device(): lax.all_gather(sectioned[10], 'pages', axis=0, tiled=True)]
    dot_general x51 -> x0, matrix products: 142 us -> none  [the longest x4 34.1 us: on_device(): jnp.einsum('phqk,pkhc->pqhc', grad_scores, key_hat, preferred_element_typ...]
    all_gather x7 -> x0, blocking collectives: 74.2 us -> none  [the longest x1 26.1 us: on_device(): lax.all_gather(sectioned[9], 'pages', axis=0, tiled=True)]
    unnamed x4 -> x1, blocking collectives: 89.9 us -> 42 us
    unnamed x409 -> x23, local copies, waits for them, and re-layouts: 41.3 us -> 2.11 us
  transfers between devices with their start and end apart: 28 -> 0, of which waited for: 20 -> 0; matrix products, arithmetic and copies ran while one was open for 19% -> 0% of each run, Pallas kernels for 0% -> 0%
where the time goes in v1:
time: 311 us; the launch traced here: 310 us
  Pallas kernels  243 us (78%)
  blocking collectives  42 us (14%)
  local copies, waits for them, and re-layouts  18.5 us (6%)
  other arithmetic  5.59 us (2%)
    pallas_call x5, Pallas kernels, run(): pl.pallas_call(kernel, name=name, out_shape=[jax.ShapeDtypeStruct(shape,...  243 us
    unnamed x1, blocking collectives  42 us

profile of v1, /device:TPU:0, one launch (start us, length us, event | category | flops | bytes accessed | tf_op | source)
XLA Modules:
  0.0 310.4 jit_solution(4287284565895581482)
XLA Ops:
  0.7 0.1 mul.121
  0.8 0.1 mul.122
  0.9 0.8 stack.27
  1.6 0.0 copy-start.9
  1.6 0.1 mul.125
  1.8 0.7 broadcast_multiply_fusion.4
  2.5 0.1 mul.114
  2.6 0.1 reshape.205
  2.8 0.1 mul.115
  2.8 0.1 mul.139
  2.9 0.7 mul.117
  3.6 0.1 mul.118
  3.7 0.1 pad.15.clone
  3.8 0.7 maximum_maximum_fusion.vec
  4.5 0.9 reshape.201
  5.4 0.9 reshape.202
  6.3 1.1 reshape.198
  7.4 0.1 copy.82
  7.5 0.2 reshape.199
  7.6 0.1 reshape.200
  7.8 0.8 concatenate.12.pack_a
  8.6 0.2 reshape.203
  8.8 0.8 reshape.204.pack_b
  9.6 0.0 copy-done.9
  9.6 0.6 pad.8.box
  10.2 77.7 %gather.1 = (bf16[8,96,1152]{2,1,0:T(8,128)(2,1)}, bf16[8,96,768]{2,1,0:T(8,128)(2,1)}, bf16[8,96,768]{2,1,0:T(8,128)(2,1)}, bf16[4,128,768]{2,1,0:T(8,128)(2,1)...) custom-call(bf16[4,24,1152]{2,1,0:T(8,128)(2,1)} %concatenate.12.pack_a, ...), custom_call_target="tpu_custom_call" | custom-call | tf_op jit(solution)/shard_map/gather/pallas_call | solution.py:296
  88.6 21.7 %attend.1 = (bf16[9,512,64]{2,1,0:T(8,128)(2,1)}, bf16[512,192]{1,0:T(8,128)(2,1)}, f32[3,512,512]{2,1,0:T(8,128)}, bf16[512,768]{1,0:T(8,128)(2,1)}, bf16[3,768...) custom-call(s32[1]{0:T(128)S(6)} %copy.87.lengths, bf16[768,1152]{1,0:T(8,128)(2,1)} %bitcast.65, ...), custom_call_target="tpu_custom_call" | custom-call | tf_op jit(solution)/shard_map/attend/pallas_call | solution.py:296
  110.3 56.8 %middle.1 = (bf16[128,768]{1,0:T(8,128)(2,1)}, f32[128,768]{1,0:T(8,128)}, bf16[4,128,192]{2,1,0:T(8,128)(2,1)}, bf16[768,192]{1,0:T(8,128)(2,1)}, bf16[768,768]...) custom-call(bf16[4,128,192]{2,1,0:T(8,128)(2,1)} %bitcast.76, bf16[128,768]{1,0:T(8,128)(2,1)} %bitcast.78, ...), custom_call_target="tpu_custom_call" | custom-call | tf_op jit(solution)/shard_map/middle/pallas_call | solution.py:296
  167.1 24.6 %attend_back.1 = (bf16[768,960]{1,0:T(8,128)(2,1)}, bf16[4,128,768]{2,1,0:T(8,128)(2,1)}, f32[1,768]{1,0:T(1,128)}) custom-call(bf16[768,1152]{1,0:T(8,128)(2,1)} %bitcast.66, bf16[512,768]{1,0:T(8,128)(2,1)} %bitcast.69, bf16[9,512,64]{2,1,0:T(8,128)(2,1)} %get-tuple-element.52.qkv, bf16[512,192]{1,0:T(8,128)(2,1)} %get-tuple-element.47.ctx, ...), custom_call_target="tpu_custom_call" | custom-call | tf_op jit(solution)/shard_map/attend_back/pallas_call | solution.py:296
  191.7 0.7 slice_reduce_fusion.7
  192.4 0.1 mul.127
  192.5 0.1 broadcast_multiply_fusion.1
  192.6 0.1 mul.131
  192.7 0.1 slice_reduce_fusion
  192.8 0.1 mul.132
  192.8 0.1 mul.136
  192.9 0.1 broadcast_multiply_fusion
  193.0 0.1 reshape_squeeze.20
  193.1 0.1 reshape_squeeze.21
  193.2 0.1 reshape_squeeze.22
  193.3 0.1 reshape_squeeze.23
  193.3 0.1 reshape_squeeze.24
  193.4 0.1 reshape_squeeze.25
  193.5 0.1 concatenate.15
  193.6 42.0 %all-reduce.2 = f32[32,312]{1,0:T(8,128)S(1)} all-reduce(f32[32,312]{1,0:T(8,128)S(1)} %concatenate.15), channel_id=2, replica_groups=mesh['pages'=8,'blk'=4] {'pages','blk'}, use_global_device_ids=true, to_apply=%region_0.1.clone | all-reduce | flops 9984 | bytes 79872
  235.7 0.6 dynamic-slice_bitcast_fusion
  236.3 0.6 dynamic-slice_bitcast_fusion.3
  236.9 0.5 dynamic-slice_bitcast_fusion.7
  237.4 2.9 pad_maximum_fusion
  240.3 61.7 %reduce.17 = (bf16[4,24,1152]{2,1,0:T(8,128)(2,1)}, bf16[4,24,768]{2,1,0:T(8,128)(2,1)}, f32[96,768]{1,0:T(8,128)}, bf16[128,768]{1,0:T(8,128)(2,1)}) custom-call(bf16[8,96,1152]{2,1,0:T(8,128)(2,1)} %bitcast.67, bf16[8,96,768]{2,1,0:T(8,128)(2,1)} %bitcast.74, bf16[8,96,768]{2,1,0:T(8,128)(2,1)} %bitcast.75, ...), custom_call_target="tpu_custom_call" | custom-call | tf_op jit(solution)/shard_map/reduce/pallas_call | solution.py:296
  302.1 1.0 slice_convert_fusion
  303.0 0.2 reshape.220
  303.2 0.2 copy.71
  303.4 0.9 reshape.215
  304.3 0.2 reshape.221
  304.5 0.3 copy.75
  304.8 1.1 reshape.219
  305.8 0.1 convert_bitcast_fusion
  306.0 0.7 reshape.216
  306.8 0.7 reshape.217
  307.6 0.7 reshape.218
  308.3 0.7 copy.88
  309.0 0.7 copy.89
  309.7 0.7 copy.90
  (37 shorter events, 0.3 us)
Async XLA Ops:
  0.6 7.0 %copy-start.7 = (bf16[24,768]{1,0:T(8,128)(2,1)S(1)}, bf16[24,768]{1,0:T(8,128)(2,1)}, u32[]{:S(2)}) copy-start(bf16[24,768]{1,0:T(8,128)(2,1)} %param.23) | copy-start | bytes 110596
  0.7 7.9 %copy-start.5 = (bf16[24,3072]{1,0:T(8,128)(2,1)S(1)}, bf16[24,3072]{1,0:T(8,128)(2,1)}, u32[]{:S(2)}) copy-start(bf16[24,3072]{1,0:T(8,128)(2,1)} %param.29) | copy-start | bytes 442372
  1.6 8.0 %copy-start.9 = (s32[1,128,2]{1,2,0:T(2,128)S(1)}, s32[1,128,2]{1,2,0:T(2,128)}, u32[]{:S(2)}) copy-start(s32[1,128,2]{1,2,0:T(2,128)} %param.19) | copy-start | bytes 3076
  167.1 25.6 %copy-start.8 = (f32[8,768]{1,0:T(8,128)S(1)}, f32[8,768]{1,0:T(8,128)}, u32[]{:S(2)}) copy-start(f32[8,768]{1,0:T(8,128)} %get-tuple-element.67) | copy-start | bytes 73732
  167.1 70.3 %copy-start = (bf16[768,192]{1,0:T(8,128)(2,1)S(1)}, bf16[768,192]{1,0:T(8,128)(2,1)}, u32[]{:S(2)}) copy-start(bf16[768,192]{1,0:T(8,128)(2,1)} %get-tuple-element.59) | copy-start | bytes 884740
  302.0 2.2 copy-start.6
  303.2 2.6 copy-start.1
  304.3 4.0 %copy-start.3 = (bf16[128,768]{1,0:T(8,128)(2,1)S(1)}, bf16[128,768]{1,0:T(8,128)(2,1)}, u32[]{:S(2)}) copy-start(bf16[128,768]{1,0:T(8,128)(2,1)} %get-tuple-element.51) | copy-start | bytes 589828
  304.5 4.5 %copy-start.4 = (bf16[128,768]{1,0:T(8,128)(2,1)S(1)}, bf16[128,768]{1,0:T(8,128)(2,1)}, u32[]{:S(2)}) copy-start(bf16[128,768]{1,0:T(8,128)(2,1)} %get-tuple-element.64) | copy-start | bytes 589828
  304.5 5.1 %copy-start.2 = (f32[96,768]{1,0:T(8,128)S(1)}, f32[96,768]{1,0:T(8,128)}, u32[]{:S(2)}) copy-start(f32[96,768]{1,0:T(8,128)} %get-tuple-element.116) | copy-start | bytes 884740

commit v2 on v0

v2 whole, which is shorter than its diff:
```python
import functools
import math

import jax
import jax.numpy as jnp
from jax import lax
from jax.experimental import pallas as pl
from jax.experimental.pallas import tpu as pltpu
from jax.sharding import PartitionSpec as P

HEAD_DIM = 64
FREQ = 192
GRID_Z = 4
GRID_X = 2
GROUP = GRID_Z * GRID_X
BLK = 4
MESH = pl.DeviceIdType.MESH
F32 = jnp.float32
BF16 = jnp.bfloat16
VMEM_BYTES = 56 << 20


def mm(left, right):
    return jnp.dot(left, right, preferred_element_type=F32)


def mm_t(left, right):
    return lax.dot_general(left, right, (((1,), (1,)), ((), ())), preferred_element_type=F32)


def tmm(left, right):
    return lax.dot_general(left, right, (((0,), (0,)), ((), ())), preferred_element_type=F32)


class Place:
    def __init__(self, spread):
        pages = lax.axis_index("pages")
        self.spread = spread
        self.hi = pages // spread
        self.lo = pages % spread
        self.z = self.hi // GRID_X
        self.x = self.hi % GRID_X
        self.b = lax.axis_index("blk")
        self.pages = pages
        self.sib = self.b + 1 - 2 * (self.b % 2)
        self.across = (self.b + 2) % BLK
        self.diag = (self.sib + 2) % BLK

    def at(self, z, x):
        return ((z * GRID_X + x) * self.spread + self.lo, self.b)

    def in_page(self, b):
        return (self.pages, b)

    def blk_peers(self):
        return (self.sib, self.across, self.diag)

    def z_at(self, step):
        return (self.z + step) % GRID_Z


def remote(src, dst, send, recv, device):
    return pltpu.make_async_remote_copy(
        src_ref=src, dst_ref=dst, send_sem=send, recv_sem=recv, device_id=device, device_id_type=MESH
    )


def meet(devices):
    barrier = pltpu.get_barrier_semaphore()
    for device in devices:
        pl.semaphore_signal(barrier, inc=1, device_id=device, device_id_type=MESH)
    pl.semaphore_wait(barrier, len(devices))


class BlkGather:
    def __init__(self, place, dst, send, recv):
        self.place, self.dst = place, dst
        b, across = place.b, place.across
        self.to_sib = remote(dst.at[b], dst.at[b], send.at[0], recv.at[0], place.in_page(place.sib))
        self.to_across = remote(dst.at[b], dst.at[b], send.at[1], recv.at[1], place.in_page(across))
        self.forward = remote(
            dst.at[across], dst.at[across], send.at[2], recv.at[2], place.in_page(place.sib)
        )

    def start(self):
        self.to_across.start()
        self.to_sib.start()

    def wait_sib(self):
        self.to_sib.wait_recv()

    def wait_across(self):
        self.to_across.wait_recv()
        self.forward.start()

    def wait_diag(self):
        self.forward.wait_recv()

    def finish(self):
        self.to_sib.wait_send()
        self.to_across.wait_send()
        self.forward.wait_send()


class BlkReduce:
    def __init__(self, place, parts, near, far, send, recv):
        self.place, self.parts, self.near, self.far = place, parts, near, far
        sib, across = place.sib, place.across
        self.sib_far = remote(
            parts.at[place.diag], near.at[1], send.at[0], recv.at[0], place.in_page(sib)
        )
        self.sib_near = remote(parts.at[sib], near.at[0], send.at[1], recv.at[1], place.in_page(sib))
        self.cross = remote(near.at[1], far, send.at[2], recv.at[2], place.in_page(across))

    def send_cross(self):
        self.sib_far.wait_recv()
        both = self.parts[self.place.across].astype(F32) + self.near[1].astype(F32)
        self.near[1] = both.astype(BF16)
        self.cross.start()

    def total(self, own):
        self.sib_near.wait_recv()
        partial = own + self.near[0].astype(F32)
        self.cross.wait_recv()
        return partial + self.far[...].astype(F32)

    def finish(self):
        self.sib_far.wait_send()
        self.sib_near.wait_send()
        self.cross.wait_send()


def vmem_call(kernel, outs, scratch, name, collective=None, smem=()):
    def run(*operands):
        params = dict(vmem_limit_bytes=VMEM_BYTES)
        if collective is not None:
            params.update(collective_id=collective, has_side_effects=True)
        return pl.pallas_call(
            kernel,
            name=name,
            out_shape=[jax.ShapeDtypeStruct(shape, kind) for shape, kind in outs],
            in_specs=[
                pl.BlockSpec(memory_space=pltpu.SMEM if i in smem else pltpu.VMEM)
                for i in range(len(operands))
            ],
            out_specs=[pl.BlockSpec(memory_space=pltpu.VMEM) for _ in outs],
            scratch_shapes=scratch,
            compiler_params=pltpu.CompilerParams(**params),
        )(*operands)

    return run


HEADS = 3
HEAD_COLS = 6 * HEAD_DIM
A_CHUNKS, B_CHUNKS, C_CHUNKS = (0, 1, 2), (3, 4), (5, 6)
CHUNKS = 7
VEC = 7
SPAN = 2 * FREQ


def centred(values):
    mean = jnp.mean(values, axis=-1, keepdims=True)
    centre = values - mean
    scale = lax.rsqrt(jnp.mean(centre * centre, axis=-1, keepdims=True) + 1e-12)
    return centre * scale, scale


def norm_back(grad_hat, hat, scale):
    first = jnp.mean(grad_hat, axis=-1, keepdims=True)
    second = jnp.mean(grad_hat * hat, axis=-1, keepdims=True)
    return scale * (grad_hat - first - hat * second)


def column_sum(values):
    return jnp.sum(values, axis=0, keepdims=True)


def block_rows(blk):
    return pl.ds(pl.multiple_of(blk * 128, 128), 128)


def layer_kernel(
    spread,
    lengths,
    w_qkv,
    w_relq,
    w_relk,
    w_out,
    w_up,
    w_down,
    hidden,
    cot,
    box,
    vec,
    out,
    grad_hid,
    sums,
    sum_c,
    vec_out,
    weights,
    grads,
    pair,
    line,
    cut,
    pack_a,
    pack_b,
    land_a,
    land_b,
    land_vec,
    all_vec,
    all_hid,
    all_box,
    all_out,
    vec_sum,
    table,
    feats,
    qkv,
    relq,
    relk,
    qrel,
    krel,
    probs,
    ctx,
    ctx_own,
    ctx_all,
    normed_all,
    act,
    slope,
    branch_all,
    g_middle,
    parts,
    near,
    far,
    g_attn_own,
    g_attn_cols,
    g_ctx_own,
    g_ctx,
    go_heads,
    g_scores,
    p_low,
    g_heads,
    g_qkv,
    gvec,
    gvec_all,
    gvec_page,
    ag_x,
    ag_z,
    rs_x,
    rs_z,
    in_swap,
    gather_sem,
    reduce_sem,
    mid_swap,
    out_swap,
):
    place = Place(spread)
    b = place.b
    peers = place.blk_peers()
    order = (b, place.sib, place.across, place.diag)
    partner = place.at(place.z, 1 - place.x)
    width = hidden.shape[1]
    tokens = BLK * hidden.shape[0]
    third = HEADS * HEAD_DIM
    ff_part = w_up.shape[1] // (GROUP * BLK)
    sends = []


    def shard_at(step, x):
        return place.z_at(step) * GRID_X + x

    def start(copy):
        copy.start()
        sends.append(copy)
        return copy

    class Spread:
        def __init__(self, whole, index, sem_x, sem_z):
            self.whole, self.index, self.sem_x, self.sem_z = whole, index, sem_x, sem_z

        def begin(self):
            own = self.whole.at[place.hi]
            self.along = []
            for step in range(1, GRID_Z):
                self.along.append(
                    start(
                        remote(
                            own,
                            own,
                            self.sem_z.at[0, self.index, step - 1],
                            self.sem_z.at[1, self.index, step - 1],
                            place.at(place.z_at(step), place.x),
                        )
                    )
                )
            self.over = [self._over(own, 0)]

        def _over(self, ref, slot):
            return start(
                remote(
                    ref,
                    ref,
                    self.sem_x.at[0, self.index, slot],
                    self.sem_x.at[1, self.index, slot],
                    partner,
                )
            )

        def pass_on(self):
            for step in range(1, GRID_Z):
                self.along[step - 1].wait_recv()
                self.over.append(self._over(self.whole.at[shard_at(GRID_Z - step, place.x)], step))

        def settle(self):
            for copy in self.over:
                copy.wait_recv()

    class Sum:
        def __init__(self, index):
            self.index = index
            self.grad = grads.at[index]

        def begin(self):
            self.over = []
            for step in (1, 2, 3, 0):
                self.over.append(
                    start(
                        remote(
                            self.grad.at[shard_at(step, 1 - place.x)],
                            pair.at[self.index, step],
                            rs_x.at[0, self.index, step],
                            rs_x.at[1, self.index, step],
                            partner,
                        )
                    )
                )

        def pass_on(self):
            self.along = []
            for step in range(1, GRID_Z):
                self.over[step - 1].wait_recv()
                both = self.grad[shard_at(step, place.x)].astype(F32) + pair[
                    self.index, step
                ].astype(F32)
                pair[self.index, step] = both.astype(BF16)
                self.along.append(
                    start(
                        remote(
                            pair.at[self.index, step],
                            line.at[self.index, step - 1],
                            rs_z.at[0, self.index, step - 1],
                            rs_z.at[1, self.index, step - 1],
                            place.at(place.z_at(step), place.x),
                        )
                    )
                )

        def settle(self):
            index = self.index
            self.over[3].wait_recv()
            value = self.grad[shard_at(0, place.x)].astype(F32) + pair[index, 0].astype(F32)
            for step in range(1, GRID_Z):
                self.along[step - 1].wait_recv()
                value = value + line[index, step - 1].astype(F32)
            if index in C_CHUNKS:
                at = (index - C_CHUNKS[0]) * HEAD_COLS
                sum_c[:, at : at + HEAD_COLS] = value
                return []
            rows = value.shape[0] // BLK
            for blk in range(BLK):
                cut[index, blk] = value[blk * rows : (blk + 1) * rows, :].astype(BF16)
            sums[index, b] = cut[index, b]
            return [
                start(
                    remote(
                        cut.at[index, peer],
                        sums.at[index, b],
                        out_swap.at[0, index, slot],
                        out_swap.at[1, index, slot],
                        place.in_page(peer),
                    )
                )
                for slot, peer in enumerate(peers)
            ]

    def swap(sem, which, source_of, target):
        return [
            start(
                remote(
                    source_of(peer),
                    target.at[b],
                    sem.at[0, which, slot],
                    sem.at[1, which, slot],
                    place.in_page(peer),
                )
            )
            for slot, peer in enumerate(peers)
        ]

    def arrive(copies):
        for copy in copies:
            copy.wait_recv()

    def blk_gather(which, dst):
        return BlkGather(place, dst, gather_sem.at[0, which], gather_sem.at[1, which])

    def blk_reduce(which):
        return BlkReduce(
            place,
            parts.at[which],
            near.at[which],
            far.at[which],
            reduce_sem.at[0, which],
            reduce_sem.at[1, which],
        )


    for blk in range(BLK):
        for head in range(HEADS):
            at = blk * third + head * HEAD_DIM
            lanes = slice(at, at + HEAD_DIM)
            columns = [
                w_qkv[:, part * width + at : part * width + at + HEAD_DIM] for part in range(3)
            ]
            columns = columns + [w_relq[:, lanes], w_relk[:, lanes], w_out[:, lanes]]
            pack_a[blk, :, head * HEAD_COLS : (head + 1) * HEAD_COLS] = jnp.concatenate(
                columns, axis=1
            )
        pack_b[blk] = jnp.concatenate(
            [
                w_up[:, (page * BLK + blk) * ff_part : (page * BLK + blk + 1) * ff_part]
                for page in range(GROUP)
            ],
            axis=1,
        )
    all_hid[b] = hidden[...]
    all_box[b] = box[...]
    for half, index in enumerate(C_CHUNKS):
        weights[index, place.hi] = w_down[:, half * HEAD_COLS : (half + 1) * HEAD_COLS]

    meet(
        [place.in_page(peer) for peer in peers]
        + [partner]
        + [place.at(place.z_at(step), place.x) for step in range(1, GRID_Z)]
    )
    chunk = [Spread(weights.at[index], index, ag_x, ag_z) for index in range(CHUNKS)]
    chunk.append(Spread(all_vec, VEC, ag_x, ag_z))
    swap_a = swap(in_swap, 0, lambda peer: pack_a.at[peer], land_a)
    swap_vec = swap(in_swap, 1, lambda peer: vec.at[peer], land_vec)
    gather_box = blk_gather(0, all_box)
    gather_hid = blk_gather(1, all_hid)
    gather_box.start()
    gather_hid.start()
    chunk[5].begin()
    swap_b = swap(in_swap, 2, lambda peer: pack_b.at[peer], land_b)

    places = lax.broadcasted_iota(jnp.int32, (256, FREQ), 0).astype(F32)
    ladder = lax.broadcasted_iota(jnp.int32, (256, FREQ), 1).astype(F32)
    angles = places * jnp.exp(ladder * (-math.log(10000.0) / FREQ))
    cosines, sines, blank = jnp.cos(angles), jnp.sin(angles), jnp.zeros((256, FREQ), F32)
    table[0:256, :] = jnp.concatenate([cosines, blank, sines, blank], axis=1).astype(BF16)
    table[256:512, :] = jnp.concatenate([blank, cosines, blank, sines], axis=1).astype(BF16)

    land_a[b] = pack_a[b]
    arrive(swap_a)
    joined = jnp.concatenate([land_a[blk].astype(F32) for blk in range(BLK)], axis=0).astype(BF16)
    for head in range(HEADS):
        weights[head, place.hi] = joined[:, head * HEAD_COLS : (head + 1) * HEAD_COLS]
    chunk[0].begin()
    land_vec[b] = vec[b]
    arrive(swap_vec)
    all_vec[place.hi] = (
        land_vec[0].astype(F32)
        + land_vec[1].astype(F32)
        + land_vec[2].astype(F32)
        + land_vec[3].astype(F32)
    ).astype(BF16)
    chunk[VEC].begin()
    gather_box.wait_across()
    gather_hid.wait_across()
    chunk[1].begin()

    gather_box.wait_sib()
    gather_box.wait_diag()
    slots = lax.broadcasted_iota(jnp.int32, (256, tokens // BLK), 0)
    for blk in range(BLK):
        hot = jnp.concatenate(
            [
                jnp.where(slots == all_box[blk][0:1, :], 1.0, 0.0),
                jnp.where(slots == all_box[blk][1:2, :], 1.0, 0.0),
            ],
            axis=0,
        ).astype(BF16)
        feats[blk * 128 : (blk + 1) * 128, :] = tmm(hot, table[...]).astype(BF16)
    land_b[b] = pack_b[b]
    arrive(swap_b)
    joined = jnp.concatenate([land_b[blk].astype(F32) for blk in range(BLK)], axis=0).astype(BF16)
    for half, index in enumerate(B_CHUNKS):
        weights[index, place.hi] = joined[:, half * HEAD_COLS : (half + 1) * HEAD_COLS]
    chunk[5].pass_on()
    chunk[2].begin()
    chunk[VEC].pass_on()
    chunk[0].pass_on()
    chunk[3].begin()
    gather_hid.wait_sib()
    gather_hid.wait_diag()
    chunk[VEC].settle()
    total = all_vec[0].astype(F32)
    for shard in range(1, GROUP):
        total = total + all_vec[shard].astype(F32)
    vec_sum[...] = total

    rows_whole = GROUP * weights.shape[2]
    whole = weights.reshape(CHUNKS, rows_whole, HEAD_COLS)
    hid = all_hid.reshape(tokens, width)
    usable = lax.broadcasted_iota(jnp.int32, (128, tokens), 1) < lengths[0]

    def head_forward(head):
        bias = vec_sum[0:1, head * 3 * HEAD_DIM : (head + 1) * 3 * HEAD_DIM]

        def project(blk, carry):
            rows = block_rows(blk)
            low = (mm(hid[rows, :], whole[head, :, : 3 * HEAD_DIM]) + bias).astype(BF16)
            for part in range(3):
                qkv[3 * part + head, rows, :] = low[:, part * HEAD_DIM : (part + 1) * HEAD_DIM]
            return carry

        lax.fori_loop(0, BLK, project, 0)
        relq[head] = whole[head, :, 3 * HEAD_DIM : 4 * HEAD_DIM]
        relk[head] = whole[head, :, 4 * HEAD_DIM : 5 * HEAD_DIM]
        all_out[b, :, head * HEAD_DIM : (head + 1) * HEAD_DIM] = whole[
            head, :, 5 * HEAD_DIM : 6 * HEAD_DIM
        ]
        yield

        def turn(blk, carry):
            rows = block_rows(blk)
            cos_part = feats[rows, :SPAN].astype(F32)
            sin_part = feats[rows, SPAN:].astype(F32)
            u = mm_t(qkv[head, rows, :], relq[head])
            u1, u2 = u[:, :SPAN], u[:, SPAN:]
            qrel[rows, :SPAN] = (u1 * cos_part + u2 * sin_part).astype(BF16)
            qrel[rows, SPAN:] = (u1 * sin_part - u2 * cos_part).astype(BF16)
            v = mm_t(qkv[3 + head, rows, :], relk[head])
            v1, v2 = v[:, :SPAN], v[:, SPAN:]
            krel[rows, :SPAN] = (v1 * cos_part - v2 * sin_part).astype(BF16)
            krel[rows, SPAN:] = (v1 * sin_part + v2 * cos_part).astype(BF16)
            return carry

        lax.fori_loop(0, BLK, turn, 0)
        yield

        def rows_of(blk, carry):
            rows = block_rows(blk)
            scores = mm_t(qrel[rows, :], feats[...])
            scores = scores + mm_t(feats[rows, :], krel[...])
            scores = scores + mm_t(qkv[head, rows, :], qkv[3 + head])
            masked = jnp.where(usable, scores * 0.125, -1e30)
            raised = jnp.exp(masked - jnp.max(masked, axis=-1, keepdims=True))
            prob = raised / jnp.sum(raised, axis=-1, keepdims=True)
            probs[head, rows, :] = prob
            ctx[blk, :, head * HEAD_DIM : (head + 1) * HEAD_DIM] = mm(
                prob.astype(BF16), qkv[6 + head]
            ).astype(BF16)
            return carry

        lax.fori_loop(0, 2, rows_of, 0)
        yield
        lax.fori_loop(2, BLK, rows_of, 0)
        yield

    def run(generator, events):
        at = 0
        for _ in generator:
            for event in events.get(at, ()):
                event()
            at += 1

    chunk[0].settle()
    run(head_forward(0), {1: (chunk[1].pass_on, chunk[4].begin)})
    chunk[1].settle()
    run(head_forward(1), {1: (chunk[2].pass_on, chunk[6].begin)})
    chunk[2].settle()
    gather_out = blk_gather(2, all_out)

    def out_there():
        gather_out.start()

    def out_passed():
        gather_out.wait_across()

    run(
        head_forward(2),
        {0: (out_there,), 1: (chunk[3].pass_on,), 3: (out_passed, chunk[4].pass_on)},
    )

    swap_ctx = swap(mid_swap, 0, lambda peer: ctx.at[peer], ctx_own)
    ctx_own[b] = ctx[b]
    gather_out.wait_sib()
    gather_out.wait_diag()
    arrive(swap_ctx)
    own = jnp.concatenate([ctx_own[blk] for blk in range(BLK)], axis=1)
    attn = jnp.concatenate([mm(own, all_out[blk]) for blk in range(BLK)], axis=1) + vec_sum[2:3, :]
    hat_one, scale_one = centred(hidden[...].astype(F32) + attn)
    gain_one = vec_sum[3:4, :]
    normed = hat_one * gain_one + vec_sum[4:5, :]
    normed_all[b] = normed.astype(BF16)
    gather_normed = blk_gather(3, normed_all)
    gather_normed.start()
    chunk[6].pass_on()
    chunk[3].settle()
    chunk[4].settle()
    reduce_one = blk_reduce(0)

    def up(blk):
        for half, index in enumerate(B_CHUNKS):
            lanes = slice(half * HEAD_COLS, (half + 1) * HEAD_COLS)
            middle = mm(normed_all[blk], whole[index]) + vec_sum[1:2, lanes]
            gate = 0.5 * (1.0 + lax.erf(middle * math.sqrt(0.5)))
            act[blk, :, lanes] = (middle * gate).astype(BF16)
            bell = jnp.exp(-0.5 * middle * middle) * (1.0 / math.sqrt(2.0 * math.pi))
            slope[blk, :, lanes] = gate + middle * bell

    def down(blk):
        return jnp.concatenate([mm(act[blk], whole[index]) for index in C_CHUNKS], axis=1)

    up(b)
    gather_normed.wait_sib()
    up(place.sib)
    chunk[5].settle()
    chunk[6].settle()
    gather_normed.wait_across()
    parts[0, place.sib] = down(place.sib).astype(BF16)
    reduce_one.sib_near.start()
    up(place.across)
    parts[0, place.across] = down(place.across).astype(BF16)
    gather_normed.wait_diag()
    up(place.diag)
    parts[0, place.diag] = down(place.diag).astype(BF16)
    reduce_one.sib_far.start()
    own_branch = down(b)
    reduce_one.send_cross()
    branch = reduce_one.total(own_branch) + vec_sum[5:6, :]

    hat_two, scale_two = centred(normed + branch)
    gain_two = vec_sum[6:7, :]
    cot_wide = cot[...].astype(F32)
    g_two = norm_back(cot_wide * gain_two, hat_two, scale_two)
    branch_all[b] = g_two.astype(BF16)
    gather_branch = blk_gather(4, branch_all)
    gather_branch.start()
    out[...] = (hat_two * gain_two + vec_sum[7:8, :]).astype(BF16)
    gvec[6:7, :] = column_sum(cot_wide * hat_two)
    gvec[7:8, :] = column_sum(cot_wide)
    gvec[5:6, :] = column_sum(branch_all[b].astype(F32))
    gvec[8:16, :] = jnp.zeros((8, width), F32)
    reduce_two = blk_reduce(1)

    def back(blk):
        slab = mm_t(branch_all[blk, :, :HEAD_COLS], whole[C_CHUNKS[0]])
        slab = slab + mm_t(branch_all[blk, :, HEAD_COLS:], whole[C_CHUNKS[1]])
        low = (slab * slope[blk]).astype(BF16)
        g_middle[blk] = low
        part = mm_t(low[:, :HEAD_COLS], whole[B_CHUNKS[0]])
        return part + mm_t(low[:, HEAD_COLS:], whole[B_CHUNKS[1]])

    own_normed = back(b)
    gather_branch.wait_sib()
    parts[1, place.sib] = back(place.sib).astype(BF16)
    reduce_two.sib_near.start()
    gather_branch.wait_across()
    parts[1, place.across] = back(place.across).astype(BF16)
    gather_branch.wait_diag()
    parts[1, place.diag] = back(place.diag).astype(BF16)
    reduce_two.sib_far.start()

    act_rows = act.reshape(tokens, act.shape[2])
    branch_rows = branch_all.reshape(tokens, width)
    normed_rows = normed_all.reshape(tokens, width)
    middle_rows = g_middle.reshape(tokens, act.shape[2])
    flat_grads = grads.reshape(CHUNKS, rows_whole, HEAD_COLS)

    def weight_grad(index, left, right):
        def step(at, carry):
            cols = pl.ds(pl.multiple_of(at * 256, 256), 256)
            flat_grads[index, cols, :] = tmm(left[:, cols], right()).astype(BF16)
            return carry

        lax.fori_loop(0, rows_whole // 256, step, 0)

    summed = [Sum(index) for index in range(CHUNKS)]
    weight_grad(5, act_rows, lambda: branch_rows[:, :HEAD_COLS])
    summed[5].begin()
    reduce_two.send_cross()
    weight_grad(6, act_rows, lambda: branch_rows[:, HEAD_COLS:])
    summed[6].begin()
    weight_grad(3, normed_rows, lambda: middle_rows[:, :HEAD_COLS])
    weight_grad(4, normed_rows, lambda: middle_rows[:, HEAD_COLS:])
    gvec[1:2, :] = column_sum(middle_rows[...].astype(F32))
    g_normed = g_two + reduce_two.total(own_normed)

    g_one = norm_back(g_normed * gain_one, hat_one, scale_one)
    g_attn = g_one.astype(BF16)
    for blk in range(BLK):
        g_attn_own[blk] = g_attn[:, blk * third : (blk + 1) * third]
    wide = mm_t(g_attn_own[0], all_out[0])
    for blk in range(1, BLK):
        wide = wide + mm_t(g_attn_own[blk], all_out[blk])
    for blk in range(BLK):
        g_ctx_own[blk] = wide[:, blk * third : (blk + 1) * third].astype(BF16)
    swap_back = swap(mid_swap, 1, lambda peer: g_ctx_own.at[peer], g_ctx)
    g_ctx[b] = g_ctx_own[b]
    gvec[3:4, :] = column_sum(g_normed * hat_one)
    gvec[4:5, :] = column_sum(g_normed)
    gvec[2:3, :] = column_sum(g_attn.astype(F32))
    summed[5].pass_on()
    summed[3].begin()
    arrive(swap_back)
    swap_attn = swap(mid_swap, 2, lambda peer: g_attn_own.at[peer], g_attn_cols)
    g_attn_cols[b] = g_attn_own[b]
    spread_ctx = swap(mid_swap, 3, lambda peer: ctx, ctx_all)
    ctx_all[b] = ctx[...]

    g_ctx_rows = g_ctx.reshape(tokens, third)
    ctx_rows = ctx.reshape(tokens, third)

    def head_backward(head):
        lanes = slice(head * HEAD_DIM, (head + 1) * HEAD_DIM)
        go_heads[...] = g_ctx_rows[:, lanes]

        def query_rows(blk, carry):
            rows = block_rows(blk)
            go = go_heads[rows, :]
            delta = jnp.sum(
                go.astype(F32) * ctx_rows[rows, lanes].astype(F32), axis=-1, keepdims=True
            )
            prob = probs[head, rows, :]
            p_low[rows, :] = prob.astype(BF16)
            ds = (prob * (mm_t(go, qkv[6 + head]) - delta)).astype(BF16)
            g_scores[rows, :] = ds
            turned = 0.125 * mm(ds, feats[...])
            a1, a2 = turned[:, :SPAN], turned[:, SPAN:]
            cos_part = feats[rows, :SPAN].astype(F32)
            sin_part = feats[rows, SPAN:].astype(F32)
            qrel[rows, :SPAN] = (a1 * cos_part + a2 * sin_part).astype(BF16)
            qrel[rows, SPAN:] = (a1 * sin_part - a2 * cos_part).astype(BF16)
            gq = 0.125 * mm(ds, qkv[3 + head]) + mm(qrel[rows, :], relq[head])
            g_heads[0, rows, :] = gq.astype(BF16)
            return carry

        lax.fori_loop(0, 2, query_rows, 0)
        yield
        lax.fori_loop(2, BLK, query_rows, 0)
        yield

        def key_rows(blk, carry):
            rows = block_rows(blk)
            ds = g_scores[:, rows]
            turned = 0.125 * tmm(ds, feats[...])
            b1, b2 = turned[:, :SPAN], turned[:, SPAN:]
            cos_part = feats[rows, :SPAN].astype(F32)
            sin_part = feats[rows, SPAN:].astype(F32)
            krel[rows, :SPAN] = (b1 * cos_part + b2 * sin_part).astype(BF16)
            krel[rows, SPAN:] = (b2 * cos_part - b1 * sin_part).astype(BF16)
            gk = 0.125 * tmm(ds, qkv[head]) + mm(krel[rows, :], relk[head])
            g_heads[1, rows, :] = gk.astype(BF16)
            g_heads[2, rows, :] = tmm(p_low[:, rows], go_heads[...]).astype(BF16)
            return carry

        lax.fori_loop(0, 2, key_rows, 0)
        yield
        lax.fori_loop(2, BLK, key_rows, 0)
        yield
        g_qkv[head] = jnp.concatenate([g_heads[part] for part in range(3)], axis=1)
        gvec[0:1, head * third : (head + 1) * third] = column_sum(g_qkv[head].astype(F32))

        def chunk_rows(at, carry):
            cols = pl.ds(pl.multiple_of(at * 256, 256), 256)
            flat_grads[head, cols, :] = jnp.concatenate(
                [
                    tmm(hid[:, cols], g_qkv[head]),
                    tmm(qrel[:, cols], qkv[head]),
                    tmm(krel[:, cols], qkv[3 + head]),
                    tmm(
                        ctx_flat(at), g_attn_cols_rows[:, lanes]
                    ),
                ],
                axis=1,
            ).astype(BF16)
            return carry

        for at in range(rows_whole // 256):
            chunk_rows(at, 0)
        yield

    g_attn_cols_rows = g_attn_cols.reshape(tokens, third)

    def ctx_flat(at):
        pieces, start_col = [], at * 256
        while start_col < (at + 1) * 256:
            owner = start_col // third
            stop = min((owner + 1) * third, (at + 1) * 256)
            pieces.append(
                ctx_all.reshape(BLK, tokens, third)[
                    owner, :, start_col - owner * third : stop - owner * third
                ]
            )
            start_col = stop
        return jnp.concatenate(pieces, axis=1)

    def cross_there():
        arrive(swap_attn)
        arrive(spread_ctx)

    finals = []

    def settle(index):
        def done():
            finals.extend(summed[index].settle())

        return done

    gvec[0:1, 3 * third :] = jnp.zeros((1, width - 3 * third), F32)
    run(
        head_backward(0),
        {
            1: (summed[6].pass_on, summed[4].begin),
            3: (cross_there,),
            4: (summed[3].pass_on, settle(5), summed[0].begin),
        },
    )
    run(
        head_backward(1),
        {
            2: (summed[4].pass_on, settle(6)),
            4: (summed[1].begin,),
        },
    )
    run(
        head_backward(2),
        {
            1: (summed[0].pass_on, settle(3)),
            4: (summed[2].begin,),
        },
    )
    gvec_all[place.hi] = gvec[...].astype(BF16)
    vec_back = Spread(gvec_all, VEC, rs_x, rs_z)
    vec_back.begin()
    reduce_hid = blk_reduce(2)

    def part_hid(blk):
        total = mm_t(g_qkv[0, block_rows(blk), :], whole[0, :, :third])
        for head in range(1, HEADS):
            total = total + mm_t(g_qkv[head, block_rows(blk), :], whole[head, :, :third])
        return total

    parts[2, place.diag] = part_hid(place.diag).astype(BF16)
    reduce_hid.sib_far.start()
    parts[2, place.across] = part_hid(place.across).astype(BF16)
    reduce_hid.send_cross()
    parts[2, place.sib] = part_hid(place.sib).astype(BF16)
    reduce_hid.sib_near.start()
    own_hid = part_hid(b) + g_one
    settle(4)()
    summed[1].pass_on()
    vec_back.pass_on()
    vec_back.settle()
    total = gvec_all[0].astype(F32)
    for shard in range(1, GROUP):
        total = total + gvec_all[shard].astype(F32)
    gvec_page[b] = total
    gather_vec = blk_gather(5, gvec_page)
    gather_vec.start()
    grad_hid[...] = reduce_hid.total(own_hid).astype(BF16)
    gather_vec.wait_across()
    settle(0)()
    summed[2].pass_on()
    settle(1)()
    gather_vec.wait_sib()
    gather_vec.wait_diag()
    vec_out[...] = gvec_page[...]
    settle(2)()
    arrive(finals)
    for copy in sends:
        copy.wait_send()
    for reduce in (reduce_one, reduce_two, reduce_hid):
        reduce.finish()
    for gather in (gather_box, gather_hid, gather_out, gather_normed, gather_branch, gather_vec):
        gather.finish()


def on_device(
    hidden,
    boxes,
    lengths,
    w_qkv,
    b_qkv,
    w_relq,
    w_relk,
    w_out,
    b_out,
    ln1_gain,
    ln1_bias,
    w_up,
    b_up,
    w_down,
    b_down,
    ln2_gain,
    ln2_bias,
    cotangent,
):
    page_count = lax.axis_size("pages")
    spread = page_count // GROUP
    b = lax.axis_index("blk")
    hi = lax.axis_index("pages") // spread
    _, tok, width = hidden.shape
    third = 3 * HEAD_DIM
    groups = [[h * spread + low for low in range(spread)] for h in range(GROUP)]

    def grow(rows):
        if spread == 1:
            return rows
        rows = lax.all_gather(rows, "blk", axis=0, tiled=True)
        rows = lax.all_gather(rows, "pages", axis=0, tiled=True, axis_index_groups=groups)
        count = rows.shape[0] // BLK
        return lax.dynamic_slice_in_dim(rows, b * count, count, 0)

    def shrink(rows):
        if spread == 1:
            return rows
        rows = lax.all_gather(rows, "blk", axis=0, tiled=True)
        rows = lax.psum_scatter(
            rows, "pages", scatter_dimension=0, tiled=True, axis_index_groups=groups
        )
        count = rows.shape[0] // BLK
        return lax.dynamic_slice_in_dim(rows, b * count, count, 0)

    w_qkv, w_relq, w_relk, w_out, w_up, w_down = map(
        grow, (w_qkv, w_relq, w_relk, w_out, w_up, w_down)
    )
    b_qkv, b_up, b_out, ln1_gain, ln1_bias, b_down, ln2_gain, ln2_bias = map(
        grow, (b_qkv, b_up, b_out, ln1_gain, ln1_bias, b_down, ln2_gain, ln2_bias)
    )
    rows = w_qkv.shape[0]
    shard = BLK * rows
    ff_part = w_up.shape[1] // (GROUP * BLK)

    here = (lax.iota(jnp.int32, GROUP * BLK) == hi * BLK + b).astype(BF16)
    spot = here[:, None]
    own_bias = (spot * b_qkv[None, :]).reshape(3, BLK, HEADS, HEAD_DIM).transpose(1, 2, 0, 3)
    own_bias = own_bias.reshape(BLK, 3 * third)
    own_bias = jnp.pad(own_bias, ((0, 0), (0, width - 3 * third)))
    up_spot = (spot * b_up[None, :]).reshape(GROUP, BLK, ff_part).transpose(1, 0, 2)
    up_spot = up_spot.reshape(BLK, GROUP * ff_part)
    plain = jnp.stack([b_out, ln1_gain, ln1_bias, b_down, ln2_gain, ln2_bias])
    plain = (spot[None] * plain[:, None, :]).reshape(6, width)
    vec = jnp.concatenate(
        [
            own_bias[:, None, :],
            up_spot[:, None, :],
            jnp.broadcast_to(plain[None], (BLK, 6, width)),
            jnp.zeros((BLK, 8, width), BF16),
        ],
        axis=1,
    )
    box = jnp.pad(boxes[0].T, ((0, 6), (0, 0)))

    tokens = BLK * tok
    sem = pltpu.SemaphoreType.DMA

    def held(*shape, kind=BF16):
        return pltpu.VMEM(shape, kind)

    outs = [
        ((tok, width), BF16),
        ((tok, width), BF16),
        ((5, BLK, rows, HEAD_COLS), BF16),
        ((shard, width), F32),
        ((BLK, 16, width), F32),
    ]
    scratch = dict(
        weights=held(CHUNKS, GROUP, shard, HEAD_COLS),
        grads=held(CHUNKS, GROUP, shard, HEAD_COLS),
        pair=held(CHUNKS, GRID_Z, shard, HEAD_COLS),
        line=held(CHUNKS, GRID_Z - 1, shard, HEAD_COLS),
        cut=held(5, BLK, rows, HEAD_COLS),
        pack_a=held(BLK, rows, 3 * HEAD_COLS),
        pack_b=held(BLK, rows, GROUP * ff_part),
        land_a=held(BLK, rows, 3 * HEAD_COLS),
        land_b=held(BLK, rows, GROUP * ff_part),
        land_vec=held(BLK, 16, width),
        all_vec=held(GROUP, 16, width),
        all_hid=held(BLK, tok, width),
        all_box=held(BLK, 8, tok, kind=jnp.int32),
        all_out=held(BLK, GROUP * shard, third),
        vec_sum=held(16, width, kind=F32),
        table=held(512, width),
        feats=held(tokens, width),
        qkv=held(9, tokens, HEAD_DIM),
        relq=held(3, width, HEAD_DIM),
        relk=held(3, width, HEAD_DIM),
        qrel=held(tokens, width),
        krel=held(tokens, width),
        probs=held(3, tokens, tokens, kind=F32),
        ctx=held(BLK, tok, third),
        ctx_own=held(BLK, tok, third),
        ctx_all=held(BLK, BLK, tok, third),
        normed_all=held(BLK, tok, width),
        act=held(BLK, tok, GROUP * ff_part),
        slope=held(BLK, tok, GROUP * ff_part, kind=F32),
        branch_all=held(BLK, tok, width),
        g_middle=held(BLK, tok, GROUP * ff_part),
        parts=held(3, BLK, tok, width),
        near=held(3, 2, tok, width),
        far=held(3, tok, width),
        g_attn_own=held(BLK, tok, third),
        g_attn_cols=held(BLK, tok, third),
        g_ctx_own=held(BLK, tok, third),
        g_ctx=held(BLK, tok, third),
        go_heads=held(tokens, HEAD_DIM),
        g_scores=held(tokens, tokens),
        p_low=held(tokens, tokens),
        g_heads=held(3, tokens, HEAD_DIM),
        g_qkv=held(3, tokens, third),
        gvec=held(16, width, kind=F32),
        gvec_all=held(GROUP, 16, width),
        gvec_page=held(BLK, 16, width, kind=F32),
        ag_x=sem((2, CHUNKS + 1, 4)),
        ag_z=sem((2, CHUNKS + 1, 3)),
        rs_x=sem((2, CHUNKS + 1, 4)),
        rs_z=sem((2, CHUNKS + 1, 3)),
        in_swap=sem((2, 3, 3)),
        gather_sem=sem((2, 6, 3)),
        reduce_sem=sem((2, 3, 3)),
        mid_swap=sem((2, 4, 3)),
        out_swap=sem((2, 5, 3)),
    )
    out, grad_hid, sums, sum_c, vec_out = vmem_call(
        functools.partial(layer_kernel, spread),
        outs,
        list(scratch.values()),
        "layer",
        collective=1,
        smem=(0,),
    )(
        lengths,
        w_qkv,
        w_relq,
        w_relk,
        w_out,
        w_up,
        w_down,
        hidden[0],
        cotangent[0],
        box,
        vec,
    )

    heads = sums[:HEADS].reshape(HEADS, BLK, rows, 6, HEAD_DIM)

    def columns(part):
        return heads[:, :, :, part].transpose(2, 1, 0, 3).reshape(rows, BLK * third).astype(F32)

    grad_qkv = heads[:, :, :, :3].transpose(2, 3, 1, 0, 4).reshape(rows, 3 * BLK * third)
    grad_qkv = grad_qkv.astype(F32)
    grad_relq, grad_relk, grad_w_out = columns(3), columns(4), columns(5)
    grad_up = sums[HEADS:].reshape(2, BLK, rows, GROUP // 2, ff_part).transpose(2, 0, 3, 1, 4)
    grad_up = grad_up.reshape(rows, GROUP * BLK * ff_part).astype(F32)

    place = lax.axis_index("pages") * BLK + b
    if spread > 1:
        vec_out = lax.psum(vec_out, "pages", axis_index_groups=groups)
    summed = jnp.sum(vec_out[:, 2:8], axis=0)
    bias_all = vec_out[:, 0, : 3 * third].reshape(BLK, HEADS, 3, HEAD_DIM).transpose(2, 0, 1, 3)
    up_all = vec_out[:, 1].reshape(BLK, GROUP, ff_part).transpose(1, 0, 2)
    count = page_count * BLK
    whole = jnp.concatenate(
        [bias_all.reshape(count, -1), up_all.reshape(count, -1)]
        + [summed[row].reshape(count, -1) for row in range(6)],
        axis=1,
    )
    vectors = lax.dynamic_slice_in_dim(whole, place, 1, 0)[0]
    sizes = [3 * BLK * third // count, GROUP * BLK * ff_part // count] + [width // count] * 6
    cuts = [sum(sizes[:at]) for at in range(len(sizes) + 1)]
    g_bias, g_up, g_out, g_gain1, g_shift1, g_down, g_gain2, g_shift2 = [
        vectors[cuts[at] : cuts[at + 1]] for at in range(8)
    ]
    return (
        out[None],
        grad_hid[None],
        shrink(grad_qkv),
        g_bias,
        shrink(grad_relq),
        shrink(grad_relk),
        shrink(grad_w_out),
        g_out,
        g_gain1,
        g_shift1,
        shrink(grad_up),
        g_up,
        shrink(sum_c),
        g_down,
        g_gain2,
        g_shift2,
    )


def solution(mesh):
    rows = P(("pages", "blk"), None)
    vector = P(("pages", "blk"))
    tokens = P("pages", "blk", None)
    return jax.shard_map(
        on_device,
        mesh=mesh,
        in_specs=(
            tokens,
            tokens,
            P("pages"),
            rows,
            vector,
            rows,
            rows,
            rows,
            vector,
            vector,
            vector,
            rows,
            vector,
            rows,
            vector,
            vector,
            vector,
            tokens,
        ),
        out_specs=(
            tokens,
            tokens,
            rows,
            vector,
            rows,
            rows,
            rows,
            vector,
            vector,
            vector,
            rows,
            vector,
            rows,
            vector,
            vector,
            vector,
        ),
        check_vma=False,
    )
```

time: 1230 us -> 191 us (0.16); the launches traced: 1220 us -> 191 us
  waiting for transfers between devices: 750 us -> 0 us
  Pallas kernels: 0 us -> 169 us
  blocking collectives: 164 us -> 0 us
  matrix products: 142 us -> 0 us
  other arithmetic: 59.7 us -> 2.33 us
  local copies, waits for them, and re-layouts: 70.4 us -> 17.3 us
  between operations: 25.2 us -> 1.6 us
    reduce_scatter x10 -> x0, waiting for transfers between devices: 419 us -> none  [the longest x1 164 us: on_device(): lax.psum_scatter(grad_set[8], 'pages', scatter_dimension=0, tiled=True)]
    pallas_call x0 -> x1, Pallas kernels: none -> 169 us  [run(): pl.pallas_call(kernel, name=name, out_shape=[jax.ShapeDtypeStruct(shape,...]
    unnamed x20 -> x0, waiting for transfers between devices: 152 us -> none
    all_gather x6 -> x0, waiting for transfers between devices: 148 us -> none  [the longest x1 71.1 us: on_device(): lax.all_gather(sectioned[10], 'pages', axis=0, tiled=True)]
    dot_general x51 -> x0, matrix products: 142 us -> none  [the longest x4 34.1 us: on_device(): jnp.einsum('phqk,pkhc->pqhc', grad_scores, key_hat, preferred_element_typ...]
    unnamed x4 -> x0, blocking collectives: 89.9 us -> none
    all_gather x7 -> x0, blocking collectives: 74.2 us -> none  [the longest x1 26.1 us: on_device(): lax.all_gather(sectioned[9], 'pages', axis=0, tiled=True)]
    unnamed x409 -> x29, local copies, waits for them, and re-layouts: 41.3 us -> 5.32 us
  transfers between devices with their start and end apart: 28 -> 0, of which waited for: 20 -> 0; matrix products, arithmetic and copies ran while one was open for 19% -> 0% of each run, Pallas kernels for 0% -> 0%
where the time goes in v2:
time: 191 us
  Pallas kernels  169 us (88%)
  local copies, waits for them, and re-layouts  17.3 us (9%)
  other arithmetic  2.33 us (1%)
    pallas_call x1, Pallas kernels, run(): pl.pallas_call(kernel, name=name, out_shape=[jax.ShapeDtypeStruct(shape,...  169 us
    unnamed x29, local copies, waits for them, and re-layouts  5.32 us

profile of v2, /device:TPU:0, one launch (start us, length us, event | category | flops | bytes accessed | tf_op | source)
XLA Modules:
  0.0 190.5 jit_solution(11536217759402237304)
XLA Ops:
  0.7 0.1 mul.81
  0.7 0.1 mul.82
  0.8 0.0 copy-start.8
  0.8 0.0 copy-start.9
  0.9 0.0 copy-start.10
  0.9 0.0 copy-start.5
  0.9 0.0 copy-start.6
  0.9 0.0 copy-start.7
  0.9 0.6 copy-done.8
  1.5 0.0 copy-done.9
  1.5 0.0 copy-done.10
  1.5 0.0 copy-done.5
  1.5 0.0 copy-done.6
  1.6 0.0 copy-done.7
  1.6 0.1 mul.85
  1.8 0.6 copy-done.11
  2.4 0.1 broadcast_multiply_fusion.2
  2.5 0.1 mul.74
  2.6 0.1 reshape.148
  2.7 0.1 mul.75
  2.8 0.1 mul.87
  2.9 0.6 copy-done.12
  3.5 0.1 mul.78
  3.6 0.1 pad.13.clone
  3.7 0.7 maximum_maximum_fusion.vec
  4.4 0.7 copy-done.4
  5.1 0.6 pad.8.box
  6.3 169.3 %layer.1 = (bf16[128,768]{1,0:T(8,128)(2,1)}, bf16[128,768]{1,0:T(8,128)(2,1)}, bf16[5,4,24,384]{3,2,1,0:T(8,128)(2,1)}, f32[96,768]{1,0:T(8,128)}, f32[4,16,768]{2,1,0:T(8,128)}) custom-call(s32[1]{0:T(128)S(6)} %copy.54.lengths, bf16[24,2304]{1,0:T(8,128)(2,1)} %w_qkv.1, bf16[24,768]{1,0:T(8,128)(2,1)} %w_relq.1, bf16[24,768]{1,0:T(8,128)(2,1)} %w_relk.1, ...), custom_call_target="tpu_custom_call" | custom-call | tf_op jit(solution)/shard_map/layer/pallas_call | solution.py:138
  175.6 1.0 slice_reduce_fusion
  176.6 0.1 slice_reduce_fusion.3
  176.7 0.1 reshape_squeeze.26
  176.7 0.1 reshape_squeeze.27
  176.8 0.1 reshape_squeeze.28
  176.9 0.1 reshape_squeeze.29
  177.0 0.1 reshape_squeeze.30
  177.1 0.1 reshape_squeeze.31
  177.2 0.9 slice_reduce_fusion.2
  178.1 0.1 reshape_squeeze.24
  178.2 0.1 reshape.150
  178.3 0.9 slice_reduce_fusion.1
  179.2 0.1 reshape_squeeze.25
  179.3 0.1 concatenate.7
  179.4 0.6 dynamic-slice_bitcast_fusion
  180.1 0.6 dynamic-slice_bitcast_fusion.3
  180.6 0.5 dynamic-slice_bitcast_fusion.7
  181.2 0.3 reshape.149
  181.5 0.4 slice_convert_fusion
  181.9 0.1 copy.47
  182.0 0.8 reshape.153
  182.8 0.1 copy.48
  182.9 0.8 reshape.154
  183.7 0.1 copy.49
  183.9 0.8 reshape.155
  184.7 0.1 convert_bitcast_fusion
  184.8 0.3 copy.44
  185.1 1.1 reshape.152
  186.2 0.3 reshape.160
  186.4 0.3 copy.50
  186.7 1.1 reshape.156
  187.8 0.7 copy.55
  188.5 0.3 copy-done.2
  188.8 0.7 copy.56
  189.5 0.4 copy-done.1
  189.8 0.7 copy.57
  (25 shorter events, 0.2 us)
Async XLA Ops:
  0.8 0.7 copy-start.8
  0.8 0.7 copy-start.9
  0.9 0.7 copy-start.10
  0.9 0.7 copy-start.5
  0.9 0.7 copy-start.6
  0.9 0.7 copy-start.7
  1.8 0.7 copy-start.11
  2.8 0.7 copy-start.12
  4.4 0.7 copy-start.4
  175.6 5.5 %copy-start = (bf16[5,4,24,384]{3,2,1,0:T(8,128)(2,1)S(1)}, bf16[5,4,24,384]{3,2,1,0:T(8,128)(2,1)}, u32[]{:S(2)}) copy-start(bf16[5,4,24,384]{3,2,1,0:T(8,128)(2,1)} %get-tuple-element.23) | copy-start | bytes 1105924
  186.7 1.1 copy-start.3
  187.8 1.0 copy-start.2
  188.8 1.0 copy-start.1

commit v3 on v2

--- a/solution.py
+++ b/solution.py
@@ -59,17 +59,36 @@
         return (self.z + step) % GRID_Z
 
 
-def remote(src, dst, send, recv, device):
+def copy_to(src, dst, send, recv, device):
     return pltpu.make_async_remote_copy(
         src_ref=src, dst_ref=dst, send_sem=send, recv_sem=recv, device_id=device, device_id_type=MESH
     )
 
 
-def meet(devices):
+def remote(src, dst, send, recv, device):
+    return copy_to(src, dst, send, recv, device)
+
+
+class Hop:
+    def __init__(self, here, make):
+        self.here, self.make = here, make
+
+    def start(self):
+        @pl.when(self.here)
+        def _():
+            self.make().start()
+
+    def wait_send(self):
+        @pl.when(self.here)
+        def _():
+            self.make().wait_send()
+
+
+def greet(devices):
     barrier = pltpu.get_barrier_semaphore()
     for device in devices:
         pl.semaphore_signal(barrier, inc=1, device_id=device, device_id_type=MESH)
-    pl.semaphore_wait(barrier, len(devices))
+    return lambda: pl.semaphore_wait(barrier, len(devices))
 
 
 class BlkGather:
@@ -197,7 +216,7 @@
     grad_hid,
     sums,
     sum_c,
-    vec_out,
+    vec_own,
     weights,
     grads,
     pair,
@@ -205,6 +224,7 @@
     cut,
     pack_a,
     pack_b,
+    pack_vec,
     land_a,
     land_b,
     land_vec,
@@ -239,7 +259,7 @@
     go_heads,
     g_scores,
     p_low,
-    g_heads,
+    g_turned,
     g_qkv,
     gvec,
     gvec_all,
@@ -266,8 +286,14 @@
     sends = []
 
 
-    def shard_at(step, x):
-        return place.z_at(step) * GRID_X + x
+    lower = place.z < 2
+    outer = (place.z == 0) | (place.z == GRID_Z - 1)
+    targets = (
+        jnp.where(lower, 3, 0),
+        jnp.where(lower, 2, 1),
+        jnp.where(lower, 1 - place.z, 5 - place.z),
+        place.z,
+    )
 
     def start(copy):
         copy.start()
@@ -278,90 +304,121 @@
         def __init__(self, whole, index, sem_x, sem_z):
             self.whole, self.index, self.sem_x, self.sem_z = whole, index, sem_x, sem_z
 
+        def _shard(self, z, x):
+            return self.whole.at[z * GRID_X + x]
+
+        def _along(self, z, slot, to):
+            ref = self._shard(z, place.x)
+            return copy_to(
+                ref,
+                ref,
+                self.sem_z.at[0, self.index, slot],
+                self.sem_z.at[1, self.index, z],
+                place.at(to, place.x),
+            )
+
+        def _over(self, z, x):
+            ref = self._shard(z, x)
+            return copy_to(
+                ref, ref, self.sem_x.at[0, self.index, z], self.sem_x.at[1, self.index, z], partner
+            )
+
         def begin(self):
-            own = self.whole.at[place.hi]
-            self.along = []
-            for step in range(1, GRID_Z):
-                self.along.append(
-                    start(
-                        remote(
-                            own,
-                            own,
-                            self.sem_z.at[0, self.index, step - 1],
-                            self.sem_z.at[1, self.index, step - 1],
-                            place.at(place.z_at(step), place.x),
-                        )
-                    )
-                )
-            self.over = [self._over(own, 0)]
-
-        def _over(self, ref, slot):
-            return start(
-                remote(
-                    ref,
-                    ref,
-                    self.sem_x.at[0, self.index, slot],
-                    self.sem_x.at[1, self.index, slot],
-                    partner,
-                )
-            )
-
-        def pass_on(self):
-            for step in range(1, GRID_Z):
-                self.along[step - 1].wait_recv()
-                self.over.append(self._over(self.whole.at[shard_at(GRID_Z - step, place.x)], step))
+            z = place.z
+            for slot, (here, to) in enumerate(((z < GRID_Z - 1, z + 1), (z > 0, z - 1))):
+                start(Hop(here, functools.partial(self._along, z, slot, to)))
+
+        def cross(self):
+            self._over(place.z, place.x).start()
+
+        def pass_on(self, distance):
+            z = place.z
+            for sign in (1, -1):
+                source, to = z - sign * distance, z + sign
+                inside = (source >= 0) & (source < GRID_Z)
+                more = inside & (to >= 0) & (to < GRID_Z)
+
+                @pl.when(inside)
+                def _(source=source, to=to):
+                    self._along(source, GRID_X, z).wait_recv()
+
+                start(Hop(more, functools.partial(self._along, source, GRID_X + source, to)))
+
+                @pl.when(inside)
+                def _(source=source):
+                    self._over(source, place.x).start()
 
         def settle(self):
-            for copy in self.over:
-                copy.wait_recv()
+            for z in range(GRID_Z):
+                self._over(z, 1 - place.x).wait_recv()
+
+        def finish(self):
+            for z in range(GRID_Z):
+                self._over(z, place.x).wait_send()
 
     class Sum:
         def __init__(self, index):
             self.index = index
             self.grad = grads.at[index]
 
+        def _over(self, slot):
+            return copy_to(
+                self.grad.at[targets[slot] * GRID_X + 1 - place.x],
+                pair.at[self.index, slot],
+                rs_x.at[0, self.index, slot],
+                rs_x.at[1, self.index, slot],
+                partner,
+            )
+
+        def _along(self, slot, land, z):
+            return copy_to(
+                pair.at[self.index, slot],
+                line.at[self.index, land],
+                rs_z.at[0, self.index, slot],
+                rs_z.at[1, self.index, land],
+                place.at(z, place.x),
+            )
+
         def begin(self):
-            self.over = []
-            for step in (1, 2, 3, 0):
-                self.over.append(
-                    start(
-                        remote(
-                            self.grad.at[shard_at(step, 1 - place.x)],
-                            pair.at[self.index, step],
-                            rs_x.at[0, self.index, step],
-                            rs_x.at[1, self.index, step],
-                            partner,
-                        )
-                    )
-                )
+            for slot in range(GRID_Z):
+                self._over(slot).start()
 
         def pass_on(self):
-            self.along = []
-            for step in range(1, GRID_Z):
-                self.over[step - 1].wait_recv()
-                both = self.grad[shard_at(step, place.x)].astype(F32) + pair[
-                    self.index, step
-                ].astype(F32)
-                pair[self.index, step] = both.astype(BF16)
-                self.along.append(
-                    start(
-                        remote(
-                            pair.at[self.index, step],
-                            line.at[self.index, step - 1],
-                            rs_z.at[0, self.index, step - 1],
-                            rs_z.at[1, self.index, step - 1],
-                            place.at(place.z_at(step), place.x),
-                        )
-                    )
-                )
+            for slot in range(GRID_Z - 1):
+                self._over(slot).wait_recv()
+                mine = self.grad[targets[slot] * GRID_X + place.x].astype(F32)
+                pair[self.index, slot] = (mine + pair[self.index, slot].astype(F32)).astype(BF16)
+
+                def send(slot=slot):
+                    self._along(slot, slot, targets[2]).start()
+
+                if slot == 2:
+                    send()
+                else:
+                    pl.when(outer)(send)
+
+        def combine(self):
+            @pl.when(jnp.logical_not(outer))
+            def _():
+                for slot in range(2):
+                    self._along(slot, slot, place.z).wait_recv()
+                    both = pair[self.index, slot].astype(F32) + line[self.index, slot].astype(F32)
+                    pair[self.index, slot] = both.astype(BF16)
+                    self._along(slot, 3, targets[slot]).start()
+
+        def finish(self):
+            for slot in range(GRID_Z):
+                self._over(slot).wait_send()
+            for slot in range(GRID_Z - 1):
+                self._along(slot, slot, targets[2]).wait_send()
 
         def settle(self):
             index = self.index
-            self.over[3].wait_recv()
-            value = self.grad[shard_at(0, place.x)].astype(F32) + pair[index, 0].astype(F32)
-            for step in range(1, GRID_Z):
-                self.along[step - 1].wait_recv()
-                value = value + line[index, step - 1].astype(F32)
+            self._over(3).wait_recv()
+            value = self.grad[place.hi].astype(F32) + pair[index, 3].astype(F32)
+            for land in (2, 3):
+                self._along(2, land, targets[2]).wait_recv()
+                value = value + line[index, land].astype(F32)
             if index in C_CHUNKS:
                 at = (index - C_CHUNKS[0]) * HEAD_COLS
                 sum_c[:, at : at + HEAD_COLS] = value
@@ -414,7 +471,14 @@
             reduce_sem.at[1, which],
         )
 
-
+    all_met = greet(
+        [place.in_page(peer) for peer in peers]
+        + [partner]
+        + [place.at(place.z_at(step), place.x) for step in range(1, GRID_Z)]
+    )
+
+    for half, index in enumerate(C_CHUNKS):
+        weights[index, place.hi] = w_down[:, half * HEAD_COLS : (half + 1) * HEAD_COLS]
     for blk in range(BLK):
         for head in range(HEADS):
             at = blk * third + head * HEAD_DIM
@@ -426,6 +490,45 @@
             pack_a[blk, :, head * HEAD_COLS : (head + 1) * HEAD_COLS] = jnp.concatenate(
                 columns, axis=1
             )
+    chunk = [Spread(weights.at[index], index, ag_x, ag_z) for index in range(CHUNKS)]
+    chunk.append(Spread(all_vec, VEC, ag_x, ag_z))
+    all_met()
+    swap_a = swap(in_swap, 0, lambda peer: pack_a.at[peer], land_a)
+    chunk[5].begin()
+    chunk[5].cross()
+    bias_part, plain_part = w_qkv.shape[1] // (GROUP * BLK), width // (GROUP * BLK)
+    spot = place.hi * BLK + b
+
+    def home(at):
+        wide = at + spot * bias_part
+        part = (wide >= width).astype(jnp.int32) + (wide >= 2 * width).astype(jnp.int32)
+        rest = wide - part * width
+        taker = sum((rest >= third * i).astype(jnp.int32) for i in range(1, BLK))
+        rest = rest - third * taker
+        head = sum((rest >= HEAD_DIM * i).astype(jnp.int32) for i in range(1, HEADS))
+        bias_column = head * third + part * HEAD_DIM + (rest - HEAD_DIM * head)
+        plain = at - (bias_part + ff_part)
+        kind = sum((plain >= plain_part * i).astype(jnp.int32) for i in range(1, 6))
+        plain_column = spot * plain_part + (plain - plain_part * kind)
+        up_column = place.hi * ff_part + (at - bias_part)
+        is_bias, is_up = at < bias_part, at < bias_part + ff_part
+        row = jnp.where(is_bias, 0, jnp.where(is_up, 1, 2 + kind))
+        column = jnp.where(is_bias, bias_column, jnp.where(is_up, up_column, plain_column))
+        return row, column, jnp.where(is_bias, taker, jnp.where(is_up, b, -1))
+
+    held = vec.shape[1]
+    _, column, _ = home(lax.broadcasted_iota(jnp.int32, (held, 1), 0))
+    spots = lax.broadcasted_iota(jnp.int32, (held, width), 1) == column
+    spots = jnp.where(spots, 1.0, 0.0).astype(BF16)
+    row, _, taker = home(lax.broadcasted_iota(jnp.int32, (1, held), 1))
+    row_here = lax.broadcasted_iota(jnp.int32, (16, held), 0) == row
+    for blk in range(BLK):
+        taken = row_here & ((taker == blk) | (taker < 0))
+        values = jnp.where(taken, jnp.broadcast_to(vec[...].astype(F32), (16, held)), 0.0)
+        pack_vec[blk] = mm(values.astype(BF16), spots).astype(BF16)
+    swap_vec = swap(in_swap, 1, lambda peer: pack_vec.at[peer], land_vec)
+
+    for blk in range(BLK):
         pack_b[blk] = jnp.concatenate(
             [
                 w_up[:, (page * BLK + blk) * ff_part : (page * BLK + blk + 1) * ff_part]
@@ -433,26 +536,13 @@
             ],
             axis=1,
         )
+    swap_b = swap(in_swap, 2, lambda peer: pack_b.at[peer], land_b)
     all_hid[b] = hidden[...]
-    all_box[b] = box[...]
-    for half, index in enumerate(C_CHUNKS):
-        weights[index, place.hi] = w_down[:, half * HEAD_COLS : (half + 1) * HEAD_COLS]
-
-    meet(
-        [place.in_page(peer) for peer in peers]
-        + [partner]
-        + [place.at(place.z_at(step), place.x) for step in range(1, GRID_Z)]
-    )
-    chunk = [Spread(weights.at[index], index, ag_x, ag_z) for index in range(CHUNKS)]
-    chunk.append(Spread(all_vec, VEC, ag_x, ag_z))
-    swap_a = swap(in_swap, 0, lambda peer: pack_a.at[peer], land_a)
-    swap_vec = swap(in_swap, 1, lambda peer: vec.at[peer], land_vec)
+    all_box[b, 0:2, :] = box[...]
     gather_box = blk_gather(0, all_box)
     gather_hid = blk_gather(1, all_hid)
     gather_box.start()
     gather_hid.start()
-    chunk[5].begin()
-    swap_b = swap(in_swap, 2, lambda peer: pack_b.at[peer], land_b)
 
     places = lax.broadcasted_iota(jnp.int32, (256, FREQ), 0).astype(F32)
     ladder = lax.broadcasted_iota(jnp.int32, (256, FREQ), 1).astype(F32)
@@ -466,8 +556,7 @@
     joined = jnp.concatenate([land_a[blk].astype(F32) for blk in range(BLK)], axis=0).astype(BF16)
     for head in range(HEADS):
         weights[head, place.hi] = joined[:, head * HEAD_COLS : (head + 1) * HEAD_COLS]
-    chunk[0].begin()
-    land_vec[b] = vec[b]
+    land_vec[b] = pack_vec[b]
     arrive(swap_vec)
     all_vec[place.hi] = (
         land_vec[0].astype(F32)
@@ -476,10 +565,16 @@
         + land_vec[3].astype(F32)
     ).astype(BF16)
     chunk[VEC].begin()
+    chunk[VEC].cross()
+    chunk[5].pass_on(1)
+    chunk[0].begin()
+    chunk[0].cross()
+    land_b[b] = pack_b[b]
+    arrive(swap_b)
+    joined = jnp.concatenate([land_b[blk].astype(F32) for blk in range(BLK)], axis=0).astype(BF16)
+    for half, index in enumerate(B_CHUNKS):
+        weights[index, place.hi] = joined[:, half * HEAD_COLS : (half + 1) * HEAD_COLS]
     gather_box.wait_across()
-    gather_hid.wait_across()
-    chunk[1].begin()
-
     gather_box.wait_sib()
     gather_box.wait_diag()
     slots = lax.broadcasted_iota(jnp.int32, (256, tokens // BLK), 0)
@@ -492,16 +587,20 @@
             axis=0,
         ).astype(BF16)
         feats[blk * 128 : (blk + 1) * 128, :] = tmm(hot, table[...]).astype(BF16)
-    land_b[b] = pack_b[b]
-    arrive(swap_b)
-    joined = jnp.concatenate([land_b[blk].astype(F32) for blk in range(BLK)], axis=0).astype(BF16)
-    for half, index in enumerate(B_CHUNKS):
-        weights[index, place.hi] = joined[:, half * HEAD_COLS : (half + 1) * HEAD_COLS]
-    chunk[5].pass_on()
+    chunk[5].pass_on(2)
+    chunk[VEC].pass_on(1)
+    chunk[0].pass_on(1)
+    chunk[5].pass_on(3)
+    chunk[VEC].pass_on(2)
+    chunk[1].begin()
+    chunk[1].cross()
+    chunk[0].pass_on(2)
+    chunk[VEC].pass_on(3)
+    gather_hid.wait_across()
+    chunk[1].pass_on(1)
+    chunk[0].pass_on(3)
     chunk[2].begin()
-    chunk[VEC].pass_on()
-    chunk[0].pass_on()
-    chunk[3].begin()
+    chunk[2].cross()
     gather_hid.wait_sib()
     gather_hid.wait_diag()
     chunk[VEC].settle()
@@ -513,19 +612,13 @@
     rows_whole = GROUP * weights.shape[2]
     whole = weights.reshape(CHUNKS, rows_whole, HEAD_COLS)
     hid = all_hid.reshape(tokens, width)
-    usable = lax.broadcasted_iota(jnp.int32, (128, tokens), 1) < lengths[0]
+    usable = lax.broadcasted_iota(jnp.int32, (tokens, tokens), 1) < lengths[0]
 
     def head_forward(head):
         bias = vec_sum[0:1, head * 3 * HEAD_DIM : (head + 1) * 3 * HEAD_DIM]
-
-        def project(blk, carry):
-            rows = block_rows(blk)
-            low = (mm(hid[rows, :], whole[head, :, : 3 * HEAD_DIM]) + bias).astype(BF16)
-            for part in range(3):
-                qkv[3 * part + head, rows, :] = low[:, part * HEAD_DIM : (part + 1) * HEAD_DIM]
-            return carry
-
-        lax.fori_loop(0, BLK, project, 0)
+        low = (mm(hid[...], whole[head, :, : 3 * HEAD_DIM]) + bias).astype(BF16)
+        for part in range(3):
+            qkv[3 * part + head] = low[:, part * HEAD_DIM : (part + 1) * HEAD_DIM]
         relq[head] = whole[head, :, 3 * HEAD_DIM : 4 * HEAD_DIM]
         relk[head] = whole[head, :, 4 * HEAD_DIM : 5 * HEAD_DIM]
         all_out[b, :, head * HEAD_DIM : (head + 1) * HEAD_DIM] = whole[
@@ -534,7 +627,7 @@
         yield
 
         def turn(blk, carry):
-            rows = block_rows(blk)
+            rows = pl.ds(pl.multiple_of(blk * 256, 256), 256)
             cos_part = feats[rows, :SPAN].astype(F32)
             sin_part = feats[rows, SPAN:].astype(F32)
             u = mm_t(qkv[head, rows, :], relq[head])
@@ -547,26 +640,20 @@
             krel[rows, SPAN:] = (v1 * sin_part + v2 * cos_part).astype(BF16)
             return carry
 
-        lax.fori_loop(0, BLK, turn, 0)
+        lax.fori_loop(0, tokens // 256, turn, 0)
         yield
-
-        def rows_of(blk, carry):
-            rows = block_rows(blk)
-            scores = mm_t(qrel[rows, :], feats[...])
-            scores = scores + mm_t(feats[rows, :], krel[...])
-            scores = scores + mm_t(qkv[head, rows, :], qkv[3 + head])
-            masked = jnp.where(usable, scores * 0.125, -1e30)
-            raised = jnp.exp(masked - jnp.max(masked, axis=-1, keepdims=True))
-            prob = raised / jnp.sum(raised, axis=-1, keepdims=True)
-            probs[head, rows, :] = prob
-            ctx[blk, :, head * HEAD_DIM : (head + 1) * HEAD_DIM] = mm(
-                prob.astype(BF16), qkv[6 + head]
-            ).astype(BF16)
-            return carry
-
-        lax.fori_loop(0, 2, rows_of, 0)
-        yield
-        lax.fori_loop(2, BLK, rows_of, 0)
+        scores = mm_t(qrel[...], feats[...])
+        scores = scores + mm_t(feats[...], krel[...])
+        scores = scores + mm_t(qkv[head], qkv[3 + head])
+        masked = jnp.where(usable, scores * 0.125, -1e30)
+        raised = jnp.exp(masked - jnp.max(masked, axis=-1, keepdims=True))
+        prob = raised / jnp.sum(raised, axis=-1, keepdims=True)
+        probs[head] = prob
+        found = mm(prob.astype(BF16), qkv[6 + head]).astype(BF16)
+        for blk in range(BLK):
+            ctx[blk, :, head * HEAD_DIM : (head + 1) * HEAD_DIM] = found[
+                blk * 128 : (blk + 1) * 128, :
+            ]
         yield
 
     def run(generator, events):
@@ -576,27 +663,42 @@
                 event()
             at += 1
 
+    chunk[1].pass_on(2)
     chunk[0].settle()
-    run(head_forward(0), {1: (chunk[1].pass_on, chunk[4].begin)})
+
+    def later(call, *rest):
+        return functools.partial(call, *rest)
+
+    run(head_forward(0), {1: (later(chunk[2].pass_on, 1), later(chunk[1].pass_on, 3))})
+    chunk[3].begin()
+    chunk[3].cross()
+    chunk[2].pass_on(2)
     chunk[1].settle()
-    run(head_forward(1), {1: (chunk[2].pass_on, chunk[6].begin)})
+    run(
+        head_forward(1),
+        {
+            1: (later(chunk[3].pass_on, 1), later(chunk[2].pass_on, 3)),
+            2: (chunk[4].begin, chunk[4].cross, later(chunk[3].pass_on, 2)),
+        },
+    )
+    gather_out = blk_gather(2, all_out)
     chunk[2].settle()
-    gather_out = blk_gather(2, all_out)
-
-    def out_there():
-        gather_out.start()
-
-    def out_passed():
-        gather_out.wait_across()
-
     run(
         head_forward(2),
-        {0: (out_there,), 1: (chunk[3].pass_on,), 3: (out_passed, chunk[4].pass_on)},
+        {
+            0: (gather_out.start, later(chunk[4].pass_on, 1)),
+            1: (later(chunk[3].pass_on, 3), chunk[6].begin, chunk[6].cross),
+            2: (later(chunk[4].pass_on, 2),),
+        },
     )
 
     swap_ctx = swap(mid_swap, 0, lambda peer: ctx.at[peer], ctx_own)
     ctx_own[b] = ctx[b]
+    gather_out.wait_across()
     gather_out.wait_sib()
+    chunk[6].pass_on(1)
+    chunk[4].pass_on(3)
+    chunk[6].pass_on(2)
     gather_out.wait_diag()
     arrive(swap_ctx)
     own = jnp.concatenate([ctx_own[blk] for blk in range(BLK)], axis=1)
@@ -607,7 +709,7 @@
     normed_all[b] = normed.astype(BF16)
     gather_normed = blk_gather(3, normed_all)
     gather_normed.start()
-    chunk[6].pass_on()
+    chunk[6].pass_on(3)
     chunk[3].settle()
     chunk[4].settle()
     reduce_one = blk_reduce(0)
@@ -627,17 +729,17 @@
     up(b)
     gather_normed.wait_sib()
     up(place.sib)
+    gather_normed.wait_across()
+    up(place.across)
+    gather_normed.wait_diag()
+    up(place.diag)
     chunk[5].settle()
     chunk[6].settle()
-    gather_normed.wait_across()
+    parts[0, place.diag] = down(place.diag).astype(BF16)
+    reduce_one.sib_far.start()
+    parts[0, place.across] = down(place.across).astype(BF16)
     parts[0, place.sib] = down(place.sib).astype(BF16)
     reduce_one.sib_near.start()
-    up(place.across)
-    parts[0, place.across] = down(place.across).astype(BF16)
-    gather_normed.wait_diag()
-    up(place.diag)
-    parts[0, place.diag] = down(place.diag).astype(BF16)
-    reduce_one.sib_far.start()
     own_branch = down(b)
     reduce_one.send_cross()
     branch = reduce_one.total(own_branch) + vec_sum[5:6, :]
@@ -680,22 +782,24 @@
     middle_rows = g_middle.reshape(tokens, act.shape[2])
     flat_grads = grads.reshape(CHUNKS, rows_whole, HEAD_COLS)
 
-    def weight_grad(index, left, right):
+    def weight_grad(indices, left, right):
         def step(at, carry):
             cols = pl.ds(pl.multiple_of(at * 256, 256), 256)
-            flat_grads[index, cols, :] = tmm(left[:, cols], right()).astype(BF16)
+            both = tmm(left[:, cols], right[...]).astype(BF16)
+            for half, index in enumerate(indices):
+                flat_grads[index, cols, :] = both[:, half * HEAD_COLS : (half + 1) * HEAD_COLS]
             return carry
 
         lax.fori_loop(0, rows_whole // 256, step, 0)
 
     summed = [Sum(index) for index in range(CHUNKS)]
-    weight_grad(5, act_rows, lambda: branch_rows[:, :HEAD_COLS])
+    weight_grad(C_CHUNKS, act_rows, branch_rows)
     summed[5].begin()
+    summed[6].begin()
     reduce_two.send_cross()
-    weight_grad(6, act_rows, lambda: branch_rows[:, HEAD_COLS:])
-    summed[6].begin()
-    weight_grad(3, normed_rows, lambda: middle_rows[:, :HEAD_COLS])
-    weight_grad(4, normed_rows, lambda: middle_rows[:, HEAD_COLS:])
+    weight_grad(B_CHUNKS, normed_rows, middle_rows)
+    summed[3].begin()
+    summed[4].begin()
     gvec[1:2, :] = column_sum(middle_rows[...].astype(F32))
     g_normed = g_two + reduce_two.total(own_normed)
 
@@ -714,12 +818,12 @@
     gvec[4:5, :] = column_sum(g_normed)
     gvec[2:3, :] = column_sum(g_attn.astype(F32))
     summed[5].pass_on()
-    summed[3].begin()
     arrive(swap_back)
     swap_attn = swap(mid_swap, 2, lambda peer: g_attn_own.at[peer], g_attn_cols)
     g_attn_cols[b] = g_attn_own[b]
-    spread_ctx = swap(mid_swap, 3, lambda peer: ctx, ctx_all)
     ctx_all[b] = ctx[...]
+    gather_ctx = blk_gather(6, ctx_all)
+    gather_ctx.start()
 
     g_ctx_rows = g_ctx.reshape(tokens, third)
     ctx_rows = ctx.reshape(tokens, third)
@@ -727,71 +831,42 @@
     def head_backward(head):
         lanes = slice(head * HEAD_DIM, (head + 1) * HEAD_DIM)
         go_heads[...] = g_ctx_rows[:, lanes]
-
-        def query_rows(blk, carry):
-            rows = block_rows(blk)
-            go = go_heads[rows, :]
-            delta = jnp.sum(
-                go.astype(F32) * ctx_rows[rows, lanes].astype(F32), axis=-1, keepdims=True
-            )
-            prob = probs[head, rows, :]
-            p_low[rows, :] = prob.astype(BF16)
-            ds = (prob * (mm_t(go, qkv[6 + head]) - delta)).astype(BF16)
-            g_scores[rows, :] = ds
-            turned = 0.125 * mm(ds, feats[...])
-            a1, a2 = turned[:, :SPAN], turned[:, SPAN:]
-            cos_part = feats[rows, :SPAN].astype(F32)
-            sin_part = feats[rows, SPAN:].astype(F32)
-            qrel[rows, :SPAN] = (a1 * cos_part + a2 * sin_part).astype(BF16)
-            qrel[rows, SPAN:] = (a1 * sin_part - a2 * cos_part).astype(BF16)
-            gq = 0.125 * mm(ds, qkv[3 + head]) + mm(qrel[rows, :], relq[head])
-            g_heads[0, rows, :] = gq.astype(BF16)
-            return carry
-
-        lax.fori_loop(0, 2, query_rows, 0)
-        yield
-        lax.fori_loop(2, BLK, query_rows, 0)
-        yield
-
-        def key_rows(blk, carry):
-            rows = block_rows(blk)
-            ds = g_scores[:, rows]
-            turned = 0.125 * tmm(ds, feats[...])
-            b1, b2 = turned[:, :SPAN], turned[:, SPAN:]
-            cos_part = feats[rows, :SPAN].astype(F32)
-            sin_part = feats[rows, SPAN:].astype(F32)
-            krel[rows, :SPAN] = (b1 * cos_part + b2 * sin_part).astype(BF16)
-            krel[rows, SPAN:] = (b2 * cos_part - b1 * sin_part).astype(BF16)
-            gk = 0.125 * tmm(ds, qkv[head]) + mm(krel[rows, :], relk[head])
-            g_heads[1, rows, :] = gk.astype(BF16)
-            g_heads[2, rows, :] = tmm(p_low[:, rows], go_heads[...]).astype(BF16)
-            return carry
-
-        lax.fori_loop(0, 2, key_rows, 0)
-        yield
-        lax.fori_loop(2, BLK, key_rows, 0)
-        yield
-        g_qkv[head] = jnp.concatenate([g_heads[part] for part in range(3)], axis=1)
+        go = go_heads[...]
+        delta = jnp.sum(
+            go.astype(F32) * ctx_rows[:, lanes].astype(F32), axis=-1, keepdims=True
+        )
+        prob = probs[head]
+        p_low[...] = prob.astype(BF16)
+        g_scores[...] = (prob * (mm_t(go, qkv[6 + head]) - delta)).astype(BF16)
+        cos_part = feats[:, :SPAN].astype(F32)
+        sin_part = feats[:, SPAN:].astype(F32)
+        turned = 0.125 * mm(g_scores[...], feats[...])
+        a1, a2 = turned[:, :SPAN], turned[:, SPAN:]
+        g_turned[0, head, :, :SPAN] = (a1 * cos_part + a2 * sin_part).astype(BF16)
+        g_turned[0, head, :, SPAN:] = (a1 * sin_part - a2 * cos_part).astype(BF16)
+        gq = 0.125 * mm(g_scores[...], qkv[3 + head]) + mm(g_turned[0, head], relq[head])
+        turned = 0.125 * tmm(g_scores[...], feats[...])
+        b1, b2 = turned[:, :SPAN], turned[:, SPAN:]
+        g_turned[1, head, :, :SPAN] = (b1 * cos_part + b2 * sin_part).astype(BF16)
+        g_turned[1, head, :, SPAN:] = (b2 * cos_part - b1 * sin_part).astype(BF16)
+        gk = 0.125 * tmm(g_scores[...], qkv[head]) + mm(g_turned[1, head], relk[head])
+        g_value = tmm(p_low[...], go)
+        g_qkv[head] = jnp.concatenate([gq, gk, g_value], axis=1).astype(BF16)
         gvec[0:1, head * third : (head + 1) * third] = column_sum(g_qkv[head].astype(F32))
 
-        def chunk_rows(at, carry):
-            cols = pl.ds(pl.multiple_of(at * 256, 256), 256)
+    def head_grads(head):
+        lanes = slice(head * HEAD_DIM, (head + 1) * HEAD_DIM)
+        for at in range(rows_whole // 256):
+            cols = slice(at * 256, (at + 1) * 256)
             flat_grads[head, cols, :] = jnp.concatenate(
                 [
                     tmm(hid[:, cols], g_qkv[head]),
-                    tmm(qrel[:, cols], qkv[head]),
-                    tmm(krel[:, cols], qkv[3 + head]),
-                    tmm(
-                        ctx_flat(at), g_attn_cols_rows[:, lanes]
-                    ),
+                    tmm(g_turned[0, head, :, cols], qkv[head]),
+                    tmm(g_turned[1, head, :, cols], qkv[3 + head]),
+                    tmm(ctx_flat(at), g_attn_cols_rows[:, lanes]),
                 ],
                 axis=1,
             ).astype(BF16)
-            return carry
-
-        for at in range(rows_whole // 256):
-            chunk_rows(at, 0)
-        yield
 
     g_attn_cols_rows = g_attn_cols.reshape(tokens, third)
 
@@ -808,44 +883,37 @@
             start_col = stop
         return jnp.concatenate(pieces, axis=1)
 
-    def cross_there():
-        arrive(swap_attn)
-        arrive(spread_ctx)
-
     finals = []
 
     def settle(index):
-        def done():
-            finals.extend(summed[index].settle())
-
-        return done
+        finals.extend(summed[index].settle())
 
     gvec[0:1, 3 * third :] = jnp.zeros((1, width - 3 * third), F32)
-    run(
-        head_backward(0),
-        {
-            1: (summed[6].pass_on, summed[4].begin),
-            3: (cross_there,),
-            4: (summed[3].pass_on, settle(5), summed[0].begin),
-        },
-    )
-    run(
-        head_backward(1),
-        {
-            2: (summed[4].pass_on, settle(6)),
-            4: (summed[1].begin,),
-        },
-    )
-    run(
-        head_backward(2),
-        {
-            1: (summed[0].pass_on, settle(3)),
-            4: (summed[2].begin,),
-        },
-    )
+    head_backward(0)
+    summed[5].combine()
+    head_backward(1)
+    gather_ctx.wait_across()
+    summed[6].pass_on()
+    head_backward(2)
     gvec_all[place.hi] = gvec[...].astype(BF16)
     vec_back = Spread(gvec_all, VEC, rs_x, rs_z)
     vec_back.begin()
+    vec_back.cross()
+    arrive(swap_attn)
+    gather_ctx.wait_sib()
+    gather_ctx.wait_diag()
+    head_grads(0)
+    summed[0].begin()
+    summed[6].combine()
+    vec_back.pass_on(1)
+    head_grads(1)
+    summed[1].begin()
+    vec_back.pass_on(2)
+    summed[3].pass_on()
+    head_grads(2)
+    summed[2].begin()
+    vec_back.pass_on(3)
+    settle(5)
     reduce_hid = blk_reduce(2)
 
     def part_hid(blk):
@@ -861,9 +929,14 @@
     parts[2, place.sib] = part_hid(place.sib).astype(BF16)
     reduce_hid.sib_near.start()
     own_hid = part_hid(b) + g_one
-    settle(4)()
-    summed[1].pass_on()
-    vec_back.pass_on()
+    summed[3].combine()
+    settle(6)
+    summed[4].pass_on()
+    grad_hid[...] = reduce_hid.total(own_hid).astype(BF16)
+    settle(3)
+    summed[4].combine()
+    summed[0].pass_on()
+    settle(4)
     vec_back.settle()
     total = gvec_all[0].astype(F32)
     for shard in range(1, GROUP):
@@ -871,22 +944,105 @@
     gvec_page[b] = total
     gather_vec = blk_gather(5, gvec_page)
     gather_vec.start()
-    grad_hid[...] = reduce_hid.total(own_hid).astype(BF16)
+    summed[0].combine()
+    summed[1].pass_on()
     gather_vec.wait_across()
-    settle(0)()
-    summed[2].pass_on()
-    settle(1)()
     gather_vec.wait_sib()
     gather_vec.wait_diag()
-    vec_out[...] = gvec_page[...]
-    settle(2)()
+
+    _, column, taker = home(lax.broadcasted_iota(jnp.int32, (1, held), 1))
+    places = lax.broadcasted_iota(jnp.int32, (width, held), 0) == column
+    places = jnp.where(places, 1.0, 0.0)
+    plain = gvec_page[0] + gvec_page[1] + gvec_page[2] + gvec_page[3]
+    plain_row = lax.broadcasted_iota(jnp.int32, (16, width), 0)
+    plain = jnp.where(plain_row < 2, 0.0, plain)
+    bias_all = jnp.concatenate([gvec_page[blk][0:1, :] for blk in range(BLK)], axis=0)
+    stacked = jnp.concatenate([plain, bias_all, gvec_page[b][1:2, :], bias_all[0:3, :]], axis=0)
+    picked = jnp.dot(stacked, places, preferred_element_type=F32, precision=lax.Precision.HIGHEST)
+    own_bias = jnp.zeros((1, held), F32)
+    for blk in range(BLK):
+        own_bias = own_bias + jnp.where(taker == blk, picked[16 + blk : 17 + blk, :], 0.0)
+    vec_own[...] = jnp.concatenate([own_bias, picked[20:21, :], picked[2:8, :]], axis=0)
+
+    settle(0)
+    summed[1].combine()
+    summed[2].pass_on()
+    settle(1)
+    summed[2].combine()
+    settle(2)
     arrive(finals)
+    for part in chunk + summed + [vec_back]:
+        part.finish()
     for copy in sends:
         copy.wait_send()
     for reduce in (reduce_one, reduce_two, reduce_hid):
         reduce.finish()
-    for gather in (gather_box, gather_hid, gather_out, gather_normed, gather_branch, gather_vec):
+    for gather in (gather_box, gather_hid, gather_out, gather_normed, gather_branch, gather_ctx, gather_vec):
         gather.finish()
+
+
+def finish_kernel(
+    out_in,
+    hid_in,
+    sums,
+    sum_c,
+    vec,
+    out,
+    grad_hid,
+    g_qkv,
+    g_bias,
+    g_relq,
+    g_relk,
+    g_out,
+    g_out_bias,
+    g_gain_one,
+    g_shift_one,
+    g_up,
+    g_up_bias,
+    g_down,
+    g_down_bias,
+    g_gain_two,
+    g_shift_two,
+):
+    out[...] = out_in[...]
+    grad_hid[...] = hid_in[...]
+    g_down[...] = sum_c[...]
+    width = sum_c.shape[1]
+    pieces = [
+        [sums[head, blk].astype(F32) for blk in range(BLK)] for head in range(HEADS)
+    ]
+
+    def gathered(part):
+        lanes = slice(part * HEAD_DIM, (part + 1) * HEAD_DIM)
+        return jnp.concatenate(
+            [pieces[head][blk][:, lanes] for blk in range(BLK) for head in range(HEADS)], axis=1
+        )
+
+    for part in range(3):
+        g_qkv[:, part * width : (part + 1) * width] = gathered(part)
+    g_relq[...] = gathered(3)
+    g_relk[...] = gathered(4)
+    g_out[...] = gathered(5)
+    per_chunk = GROUP // len(B_CHUNKS)
+    part = HEAD_COLS // per_chunk
+    for half, index in enumerate(B_CHUNKS):
+        wide = [sums[index, blk].astype(F32) for blk in range(BLK)]
+        columns = jnp.concatenate(
+            [
+                wide[blk][:, page * part : (page + 1) * part]
+                for page in range(per_chunk)
+                for blk in range(BLK)
+            ],
+            axis=1,
+        )
+        g_up[:, half * columns.shape[1] : (half + 1) * columns.shape[1]] = columns
+    for row, target in enumerate(
+        (g_bias, g_up_bias, g_out_bias, g_gain_one, g_shift_one, g_down_bias, g_gain_two, g_shift_two)
+    ):
+        first = 0 if row == 0 else g_bias.shape[1]
+        if row > 1:
+            first = first + g_up_bias.shape[1] + (row - 2) * target.shape[1]
+        target[...] = vec[row : row + 1, first : first + target.shape[1]]
 
 
 def on_device(
@@ -945,26 +1101,9 @@
     shard = BLK * rows
     ff_part = w_up.shape[1] // (GROUP * BLK)
 
-    here = (lax.iota(jnp.int32, GROUP * BLK) == hi * BLK + b).astype(BF16)
-    spot = here[:, None]
-    own_bias = (spot * b_qkv[None, :]).reshape(3, BLK, HEADS, HEAD_DIM).transpose(1, 2, 0, 3)
-    own_bias = own_bias.reshape(BLK, 3 * third)
-    own_bias = jnp.pad(own_bias, ((0, 0), (0, width - 3 * third)))
-    up_spot = (spot * b_up[None, :]).reshape(GROUP, BLK, ff_part).transpose(1, 0, 2)
-    up_spot = up_spot.reshape(BLK, GROUP * ff_part)
-    plain = jnp.stack([b_out, ln1_gain, ln1_bias, b_down, ln2_gain, ln2_bias])
-    plain = (spot[None] * plain[:, None, :]).reshape(6, width)
-    vec = jnp.concatenate(
-        [
-            own_bias[:, None, :],
-            up_spot[:, None, :],
-            jnp.broadcast_to(plain[None], (BLK, 6, width)),
-            jnp.zeros((BLK, 8, width), BF16),
-        ],
-        axis=1,
-    )
-    box = jnp.pad(boxes[0].T, ((0, 6), (0, 0)))
-
+    vec = jnp.concatenate([b_qkv, b_up, b_out, ln1_gain, ln1_bias, b_down, ln2_gain, ln2_bias])
+    vec = jnp.pad(vec, (0, 384 - vec.shape[0]))[None]
+    box = boxes[0].T
     tokens = BLK * tok
     sem = pltpu.SemaphoreType.DMA
 
@@ -976,16 +1115,17 @@
         ((tok, width), BF16),
         ((5, BLK, rows, HEAD_COLS), BF16),
         ((shard, width), F32),
-        ((BLK, 16, width), F32),
+        ((8, 384), F32),
     ]
     scratch = dict(
         weights=held(CHUNKS, GROUP, shard, HEAD_COLS),
         grads=held(CHUNKS, GROUP, shard, HEAD_COLS),
         pair=held(CHUNKS, GRID_Z, shard, HEAD_COLS),
-        line=held(CHUNKS, GRID_Z - 1, shard, HEAD_COLS),
+        line=held(CHUNKS, GRID_Z, shard, HEAD_COLS),
         cut=held(5, BLK, rows, HEAD_COLS),
         pack_a=held(BLK, rows, 3 * HEAD_COLS),
         pack_b=held(BLK, rows, GROUP * ff_part),
+        pack_vec=held(BLK, 16, width),
         land_a=held(BLK, rows, 3 * HEAD_COLS),
         land_b=held(BLK, rows, GROUP * ff_part),
         land_vec=held(BLK, 16, width),
@@ -1020,22 +1160,22 @@
         go_heads=held(tokens, HEAD_DIM),
         g_scores=held(tokens, tokens),
         p_low=held(tokens, tokens),
-        g_heads=held(3, tokens, HEAD_DIM),
+        g_turned=held(2, HEADS, tokens, width),
         g_qkv=held(3, tokens, third),
         gvec=held(16, width, kind=F32),
         gvec_all=held(GROUP, 16, width),
         gvec_page=held(BLK, 16, width, kind=F32),
         ag_x=sem((2, CHUNKS + 1, 4)),
-        ag_z=sem((2, CHUNKS + 1, 3)),
+        ag_z=sem((2, CHUNKS + 1, 6)),
         rs_x=sem((2, CHUNKS + 1, 4)),
-        rs_z=sem((2, CHUNKS + 1, 3)),
+        rs_z=sem((2, CHUNKS + 1, 6)),
         in_swap=sem((2, 3, 3)),
-        gather_sem=sem((2, 6, 3)),
+        gather_sem=sem((2, 7, 3)),
         reduce_sem=sem((2, 3, 3)),
-        mid_swap=sem((2, 4, 3)),
+        mid_swap=sem((2, 3, 3)),
         out_swap=sem((2, 5, 3)),
     )
-    out, grad_hid, sums, sum_c, vec_out = vmem_call(
+    out, grad_hid, sums, sum_c, vec_own = vmem_call(
         functools.partial(layer_kernel, spread),
         outs,
         list(scratch.values()),
@@ -1056,53 +1196,33 @@
         vec,
     )
 
-    heads = sums[:HEADS].reshape(HEADS, BLK, rows, 6, HEAD_DIM)
-
-    def columns(part):
-        return heads[:, :, :, part].transpose(2, 1, 0, 3).reshape(rows, BLK * third).astype(F32)
-
-    grad_qkv = heads[:, :, :, :3].transpose(2, 3, 1, 0, 4).reshape(rows, 3 * BLK * third)
-    grad_qkv = grad_qkv.astype(F32)
-    grad_relq, grad_relk, grad_w_out = columns(3), columns(4), columns(5)
-    grad_up = sums[HEADS:].reshape(2, BLK, rows, GROUP // 2, ff_part).transpose(2, 0, 3, 1, 4)
-    grad_up = grad_up.reshape(rows, GROUP * BLK * ff_part).astype(F32)
-
-    place = lax.axis_index("pages") * BLK + b
-    if spread > 1:
-        vec_out = lax.psum(vec_out, "pages", axis_index_groups=groups)
-    summed = jnp.sum(vec_out[:, 2:8], axis=0)
-    bias_all = vec_out[:, 0, : 3 * third].reshape(BLK, HEADS, 3, HEAD_DIM).transpose(2, 0, 1, 3)
-    up_all = vec_out[:, 1].reshape(BLK, GROUP, ff_part).transpose(1, 0, 2)
-    count = page_count * BLK
-    whole = jnp.concatenate(
-        [bias_all.reshape(count, -1), up_all.reshape(count, -1)]
-        + [summed[row].reshape(count, -1) for row in range(6)],
-        axis=1,
-    )
-    vectors = lax.dynamic_slice_in_dim(whole, place, 1, 0)[0]
-    sizes = [3 * BLK * third // count, GROUP * BLK * ff_part // count] + [width // count] * 6
-    cuts = [sum(sizes[:at]) for at in range(len(sizes) + 1)]
-    g_bias, g_up, g_out, g_gain1, g_shift1, g_down, g_gain2, g_shift2 = [
-        vectors[cuts[at] : cuts[at + 1]] for at in range(8)
-    ]
-    return (
-        out[None],
-        grad_hid[None],
-        shrink(grad_qkv),
-        g_bias,
-        shrink(grad_relq),
-        shrink(grad_relk),
-        shrink(grad_w_out),
-        g_out,
-        g_gain1,
-        g_shift1,
-        shrink(grad_up),
-        g_up,
-        shrink(sum_c),
-        g_down,
-        g_gain2,
-        g_shift2,
-    )
+    square = ((rows, BLK * third), F32)
+    plain = ((1, rows), F32)
+    results = vmem_call(
+        finish_kernel,
+        [
+            ((tok, width), BF16),
+            ((tok, width), BF16),
+            ((rows, 3 * BLK * third), F32),
+            ((1, 3 * rows), F32),
+            square,
+            square,
+            square,
+            plain,
+            plain,
+            plain,
+            ((rows, GROUP * BLK * ff_part), F32),
+            ((1, ff_part), F32),
+            ((shard, width), F32),
+            plain,
+            plain,
+            plain,
+        ],
+        [],
+        "finish",
+    )(out, grad_hid, sums, sum_c, vec_own)
+    flat = [part[0] if part.shape[0] == 1 else part for part in results[2:]]
+    return (results[0][None], results[1][None]) + tuple(shrink(part) for part in flat)
 
 
 def solution(mesh):

time: 191 us -> 159 us (0.83)
  local copies, waits for them, and re-layouts: 17.3 us -> 1.38 us
  Pallas kernels: 169 us -> 156 us
  other arithmetic: 2.33 us -> 0 us
    pallas_call x1 -> x2, Pallas kernels: 169 us -> 156 us  [run(): pl.pallas_call(kernel, name=name, out_shape=[jax.ShapeDtypeStruct(shape,...]
    convert_element_type x11 -> x0, local copies, waits for them, and re-layouts: 5.65 us -> none  [the longest x6 2.72 us: columns(): heads[:, :, :, part].transpose(2, 1, 0, 3).reshape(rows, BLK * third)]
    unnamed x29 -> x16, local copies, waits for them, and re-layouts: 5.32 us -> 0.7 us
    slice x7 -> x0, local copies, waits for them, and re-layouts: 3.66 us -> none  [the longest x3 1.72 us: on_device(): vectors[cuts[at]:cuts[at + 1]]]
where the time goes in v3:
time: 159 us
  Pallas kernels  156 us (98%)
    pallas_call x2, Pallas kernels, run(): pl.pallas_call(kernel, name=name, out_shape=[jax.ShapeDtypeStruct(shape,...  156 us

profile of v3, /device:TPU:0, one launch (start us, length us, event | category | flops | bytes accessed | tf_op | source)
XLA Modules:
  0.0 158.7 jit_solution(14031952589307363495)
XLA Ops:
  1.3 0.0 copy-start.7
  1.3 0.0 copy-start.3
  1.3 0.0 copy-start.4
  1.3 0.0 copy-start.5
  1.3 0.0 copy-start.6
  1.3 0.0 copy-start
  1.4 0.0 copy-start.1
  1.4 0.0 copy-start.2
  1.4 0.6 copy-done.7
  2.0 0.0 copy-done.3
  2.0 0.0 copy-done.4
  2.0 0.0 copy-done.5
  2.0 0.0 copy-done.6
  2.0 0.0 copy-done
  2.0 0.0 copy-done.1
  2.0 0.0 copy-done.2
  2.1 0.1 concatenate.3
  2.2 0.6 broadcast_in_dim.9.vec
  2.7 153.2 %layer.1 = (bf16[128,768]{1,0:T(8,128)(2,1)}, bf16[128,768]{1,0:T(8,128)(2,1)}, bf16[5,4,24,384]{3,2,1,0:T(8,128)(2,1)}, f32[96,768]{1,0:T(8,128)}, f32[8,384]{1,0:T(8,128)}) custom-call(s32[1]{0:T(128)S(6)} %copy.34.lengths, bf16[24,2304]{1,0:T(8,128)(2,1)} %w_qkv.1, bf16[24,768]{1,0:T(8,128)(2,1)} %w_relq.1, bf16[24,768]{1,0:T(8,128)(2,1)} %w_relk.1, ...), custom_call_target="tpu_custom_call" | custom-call | tf_op jit(solution)/shard_map/layer/pallas_call | solution.py:157
  155.9 2.5 %finish.1 = (bf16[128,768]{1,0:T(8,128)(2,1)}, bf16[128,768]{1,0:T(8,128)(2,1)}, f32[24,2304]{1,0:T(8,128)}, f32[1,72]{1,0:T(1,128)}, f32[24,768]{1,0:T(8,128)},...) custom-call(bf16[128,768]{1,0:T(8,128)(2,1)} %get-tuple-element.37.o, ...), custom_call_target="tpu_custom_call" | custom-call | tf_op jit(solution)/shard_map/finish/pallas_call | solution.py:157
  (1 shorter events, 0.0 us)
Async XLA Ops:
  1.3 0.7 copy-start.7
  1.3 0.7 copy-start.3
  1.3 0.7 copy-start.4
  1.3 0.7 copy-start.5
  1.3 0.7 copy-start.6
  1.3 0.7 copy-start
  1.4 0.7 copy-start.1
  1.4 0.7 copy-start.2

commit v4 on v3

--- a/solution.py
+++ b/solution.py
@@ -221,6 +221,7 @@
     grads,
     pair,
     line,
+    beside,
     cut,
     pack_a,
     pack_b,
@@ -231,7 +232,8 @@
     all_vec,
     all_hid,
     all_box,
-    all_out,
+    all_out_a,
+    all_out_b,
     vec_sum,
     table,
     feats,
@@ -294,6 +296,7 @@
         jnp.where(lower, 1 - place.z, 5 - place.z),
         place.z,
     )
+    mate = targets[2]
 
     def start(copy):
         copy.start()
@@ -303,9 +306,13 @@
     class Spread:
         def __init__(self, whole, index, sem_x, sem_z):
             self.whole, self.index, self.sem_x, self.sem_z = whole, index, sem_x, sem_z
-
-        def _shard(self, z, x):
-            return self.whole.at[z * GRID_X + x]
+            self.halved = index != VEC
+
+        def _shard(self, z, x, part=None):
+            if part is None or not self.halved:
+                return self.whole.at[z * GRID_X + x]
+            rows = self.whole.shape[1] // 2
+            return self.whole.at[z * GRID_X + x, part * rows : (part + 1) * rows]
 
         def _along(self, z, slot, to):
             ref = self._shard(z, place.x)
@@ -317,11 +324,26 @@
                 place.at(to, place.x),
             )
 
-        def _over(self, z, x):
-            ref = self._shard(z, x)
+        def _over(self, z, x, part=None):
+            ref = self._shard(z, x, part)
             return copy_to(
                 ref, ref, self.sem_x.at[0, self.index, z], self.sem_x.at[1, self.index, z], partner
             )
+
+        def _beside(self):
+            ref = self._shard(place.z, 1 - place.x, 1)
+            return copy_to(
+                ref,
+                ref,
+                self.sem_z.at[0, self.index, GRID_X + place.z],
+                self.sem_z.at[1, self.index, GRID_Z],
+                place.at(mate, place.x),
+            )
+
+        def relay(self):
+            self._over(place.z, 1 - place.x).wait_recv()
+            if self.halved:
+                self._beside().start()
 
         def begin(self):
             z = place.z
@@ -344,17 +366,37 @@
 
                 start(Hop(more, functools.partial(self._along, source, GRID_X + source, to)))
 
-                @pl.when(inside)
-                def _(source=source):
-                    self._over(source, place.x).start()
+                if distance > 1:
+
+                    @pl.when(inside)
+                    def _(source=source):
+                        self._over(source, place.x).start()
+
+                else:
+
+                    @pl.when(inside & (source == mate))
+                    def _(source=source):
+                        self._over(source, place.x, 0).start()
+
+                    @pl.when(inside & (source != mate))
+                    def _(source=source):
+                        self._over(source, place.x).start()
 
         def settle(self):
-            for z in range(GRID_Z):
-                self._over(z, 1 - place.x).wait_recv()
+            for slot in range(2):
+                self._over(targets[slot], 1 - place.x).wait_recv()
+            self._over(mate, 1 - place.x, 0).wait_recv()
+            if self.halved:
+                self._beside().wait_recv()
 
         def finish(self):
-            for z in range(GRID_Z):
-                self._over(z, place.x).wait_send()
+            for slot in (0, 1, 3):
+                self._over(targets[slot], place.x).wait_send()
+            self._over(mate, place.x, 0).wait_send()
+            if self.halved:
+                self._beside().wait_send()
+
+    half_rows = grads.shape[2] // 2
 
     class Sum:
         def __init__(self, index):
@@ -362,12 +404,22 @@
             self.grad = grads.at[index]
 
         def _over(self, slot):
+            shard = targets[min(slot, 3)] * GRID_X + 1 - place.x
+            src, dst = self.grad.at[shard], pair.at[self.index, min(slot, 3)]
+            if slot >= 9:
+                rows = slice(half_rows, None) if slot == 4 else slice(0, half_rows)
+                src, dst = src.at[rows], dst.at[rows]
             return copy_to(
-                self.grad.at[targets[slot] * GRID_X + 1 - place.x],
-                pair.at[self.index, slot],
-                rs_x.at[0, self.index, slot],
-                rs_x.at[1, self.index, slot],
-                partner,
+                src, dst, rs_x.at[0, self.index, slot], rs_x.at[1, self.index, slot], partner
+            )
+
+        def _beside(self):
+            return copy_to(
+                self.grad.at[mate * GRID_X + 1 - place.x, half_rows:],
+                beside.at[self.index],
+                rs_z.at[0, self.index, 3],
+                rs_z.at[1, self.index, 4],
+                place.at(mate, place.x),
             )
 
         def _along(self, slot, land, z):
@@ -383,11 +435,22 @@
             for slot in range(GRID_Z):
                 self._over(slot).start()
 
+        def relay(self):
+            return
+
+
         def pass_on(self):
             for slot in range(GRID_Z - 1):
                 self._over(slot).wait_recv()
-                mine = self.grad[targets[slot] * GRID_X + place.x].astype(F32)
-                pair[self.index, slot] = (mine + pair[self.index, slot].astype(F32)).astype(BF16)
+                shard = targets[slot] * GRID_X + place.x
+                if slot < 9:
+                    both = self.grad[shard].astype(F32) + pair[self.index, slot].astype(F32)
+                    pair[self.index, slot] = both.astype(BF16)
+                else:
+                    mine = self.grad[shard, :half_rows].astype(F32)
+                    both = mine + pair[self.index, slot, :half_rows].astype(F32)
+                    pair[self.index, slot, :half_rows] = both.astype(BF16)
+                    pair[self.index, slot, half_rows:] = self.grad[shard, half_rows:]
 
                 def send(slot=slot):
                     self._along(slot, slot, targets[2]).start()
@@ -556,6 +619,8 @@
     joined = jnp.concatenate([land_a[blk].astype(F32) for blk in range(BLK)], axis=0).astype(BF16)
     for head in range(HEADS):
         weights[head, place.hi] = joined[:, head * HEAD_COLS : (head + 1) * HEAD_COLS]
+    chunk[0].begin()
+    chunk[0].cross()
     land_vec[b] = pack_vec[b]
     arrive(swap_vec)
     all_vec[place.hi] = (
@@ -567,14 +632,19 @@
     chunk[VEC].begin()
     chunk[VEC].cross()
     chunk[5].pass_on(1)
-    chunk[0].begin()
-    chunk[0].cross()
     land_b[b] = pack_b[b]
     arrive(swap_b)
     joined = jnp.concatenate([land_b[blk].astype(F32) for blk in range(BLK)], axis=0).astype(BF16)
     for half, index in enumerate(B_CHUNKS):
         weights[index, place.hi] = joined[:, half * HEAD_COLS : (half + 1) * HEAD_COLS]
+    chunk[5].relay()
+    chunk[5].pass_on(2)
+    chunk[0].pass_on(1)
+    chunk[1].begin()
+    chunk[1].cross()
     gather_box.wait_across()
+    gather_hid.wait_across()
+    chunk[VEC].pass_on(1)
     gather_box.wait_sib()
     gather_box.wait_diag()
     slots = lax.broadcasted_iota(jnp.int32, (256, tokens // BLK), 0)
@@ -587,22 +657,20 @@
             axis=0,
         ).astype(BF16)
         feats[blk * 128 : (blk + 1) * 128, :] = tmm(hot, table[...]).astype(BF16)
-    chunk[5].pass_on(2)
-    chunk[VEC].pass_on(1)
-    chunk[0].pass_on(1)
     chunk[5].pass_on(3)
+    chunk[0].relay()
+    chunk[0].pass_on(2)
+    chunk[VEC].relay()
     chunk[VEC].pass_on(2)
-    chunk[1].begin()
-    chunk[1].cross()
-    chunk[0].pass_on(2)
-    chunk[VEC].pass_on(3)
-    gather_hid.wait_across()
     chunk[1].pass_on(1)
-    chunk[0].pass_on(3)
     chunk[2].begin()
     chunk[2].cross()
+    chunk[0].pass_on(3)
+    chunk[VEC].pass_on(3)
     gather_hid.wait_sib()
     gather_hid.wait_diag()
+    chunk[1].relay()
+    chunk[1].pass_on(2)
     chunk[VEC].settle()
     total = all_vec[0].astype(F32)
     for shard in range(1, GROUP):
@@ -614,16 +682,23 @@
     hid = all_hid.reshape(tokens, width)
     usable = lax.broadcasted_iota(jnp.int32, (tokens, tokens), 1) < lengths[0]
 
+    gather_out = [blk_gather(2, all_out_a), blk_gather(7, all_out_b)]
+
     def head_forward(head):
+        out_part = whole[head, :, 5 * HEAD_DIM : 6 * HEAD_DIM]
+        if head == 2:
+            all_out_b[b] = out_part
+            gather_out[1].start()
+        else:
+            all_out_a[b, :, head * HEAD_DIM : (head + 1) * HEAD_DIM] = out_part
+        if head == 1:
+            gather_out[0].start()
         bias = vec_sum[0:1, head * 3 * HEAD_DIM : (head + 1) * 3 * HEAD_DIM]
         low = (mm(hid[...], whole[head, :, : 3 * HEAD_DIM]) + bias).astype(BF16)
         for part in range(3):
             qkv[3 * part + head] = low[:, part * HEAD_DIM : (part + 1) * HEAD_DIM]
         relq[head] = whole[head, :, 3 * HEAD_DIM : 4 * HEAD_DIM]
         relk[head] = whole[head, :, 4 * HEAD_DIM : 5 * HEAD_DIM]
-        all_out[b, :, head * HEAD_DIM : (head + 1) * HEAD_DIM] = whole[
-            head, :, 5 * HEAD_DIM : 6 * HEAD_DIM
-        ]
         yield
 
         def turn(blk, carry):
@@ -663,53 +738,63 @@
                 event()
             at += 1
 
-    chunk[1].pass_on(2)
+    chunk[2].pass_on(1)
+    chunk[3].begin()
+    chunk[3].cross()
     chunk[0].settle()
 
     def later(call, *rest):
         return functools.partial(call, *rest)
 
-    run(head_forward(0), {1: (later(chunk[2].pass_on, 1), later(chunk[1].pass_on, 3))})
-    chunk[3].begin()
-    chunk[3].cross()
+    run(head_forward(0), {0: (later(chunk[1].pass_on, 3),)})
+    chunk[2].relay()
     chunk[2].pass_on(2)
     chunk[1].settle()
     run(
         head_forward(1),
         {
-            1: (later(chunk[3].pass_on, 1), later(chunk[2].pass_on, 3)),
-            2: (chunk[4].begin, chunk[4].cross, later(chunk[3].pass_on, 2)),
+            0: (later(chunk[3].pass_on, 1), chunk[4].begin, chunk[4].cross),
+            1: (later(chunk[2].pass_on, 3),),
         },
     )
-    gather_out = blk_gather(2, all_out)
+    chunk[3].relay()
+    chunk[3].pass_on(2)
+    chunk[4].pass_on(1)
+    chunk[6].begin()
+    chunk[6].cross()
     chunk[2].settle()
     run(
         head_forward(2),
         {
-            0: (gather_out.start, later(chunk[4].pass_on, 1)),
-            1: (later(chunk[3].pass_on, 3), chunk[6].begin, chunk[6].cross),
-            2: (later(chunk[4].pass_on, 2),),
+            0: (gather_out[0].wait_across,),
+            1: (later(chunk[3].pass_on, 3),),
         },
     )
 
     swap_ctx = swap(mid_swap, 0, lambda peer: ctx.at[peer], ctx_own)
     ctx_own[b] = ctx[b]
-    gather_out.wait_across()
-    gather_out.wait_sib()
+    chunk[4].relay()
+    chunk[4].pass_on(2)
     chunk[6].pass_on(1)
-    chunk[4].pass_on(3)
-    chunk[6].pass_on(2)
-    gather_out.wait_diag()
+    gather_out[1].wait_across()
+    for gather in gather_out:
+        gather.wait_sib()
+        gather.wait_diag()
     arrive(swap_ctx)
     own = jnp.concatenate([ctx_own[blk] for blk in range(BLK)], axis=1)
-    attn = jnp.concatenate([mm(own, all_out[blk]) for blk in range(BLK)], axis=1) + vec_sum[2:3, :]
+    attn = jnp.concatenate(
+        [mm(own, part[blk]) for blk in range(BLK) for part in (all_out_a, all_out_b)], axis=1
+    )
+    attn = attn + vec_sum[2:3, :]
     hat_one, scale_one = centred(hidden[...].astype(F32) + attn)
     gain_one = vec_sum[3:4, :]
     normed = hat_one * gain_one + vec_sum[4:5, :]
     normed_all[b] = normed.astype(BF16)
     gather_normed = blk_gather(3, normed_all)
     gather_normed.start()
-    chunk[6].pass_on(3)
+    chunk[4].pass_on(3)
+    chunk[6].relay()
+    chunk[6].pass_on(2)
     chunk[3].settle()
     chunk[4].settle()
     reduce_one = blk_reduce(0)
@@ -727,6 +812,7 @@
         return jnp.concatenate([mm(act[blk], whole[index]) for index in C_CHUNKS], axis=1)
 
     up(b)
+    chunk[6].pass_on(3)
     gather_normed.wait_sib()
     up(place.sib)
     gather_normed.wait_across()
@@ -801,15 +887,18 @@
     summed[3].begin()
     summed[4].begin()
     gvec[1:2, :] = column_sum(middle_rows[...].astype(F32))
+    for index in (5, 6, 3, 4):
+        summed[index].relay()
     g_normed = g_two + reduce_two.total(own_normed)
 
     g_one = norm_back(g_normed * gain_one, hat_one, scale_one)
     g_attn = g_one.astype(BF16)
     for blk in range(BLK):
         g_attn_own[blk] = g_attn[:, blk * third : (blk + 1) * third]
-    wide = mm_t(g_attn_own[0], all_out[0])
-    for blk in range(1, BLK):
-        wide = wide + mm_t(g_attn_own[blk], all_out[blk])
+    wide = jnp.zeros(g_one.shape, F32)
+    for blk in range(BLK):
+        wide = wide + mm_t(g_attn_own[blk, :, : 2 * HEAD_DIM], all_out_a[blk])
+        wide = wide + mm_t(g_attn_own[blk, :, 2 * HEAD_DIM :], all_out_b[blk])
     for blk in range(BLK):
         g_ctx_own[blk] = wide[:, blk * third : (blk + 1) * third].astype(BF16)
     swap_back = swap(mid_swap, 1, lambda peer: g_ctx_own.at[peer], g_ctx)
@@ -890,10 +979,8 @@
 
     gvec[0:1, 3 * third :] = jnp.zeros((1, width - 3 * third), F32)
     head_backward(0)
-    summed[5].combine()
     head_backward(1)
     gather_ctx.wait_across()
-    summed[6].pass_on()
     head_backward(2)
     gvec_all[place.hi] = gvec[...].astype(BF16)
     vec_back = Spread(gvec_all, VEC, rs_x, rs_z)
@@ -904,16 +991,22 @@
     gather_ctx.wait_diag()
     head_grads(0)
     summed[0].begin()
-    summed[6].combine()
+    summed[6].pass_on()
+    summed[5].combine()
     vec_back.pass_on(1)
     head_grads(1)
     summed[1].begin()
+    summed[0].relay()
+    vec_back.relay()
     vec_back.pass_on(2)
-    summed[3].pass_on()
     head_grads(2)
     summed[2].begin()
+    summed[1].relay()
+    summed[3].pass_on()
+    summed[6].combine()
     vec_back.pass_on(3)
     settle(5)
+    summed[2].relay()
     reduce_hid = blk_reduce(2)
 
     def part_hid(blk):
@@ -977,7 +1070,7 @@
         copy.wait_send()
     for reduce in (reduce_one, reduce_two, reduce_hid):
         reduce.finish()
-    for gather in (gather_box, gather_hid, gather_out, gather_normed, gather_branch, gather_ctx, gather_vec):
+    for gather in (gather_box, gather_hid, *gather_out, gather_normed, gather_branch, gather_ctx, gather_vec):
         gather.finish()
 
 
@@ -1122,6 +1215,7 @@
         grads=held(CHUNKS, GROUP, shard, HEAD_COLS),
         pair=held(CHUNKS, GRID_Z, shard, HEAD_COLS),
         line=held(CHUNKS, GRID_Z, shard, HEAD_COLS),
+        beside=held(CHUNKS, shard // 2, HEAD_COLS),
         cut=held(5, BLK, rows, HEAD_COLS),
         pack_a=held(BLK, rows, 3 * HEAD_COLS),
         pack_b=held(BLK, rows, GROUP * ff_part),
@@ -1132,7 +1226,8 @@
         all_vec=held(GROUP, 16, width),
         all_hid=held(BLK, tok, width),
         all_box=held(BLK, 8, tok, kind=jnp.int32),
-        all_out=held(BLK, GROUP * shard, third),
+        all_out_a=held(BLK, GROUP * shard, 2 * HEAD_DIM),
+        all_out_b=held(BLK, GROUP * shard, HEAD_DIM),
         vec_sum=held(16, width, kind=F32),
         table=held(512, width),
         feats=held(tokens, width),
@@ -1167,10 +1262,10 @@
         gvec_page=held(BLK, 16, width, kind=F32),
         ag_x=sem((2, CHUNKS + 1, 4)),
         ag_z=sem((2, CHUNKS + 1, 6)),
-        rs_x=sem((2, CHUNKS + 1, 4)),
+        rs_x=sem((2, CHUNKS + 1, 5)),
         rs_z=sem((2, CHUNKS + 1, 6)),
         in_swap=sem((2, 3, 3)),
-        gather_sem=sem((2, 7, 3)),
+        gather_sem=sem((2, 8, 3)),
         reduce_sem=sem((2, 3, 3)),
         mid_swap=sem((2, 3, 3)),
         out_swap=sem((2, 5, 3)),

time: 159 us -> 154 us (0.969)
  Pallas kernels: 156 us -> 151 us
    pallas_call x2, Pallas kernels: 156 us -> 151 us  [run(): pl.pallas_call(kernel, name=name, out_shape=[jax.ShapeDtypeStruct(shape,...]
where the time goes in v4:
time: 154 us
  Pallas kernels  151 us (98%)
  between operations  1.57 us (1%)
    pallas_call x2, Pallas kernels, run(): pl.pallas_call(kernel, name=name, out_shape=[jax.ShapeDtypeStruct(shape,...  151 us

profile of v4, /device:TPU:0, one launch (start us, length us, event | category | flops | bytes accessed | tf_op | source)
XLA Modules:
  0.0 154.0 jit_solution(8271358133355749015)
XLA Ops:
  1.3 0.0 copy-start.7
  1.3 0.0 copy-start.3
  1.3 0.0 copy-start.4
  1.3 0.0 copy-start.5
  1.3 0.0 copy-start.6
  1.3 0.0 copy-start
  1.4 0.0 copy-start.1
  1.4 0.0 copy-start.2
  1.4 0.6 copy-done.7
  2.0 0.0 copy-done.3
  2.0 0.0 copy-done.4
  2.0 0.0 copy-done.5
  2.0 0.0 copy-done.6
  2.0 0.0 copy-done
  2.0 0.0 copy-done.1
  2.0 0.0 copy-done.2
  2.1 0.1 concatenate.3
  2.2 0.6 broadcast_in_dim.9.vec
  2.7 148.5 %layer.1 = (bf16[128,768]{1,0:T(8,128)(2,1)}, bf16[128,768]{1,0:T(8,128)(2,1)}, bf16[5,4,24,384]{3,2,1,0:T(8,128)(2,1)}, f32[96,768]{1,0:T(8,128)}, f32[8,384]{1,0:T(8,128)}) custom-call(s32[1]{0:T(128)S(6)} %copy.34.lengths, bf16[24,2304]{1,0:T(8,128)(2,1)} %w_qkv.1, bf16[24,768]{1,0:T(8,128)(2,1)} %w_relq.1, bf16[24,768]{1,0:T(8,128)(2,1)} %w_relk.1, ...), custom_call_target="tpu_custom_call" | custom-call | tf_op jit(solution)/shard_map/layer/pallas_call | solution.py:157
  151.2 2.5 %finish.1 = (bf16[128,768]{1,0:T(8,128)(2,1)}, bf16[128,768]{1,0:T(8,128)(2,1)}, f32[24,2304]{1,0:T(8,128)}, f32[1,72]{1,0:T(1,128)}, f32[24,768]{1,0:T(8,128)},...) custom-call(bf16[128,768]{1,0:T(8,128)(2,1)} %get-tuple-element.37.o, ...), custom_call_target="tpu_custom_call" | custom-call | tf_op jit(solution)/shard_map/finish/pallas_call | solution.py:157
  (1 shorter events, 0.0 us)
Async XLA Ops:
  1.3 0.7 copy-start.7
  1.3 0.7 copy-start.3
  1.3 0.7 copy-start.4
  1.3 0.7 copy-start.5
  1.3 0.7 copy-start.6
  1.3 0.7 copy-start
  1.4 0.7 copy-start.1
  1.4 0.7 copy-start.2

commit v5 on v4

--- a/solution.py
+++ b/solution.py
@@ -562,6 +562,12 @@
     bias_part, plain_part = w_qkv.shape[1] // (GROUP * BLK), width // (GROUP * BLK)
     spot = place.hi * BLK + b
 
+    def folded(rows):
+        return jnp.concatenate([rows[0:8, : width // 2], rows[0:8, width // 2 :]], axis=0)
+
+    def unfolded(rows):
+        return jnp.concatenate([rows[0:8], rows[8:16]], axis=1)
+
     def home(at):
         wide = at + spot * bias_part
         part = (wide >= width).astype(jnp.int32) + (wide >= 2 * width).astype(jnp.int32)
@@ -588,7 +594,7 @@
     for blk in range(BLK):
         taken = row_here & ((taker == blk) | (taker < 0))
         values = jnp.where(taken, jnp.broadcast_to(vec[...].astype(F32), (16, held)), 0.0)
-        pack_vec[blk] = mm(values.astype(BF16), spots).astype(BF16)
+        pack_vec[blk] = folded(mm(values.astype(BF16), spots)).astype(BF16)
     swap_vec = swap(in_swap, 1, lambda peer: pack_vec.at[peer], land_vec)
 
     for blk in range(BLK):
@@ -675,7 +681,7 @@
     total = all_vec[0].astype(F32)
     for shard in range(1, GROUP):
         total = total + all_vec[shard].astype(F32)
-    vec_sum[...] = total
+    vec_sum[...] = unfolded(total)
 
     rows_whole = GROUP * weights.shape[2]
     whole = weights.reshape(CHUNKS, rows_whole, HEAD_COLS)
@@ -841,7 +847,6 @@
     gvec[6:7, :] = column_sum(cot_wide * hat_two)
     gvec[7:8, :] = column_sum(cot_wide)
     gvec[5:6, :] = column_sum(branch_all[b].astype(F32))
-    gvec[8:16, :] = jnp.zeros((8, width), F32)
     reduce_two = blk_reduce(1)
 
     def back(blk):
@@ -982,7 +987,7 @@
     head_backward(1)
     gather_ctx.wait_across()
     head_backward(2)
-    gvec_all[place.hi] = gvec[...].astype(BF16)
+    gvec_all[place.hi] = folded(gvec[...]).astype(BF16)
     vec_back = Spread(gvec_all, VEC, rs_x, rs_z)
     vec_back.begin()
     vec_back.cross()
@@ -992,9 +997,9 @@
     head_grads(0)
     summed[0].begin()
     summed[6].pass_on()
-    summed[5].combine()
     vec_back.pass_on(1)
     head_grads(1)
+    summed[5].combine()
     summed[1].begin()
     summed[0].relay()
     vec_back.relay()
@@ -1005,7 +1010,6 @@
     summed[3].pass_on()
     summed[6].combine()
     vec_back.pass_on(3)
-    settle(5)
     summed[2].relay()
     reduce_hid = blk_reduce(2)
 
@@ -1023,18 +1027,15 @@
     reduce_hid.sib_near.start()
     own_hid = part_hid(b) + g_one
     summed[3].combine()
-    settle(6)
     summed[4].pass_on()
     grad_hid[...] = reduce_hid.total(own_hid).astype(BF16)
-    settle(3)
     summed[4].combine()
     summed[0].pass_on()
-    settle(4)
     vec_back.settle()
     total = gvec_all[0].astype(F32)
     for shard in range(1, GROUP):
         total = total + gvec_all[shard].astype(F32)
-    gvec_page[b] = total
+    gvec_page[b] = unfolded(total)
     gather_vec = blk_gather(5, gvec_page)
     gather_vec.start()
     summed[0].combine()
@@ -1047,21 +1048,25 @@
     places = lax.broadcasted_iota(jnp.int32, (width, held), 0) == column
     places = jnp.where(places, 1.0, 0.0)
     plain = gvec_page[0] + gvec_page[1] + gvec_page[2] + gvec_page[3]
-    plain_row = lax.broadcasted_iota(jnp.int32, (16, width), 0)
+    plain_row = lax.broadcasted_iota(jnp.int32, (8, width), 0)
     plain = jnp.where(plain_row < 2, 0.0, plain)
     bias_all = jnp.concatenate([gvec_page[blk][0:1, :] for blk in range(BLK)], axis=0)
     stacked = jnp.concatenate([plain, bias_all, gvec_page[b][1:2, :], bias_all[0:3, :]], axis=0)
     picked = jnp.dot(stacked, places, preferred_element_type=F32, precision=lax.Precision.HIGHEST)
     own_bias = jnp.zeros((1, held), F32)
     for blk in range(BLK):
-        own_bias = own_bias + jnp.where(taker == blk, picked[16 + blk : 17 + blk, :], 0.0)
-    vec_own[...] = jnp.concatenate([own_bias, picked[20:21, :], picked[2:8, :]], axis=0)
-
-    settle(0)
+        own_bias = own_bias + jnp.where(taker == blk, picked[8 + blk : 9 + blk, :], 0.0)
+    vec_own[...] = jnp.concatenate([own_bias, picked[12:13, :], picked[2:8, :]], axis=0)
+
+    settle(5)
+    settle(6)
     summed[1].combine()
     summed[2].pass_on()
+    settle(3)
+    settle(4)
+    summed[2].combine()
+    settle(0)
     settle(1)
-    summed[2].combine()
     settle(2)
     arrive(finals)
     for part in chunk + summed + [vec_back]:
@@ -1219,16 +1224,16 @@
         cut=held(5, BLK, rows, HEAD_COLS),
         pack_a=held(BLK, rows, 3 * HEAD_COLS),
         pack_b=held(BLK, rows, GROUP * ff_part),
-        pack_vec=held(BLK, 16, width),
+        pack_vec=held(BLK, 16, width // 2),
         land_a=held(BLK, rows, 3 * HEAD_COLS),
         land_b=held(BLK, rows, GROUP * ff_part),
-        land_vec=held(BLK, 16, width),
-        all_vec=held(GROUP, 16, width),
+        land_vec=held(BLK, 16, width // 2),
+        all_vec=held(GROUP, 16, width // 2),
         all_hid=held(BLK, tok, width),
         all_box=held(BLK, 8, tok, kind=jnp.int32),
         all_out_a=held(BLK, GROUP * shard, 2 * HEAD_DIM),
         all_out_b=held(BLK, GROUP * shard, HEAD_DIM),
-        vec_sum=held(16, width, kind=F32),
+        vec_sum=held(8, width, kind=F32),
         table=held(512, width),
         feats=held(tokens, width),
         qkv=held(9, tokens, HEAD_DIM),
@@ -1257,9 +1262,9 @@
         p_low=held(tokens, tokens),
         g_turned=held(2, HEADS, tokens, width),
         g_qkv=held(3, tokens, third),
-        gvec=held(16, width, kind=F32),
-        gvec_all=held(GROUP, 16, width),
-        gvec_page=held(BLK, 16, width, kind=F32),
+        gvec=held(8, width, kind=F32),
+        gvec_all=held(GROUP, 16, width // 2),
+        gvec_page=held(BLK, 8, width, kind=F32),
         ag_x=sem((2, CHUNKS + 1, 4)),
         ag_z=sem((2, CHUNKS + 1, 6)),
         rs_x=sem((2, CHUNKS + 1, 5)),

time: 154 us -> 150 us (0.974)
  Pallas kernels: 151 us -> 147 us
    pallas_call x2, Pallas kernels: 151 us -> 147 us  [run(): pl.pallas_call(kernel, name=name, out_shape=[jax.ShapeDtypeStruct(shape,...]
where the time goes in v5:
time: 150 us
  Pallas kernels  147 us (98%)
  between operations  1.57 us (1%)
    pallas_call x2, Pallas kernels, run(): pl.pallas_call(kernel, name=name, out_shape=[jax.ShapeDtypeStruct(shape,...  147 us

profile of v5, /device:TPU:0, one launch (start us, length us, event | category | flops | bytes accessed | tf_op | source)
XLA Modules:
  0.0 150.3 jit_solution(4271362087337602969)
XLA Ops:
  1.3 0.0 copy-start.7
  1.3 0.0 copy-start.3
  1.3 0.0 copy-start.4
  1.3 0.0 copy-start.5
  1.3 0.0 copy-start.6
  1.3 0.0 copy-start
  1.4 0.0 copy-start.1
  1.4 0.0 copy-start.2
  1.4 0.6 copy-done.7
  2.0 0.0 copy-done.3
  2.0 0.0 copy-done.4
  2.0 0.0 copy-done.5
  2.0 0.0 copy-done.6
  2.0 0.0 copy-done
  2.0 0.0 copy-done.1
  2.0 0.0 copy-done.2
  2.1 0.1 concatenate.3
  2.2 0.6 broadcast_in_dim.9.vec
  2.7 144.8 %layer.1 = (bf16[128,768]{1,0:T(8,128)(2,1)}, bf16[128,768]{1,0:T(8,128)(2,1)}, bf16[5,4,24,384]{3,2,1,0:T(8,128)(2,1)}, f32[96,768]{1,0:T(8,128)}, f32[8,384]{1,0:T(8,128)}) custom-call(s32[1]{0:T(128)S(6)} %copy.34.lengths, bf16[24,2304]{1,0:T(8,128)(2,1)} %w_qkv.1, bf16[24,768]{1,0:T(8,128)(2,1)} %w_relq.1, bf16[24,768]{1,0:T(8,128)(2,1)} %w_relk.1, ...), custom_call_target="tpu_custom_call" | custom-call | tf_op jit(solution)/shard_map/layer/pallas_call | solution.py:157
  147.5 2.5 %finish.1 = (bf16[128,768]{1,0:T(8,128)(2,1)}, bf16[128,768]{1,0:T(8,128)(2,1)}, f32[24,2304]{1,0:T(8,128)}, f32[1,72]{1,0:T(1,128)}, f32[24,768]{1,0:T(8,128)},...) custom-call(bf16[128,768]{1,0:T(8,128)(2,1)} %get-tuple-element.37.o, ...), custom_call_target="tpu_custom_call" | custom-call | tf_op jit(solution)/shard_map/finish/pallas_call | solution.py:157
  (1 shorter events, 0.0 us)
Async XLA Ops:
  1.3 0.7 copy-start.7
  1.3 0.7 copy-start.3
  1.3 0.7 copy-start.4
  1.3 0.7 copy-start.5
  1.3 0.7 copy-start.6
  1.3 0.7 copy-start
  1.4 0.7 copy-start.1
  1.4 0.7 copy-start.2
